TPU v7x, 32 devices: a whole 2x2x4 slice. The times are simulated.
32 devices in a mesh: wide: 8 (over y, x, core), narrow: 4 (over z).
Axes of the slice: x: 2, y: 2, z: 4, core: 2. Of those that a mesh axis runs over, the one named last changes fastest.
Arguments:
- tokens: bfloat16 [16384, 768], P(('wide', 'narrow')), may hold values from -6 to 6
- block_size: int32 [8], P('wide'), may hold values from 4 to 16, as said below
- norm_gain: float32 [2, 2, 768], replicated, may hold values from 0.5 to 1.5
- norm_shift: float32 [2, 2, 768], replicated, may hold values from -2 to 2
- mixer_weight: bfloat16 [2, 768, 3, 768], P(None, None, None, 'narrow'), may hold values from -0.21875 to 0.21875
- mixer_bias: float32 [2, 3, 768], P(None, None, 'narrow'), may hold values from -2 to 2
- output_weight: bfloat16 [2, 768, 768], P(None, 'narrow'), may hold values from -1.75 to 1.75
- output_bias: float32 [2, 2, 768], replicated, may hold values from -2 to 2
- up_weight: bfloat16 [2, 768, 3072], P(None, None, 'narrow'), may hold values from -0.21875 to 0.21875
- up_bias: float32 [2, 3072], P(None, 'narrow'), may hold values from -2 to 2
- down_weight: bfloat16 [2, 3072, 768], P(None, 'narrow'), may hold values from -0.109375 to 0.109375
- cotangent: bfloat16 [16384, 768], P(('wide', 'narrow')), may hold values from -6 to 6
Outputs:
- block_out: bfloat16 [16384, 768], P(('wide', 'narrow'))
- tokens_grad: bfloat16 [16384, 768], P(('wide', 'narrow'))
- gain_grad: float32 [2, 2, 768], replicated
- shift_grad: float32 [2, 2, 768], replicated
- mixer_grad: float32 [2, 768, 3, 768], P(None, None, None, 'narrow')
- mixer_bias_grad: float32 [2, 3, 768], P(None, None, 'narrow')
- output_grad: float32 [2, 768, 768], P(None, 'narrow')
- output_bias_grad: float32 [2, 2, 768], replicated
- up_grad: float32 [2, 768, 3072], P(None, None, 'narrow')
- up_bias_grad: float32 [2, 3072], P(None, 'narrow')
- down_grad: float32 [2, 3072, 768], P(None, 'narrow')
Inputs may be any that keep to these rules, and one draw needn't show every extreme that they name: `block_size`: each entry is 4, 8 or 16; some sequence has 16 and some has 4.
All inputs are finite; a program needn't handle non-finite values.
Results may differ from a plain program's by a relative error of at most 0.028.
Values may be sent and summed in bfloat16 or wider, within the bound.
No kernel may reach another device: no remote copies, remote signals or barrier semaphores. Data moves between devices by JAX's collectives and lax.ppermute only.
A program may use at most 192 MiB of HBM per device.

v0:
```python
import math

import jax
import jax.numpy as jnp
from jax import lax
from jax.sharding import PartitionSpec as P

HEAD_DIM = 64
LEN = 1024


EPSILON = 1e-05
CONTRACT_COLS = (((1,), (1,)), ((), ()))
CONTRACT_ROWS = (((0,), (0,)), ((), ()))


def layer_norm(values, gain, shift):
    center = values - jnp.mean(values, axis=-1, keepdims=True)
    inverse = lax.rsqrt(jnp.mean(center * center, axis=-1, keepdims=True) + EPSILON)
    unit_rows = center * inverse
    return (unit_rows * gain + shift, unit_rows, inverse)


def norm_backward(grad_in, unit_rows, inverse, gain):
    scaled = grad_in * gain
    return inverse * (
        scaled
        - jnp.mean(scaled, axis=-1, keepdims=True)
        - unit_rows * jnp.mean(scaled * unit_rows, axis=-1, keepdims=True)
    )


def gelu_tanh(arguments_in):
    return jax.nn.gelu(arguments_in, approximate=True)


def rotary_tables(row_count):
    halfway = HEAD_DIM // 2
    positions = (jnp.arange(row_count, dtype=jnp.int32) % LEN).astype(jnp.float32)
    frequency = jnp.exp(jnp.arange(halfway, dtype=jnp.float32) * (-math.log(10000.0) / halfway))
    angles = positions[:, None] * frequency[None, :]
    return (jnp.cos(angles)[:, None, :], jnp.sin(angles)[:, None, :])


def rotate(heads_in, cosine, sine_table):
    halfway = heads_in.shape[-1] // 2
    first_half = heads_in[..., :halfway]
    second_half = heads_in[..., halfway:]
    return jnp.concatenate(
        [
            first_half * cosine - second_half * sine_table,
            first_half * sine_table + second_half * cosine,
        ],
        axis=-1,
    )


def unrotate(grads_in, cosine, sine_table):
    halfway = grads_in.shape[-1] // 2
    first_half = grads_in[..., :halfway]
    second_half = grads_in[..., halfway:]
    return jnp.concatenate(
        [
            first_half * cosine + second_half * sine_table,
            second_half * cosine - first_half * sine_table,
        ],
        axis=-1,
    )


def allowed_pairs(query_rows, key_rows, block_width):
    noisy_query = query_rows < LEN
    noisy_key = key_rows < LEN
    query_block = query_rows % LEN // block_width
    key_block = key_rows % LEN // block_width
    same_block = query_block[:, None] == key_block[None, :]
    earlier = key_block[None, :] < query_block[:, None]
    noisy_case = jnp.where(noisy_key[None, :], same_block, earlier)
    clean_case = jnp.logical_and(
        jnp.logical_not(noisy_key)[None, :], jnp.logical_or(earlier, same_block)
    )
    return jnp.where(noisy_query[:, None], noisy_case, clean_case)


def masked_scores(query_block, keys_all, offset, block_width):
    row_count = keys_all.shape[0]
    block_rows = query_block.shape[0]
    score_scale = query_block.shape[-1] ** (-0.5)
    scores = (
        jnp.einsum("qhd,khd->hqk", query_block, keys_all, preferred_element_type=jnp.float32)
        * score_scale
    )
    query_rows = offset + jnp.arange(block_rows, dtype=jnp.int32)
    key_rows = jnp.arange(row_count, dtype=jnp.int32)
    return jnp.where(allowed_pairs(query_rows, key_rows, block_width)[None], scores, -1e30)


def attend_forward(queries, keys_all, values, block_width):
    row_count = queries.shape[0]
    block_rows = min(512, row_count)

    def one_block(offset):
        query_block = lax.dynamic_slice_in_dim(queries, offset, block_rows, 0)
        scores = masked_scores(query_block, keys_all, offset, block_width)
        highest = jnp.max(scores, axis=-1, keepdims=True)
        weights = jnp.exp(scores - highest)
        row_total = jnp.sum(weights, axis=-1, keepdims=True)
        chances = (weights / row_total).astype(jnp.bfloat16)
        attended = jnp.einsum("hqk,khd->qhd", chances, values, preferred_element_type=jnp.float32)
        return (attended.astype(jnp.bfloat16), (highest + jnp.log(row_total))[..., 0])

    offsets = jnp.arange(row_count // block_rows, dtype=jnp.int32) * block_rows
    attended, log_totals = lax.map(one_block, offsets)
    return (attended.reshape(queries.shape), log_totals)


def attend_backward(queries, keys_all, values, log_totals, grad_out, block_width):
    row_count = queries.shape[0]
    block_rows = min(512, row_count)
    score_scale = queries.shape[-1] ** (-0.5)

    def one_block(running, pieces):
        grad_keys, grad_values = running
        offset, log_block = pieces
        query_block = lax.dynamic_slice_in_dim(queries, offset, block_rows, 0)
        grad_block = lax.dynamic_slice_in_dim(grad_out, offset, block_rows, 0)
        scores = masked_scores(query_block, keys_all, offset, block_width)
        chances = jnp.exp(scores - log_block[..., None])
        grad_chances = jnp.einsum(
            "qhd,khd->hqk", grad_block, values, preferred_element_type=jnp.float32
        )
        row_dot = jnp.sum(chances * grad_chances, axis=-1, keepdims=True)
        grad_scores = (chances * (grad_chances - row_dot)).astype(jnp.bfloat16)
        grad_queries = (
            jnp.einsum("hqk,khd->qhd", grad_scores, keys_all, preferred_element_type=jnp.float32)
            * score_scale
        )
        grad_keys = (
            grad_keys
            + jnp.einsum(
                "hqk,qhd->khd", grad_scores, query_block, preferred_element_type=jnp.float32
            )
            * score_scale
        )
        grad_values = grad_values + jnp.einsum(
            "hqk,qhd->khd",
            chances.astype(jnp.bfloat16),
            grad_block,
            preferred_element_type=jnp.float32,
        )
        return ((grad_keys, grad_values), grad_queries)

    offsets = jnp.arange(row_count // block_rows, dtype=jnp.int32) * block_rows
    zero_keys = jnp.zeros(keys_all.shape, jnp.float32)
    final_pair, grad_queries = lax.scan(one_block, (zero_keys, zero_keys), (offsets, log_totals))
    return (grad_queries.reshape(queries.shape), final_pair[0], final_pair[1])


def by_sequence(array_in, seq_count):
    return array_in.reshape((seq_count, array_in.shape[0] // seq_count) + array_in.shape[1:])


def gather_normed(normed):
    return lax.all_gather(normed, "narrow", axis=0, tiled=True)


def gather_grads(grads_in):
    return lax.all_gather(grads_in, "narrow", axis=0, tiled=True)


def branch_sum(full_rows, weight):
    return lax.psum_scatter(
        jnp.dot(full_rows, weight, preferred_element_type=jnp.float32).astype(jnp.bfloat16),
        "narrow",
        scatter_dimension=0,
        tiled=True,
    ).astype(jnp.float32)


def input_sum(grad_three, weight_three):
    grad_full = grad_three.reshape(grad_three.shape[0], grad_three.shape[1] * grad_three.shape[2])
    weight = weight_three.reshape(
        weight_three.shape[0], weight_three.shape[1] * weight_three.shape[2]
    )
    return lax.psum_scatter(
        lax.dot_general(
            grad_full, weight, CONTRACT_COLS, preferred_element_type=jnp.float32
        ).astype(jnp.bfloat16),
        "narrow",
        scatter_dimension=0,
        tiled=True,
    ).astype(jnp.float32)


def layer_forward(residual, block_sizes, cosine, sine_table, params):
    (
        norm_gain,
        norm_shift,
        mixer_weight,
        mixer_bias,
        output_weight,
        output_bias,
        up_weight,
        up_bias,
        down_weight,
    ) = params
    model_width = mixer_weight.shape[0]
    local_width = mixer_weight.shape[-1]
    heads_here = local_width // HEAD_DIM
    seq_count = block_sizes.shape[0]
    normed, unit_first, inverse_first = layer_norm(residual, norm_gain[0], norm_shift[0])
    normed_first = gather_normed(normed.astype(jnp.bfloat16))
    row_count = normed_first.shape[0]
    projected = jnp.dot(
        normed_first,
        mixer_weight.reshape(model_width, 3 * local_width),
        preferred_element_type=jnp.float32,
    ) + mixer_bias.reshape(3 * local_width)
    projected = projected.reshape(row_count, 3, heads_here, HEAD_DIM)
    queries = rotate(projected[:, 0], cosine, sine_table).astype(jnp.bfloat16)
    keys_all = rotate(projected[:, 1], cosine, sine_table).astype(jnp.bfloat16)
    values = projected[:, 2].astype(jnp.bfloat16)

    def per_sequence(seq_items):
        return attend_forward(seq_items[0], seq_items[1], seq_items[2], seq_items[3])

    attended, log_totals = lax.map(
        per_sequence,
        (
            by_sequence(queries, seq_count),
            by_sequence(keys_all, seq_count),
            by_sequence(values, seq_count),
            block_sizes,
        ),
    )
    attended = attended.reshape(row_count, local_width)
    branch = branch_sum(attended, output_weight) + output_bias[0]
    middle = residual + branch
    normed, unit_second, inverse_second = layer_norm(middle, norm_gain[1], norm_shift[1])
    normed_second = gather_normed(normed.astype(jnp.bfloat16))
    hidden = jnp.dot(normed_second, up_weight, preferred_element_type=jnp.float32) + up_bias
    active = gelu_tanh(hidden).astype(jnp.bfloat16)
    result = middle + (branch_sum(active, down_weight) + output_bias[1])
    stored = (
        unit_first,
        inverse_first,
        normed_first,
        queries,
        keys_all,
        values,
        attended,
        log_totals,
        unit_second,
        inverse_second,
        normed_second,
        hidden,
        active,
    )
    return (result, stored)


def layer_backward(upstream, block_sizes, cosine, sine_table, params, stored):
    (
        norm_gain,
        norm_shift,
        mixer_weight,
        mixer_bias,
        output_weight,
        output_bias,
        up_weight,
        up_bias,
        down_weight,
    ) = params
    (
        unit_first,
        inverse_first,
        normed_first,
        queries,
        keys_all,
        values,
        attended,
        log_totals,
        unit_second,
        inverse_second,
        normed_second,
        hidden,
        active,
    ) = stored
    model_width = mixer_weight.shape[0]
    local_width = mixer_weight.shape[-1]
    heads_here = local_width // HEAD_DIM
    row_count = normed_first.shape[0]
    seq_count = block_sizes.shape[0]
    down_low = upstream.astype(jnp.bfloat16)
    down_bias_grad = jnp.sum(down_low.astype(jnp.float32), axis=0)
    down_rows = gather_grads(down_low)
    grad_active = lax.dot_general(
        down_rows, down_weight, CONTRACT_COLS, preferred_element_type=jnp.float32
    )
    down_grad = lax.dot_general(
        active, down_rows, CONTRACT_ROWS, preferred_element_type=jnp.float32
    )
    gelu_pull = jax.vjp(gelu_tanh, hidden)[1]
    grad_hidden = gelu_pull(grad_active)[0].astype(jnp.bfloat16)
    up_bias_grad = jnp.sum(grad_hidden.astype(jnp.float32), axis=0)
    up_grad = lax.dot_general(
        normed_second, grad_hidden, CONTRACT_ROWS, preferred_element_type=jnp.float32
    )
    grad_normed = input_sum(
        grad_hidden.reshape(row_count, 1, grad_hidden.shape[1]),
        up_weight.reshape(model_width, 1, up_weight.shape[1]),
    )
    gain_second = jnp.sum(grad_normed * unit_second, axis=0)
    shift_second = jnp.sum(grad_normed, axis=0)
    upstream = upstream + norm_backward(grad_normed, unit_second, inverse_second, norm_gain[1])
    attn_low = upstream.astype(jnp.bfloat16)
    attn_bias_grad = jnp.sum(attn_low.astype(jnp.float32), axis=0)
    attn_rows = gather_grads(attn_low)
    grad_attended = lax.dot_general(
        attn_rows, output_weight, CONTRACT_COLS, preferred_element_type=jnp.float32
    ).astype(jnp.bfloat16)
    output_grad = lax.dot_general(
        attended, attn_rows, CONTRACT_ROWS, preferred_element_type=jnp.float32
    )
    grad_heads = grad_attended.reshape(row_count, heads_here, HEAD_DIM)

    def per_sequence_back(seq_items):
        return attend_backward(
            seq_items[0], seq_items[1], seq_items[2], seq_items[3], seq_items[4], seq_items[5]
        )

    grad_queries, grad_keys, grad_values = lax.map(
        per_sequence_back,
        (
            by_sequence(queries, seq_count),
            by_sequence(keys_all, seq_count),
            by_sequence(values, seq_count),
            log_totals,
            by_sequence(grad_heads, seq_count),
            block_sizes,
        ),
    )
    head_shape = (row_count, heads_here, HEAD_DIM)
    grad_queries = unrotate(grad_queries.reshape(head_shape), cosine, sine_table)
    grad_keys = unrotate(grad_keys.reshape(head_shape), cosine, sine_table)
    grad_projected = jnp.stack([grad_queries, grad_keys, grad_values.reshape(head_shape)], axis=1)
    grad_projected = grad_projected.reshape(row_count, 3, local_width).astype(jnp.bfloat16)
    mixer_bias_grad = jnp.sum(grad_projected.astype(jnp.float32), axis=0)
    mixer_grad = lax.dot_general(
        normed_first,
        grad_projected.reshape(row_count, 3 * local_width),
        CONTRACT_ROWS,
        preferred_element_type=jnp.float32,
    ).reshape(model_width, 3, local_width)
    grad_normed = input_sum(grad_projected, mixer_weight)
    gain_first = jnp.sum(grad_normed * unit_first, axis=0)
    shift_first = jnp.sum(grad_normed, axis=0)
    upstream = upstream + norm_backward(grad_normed, unit_first, inverse_first, norm_gain[0])
    owned = (mixer_grad, mixer_bias_grad, output_grad, up_grad, up_bias_grad, down_grad)
    shared = (
        jnp.stack([gain_first, gain_second]),
        jnp.stack([shift_first, shift_second]),
        jnp.stack([attn_bias_grad, down_bias_grad]),
    )
    return (upstream, owned, shared)


def per_device(
    tokens,
    block_size,
    norm_gain,
    norm_shift,
    mixer_weight,
    mixer_bias,
    output_weight,
    output_bias,
    up_weight,
    up_bias,
    down_weight,
    cotangent,
):
    layer_count = norm_gain.shape[0]
    cosine, sine_table = rotary_tables(lax.axis_size("narrow") * tokens.shape[0])

    def layer_params(layer_idx):
        return (
            norm_gain[layer_idx],
            norm_shift[layer_idx],
            mixer_weight[layer_idx],
            mixer_bias[layer_idx],
            output_weight[layer_idx],
            output_bias[layer_idx],
            up_weight[layer_idx],
            up_bias[layer_idx],
            down_weight[layer_idx],
        )

    layer_wholes = []
    for layer_idx in range(layer_count):
        layer_wholes.append((None, None, None, None))
    residual = tokens.astype(jnp.float32)
    layer_inputs = []
    layer_stores = []
    for layer_idx in range(layer_count):
        layer_inputs.append(residual)
        residual, stored = layer_forward(
            residual, block_size, cosine, sine_table, layer_params(layer_idx)
        )
        layer_stores.append(stored)
    block_out = residual.astype(jnp.bfloat16)
    upstream = cotangent.astype(jnp.float32)
    owned_list = [None] * layer_count
    shared_list = [None] * layer_count
    for layer_idx in reversed(range(layer_count)):
        stored = layer_forward(
            layer_inputs[layer_idx], block_size, cosine, sine_table, layer_params(layer_idx)
        )[1]
        upstream, owned, shared = layer_backward(
            upstream, block_size, cosine, sine_table, layer_params(layer_idx), stored
        )
        owned_list[layer_idx] = owned
        shared_list[layer_idx] = shared
    stacked = [
        jnp.stack([owned_list[layer_idx][member] for layer_idx in range(layer_count)])
        for member in range(6)
    ]
    stacked = lax.psum(
        (stacked[0], stacked[1], stacked[2], stacked[3], stacked[4], stacked[5]), "wide"
    )
    gain_stack = jnp.stack([shared_list[layer_idx][0] for layer_idx in range(layer_count)])
    shift_stack = jnp.stack([shared_list[layer_idx][1] for layer_idx in range(layer_count)])
    bias_stack = jnp.stack([shared_list[layer_idx][2] for layer_idx in range(layer_count)])
    gain_grad, shift_grad, output_bias_grad = lax.psum(
        (gain_stack, shift_stack, bias_stack), ("wide", "narrow")
    )
    return (
        block_out,
        upstream.astype(jnp.bfloat16),
        gain_grad,
        shift_grad,
        stacked[0],
        stacked[1],
        stacked[2],
        output_bias_grad,
        stacked[3],
        stacked[4],
        stacked[5],
    )


def solution(mesh):
    in_specs = (
        P(("wide", "narrow"), None),
        P("wide"),
        P(),
        P(),
        P(None, None, None, "narrow"),
        P(None, None, "narrow"),
        P(None, "narrow", None),
        P(),
        P(None, None, "narrow"),
        P(None, "narrow"),
        P(None, "narrow", None),
        P(("wide", "narrow"), None),
    )
    out_specs = (
        P(("wide", "narrow"), None),
        P(("wide", "narrow"), None),
        P(),
        P(),
        P(None, None, None, "narrow"),
        P(None, None, "narrow"),
        P(None, "narrow", None),
        P(),
        P(None, None, "narrow"),
        P(None, "narrow"),
        P(None, "narrow", None),
    )
    return jax.shard_map(
        per_device, mesh=mesh, in_specs=in_specs, out_specs=out_specs, check_vma=False
    )
```

profile of v0, /device:TPU:0, one launch (start us, length us, event | category | flops | bytes accessed | tf_op | source)
XLA Modules:
  0.0 2265.9 jit_solution(1651564727914734148)
XLA Ops:
  18.2 62.9 %all-gather.11.cloned.1.call-done = bf16[2048,768]{1,0:T(8,128)(2,1)} async-done(((bf16[512,768]{1,0:T(8,128)(2,1)}), bf16[2048,768]{1,0:T(8,128)(2,1)}) %all-gather.11.cloned.1.call-update) | async-done | bytes 3145744 | tf_op jit(solution)/shard_map/all_gather | solution.py:164
  87.0 95.1 %while.146 = (s32[]{:T(128)}, bf16[4,512,3,64]{1,3,2,0:T(8,128)(2,1)S(1)}, s32[4]{0:T(128)S(1)}, s32[]{:T(128)}, s32[]{:T(128)}, /*index=5*/bf16[2048,3,64]{0,2,...) while((s32[]{:T(128)}, ...), condition=%wide.region_5.6_spmd, body=%wide.region_2.5_spmd.sunk | while | flops 830616576 | bytes 29273284 | solution.py:113
  186.0 111.1 %while.149 = (s32[]{:T(128)}, bf16[4,512,3,64]{1,3,2,0:T(8,128)(2,1)S(1)}, f32[4,3,512]{2,1,0:T(4,128)S(1)}, s32[4]{0:T(128)S(1)}, s32[]{:T(128)}, /*index=5*/s3...) while((s32[]{:T(128)}, ...), condition=%wide.region_39.40_spmd, body=%wide.region_36.39_spmd.sunk | while | flops 849487360 | bytes 43998412 | solution.py:113
  303.0 57.8 %reduce-scatter.25.cloned.1.call-done = bf16[512,768]{1,0:T(8,128)(2,1)} async-done(((bf16[2048,768]{1,0:T(8,128)(2,1)}), bf16[512,768]{1,0:T(8,128)(2,1)}) %reduce-scatter.25.cloned.1.call-update) | async-done | bytes 786448 | tf_op jit(solution)/shard_map/reduce_scatter | solution.py:172
  368.1 63.0 %all-gather.13.cloned.1.call-done = bf16[2048,768]{1,0:T(8,128)(2,1)} async-done(((bf16[512,768]{1,0:T(8,128)(2,1)}), bf16[2048,768]{1,0:T(8,128)(2,1)}) %all-gather.13.cloned.1.call-update) | async-done | bytes 3145744 | tf_op jit(solution)/shard_map/all_gather | solution.py:164
  440.6 59.0 %reduce-scatter.13.cloned.1.call-done = bf16[512,768]{1,0:T(8,128)(2,1)} async-done(((bf16[2048,768]{1,0:T(8,128)(2,1)}), bf16[512,768]{1,0:T(8,128)(2,1)}) %reduce-scatter.13.cloned.1.call-update) | async-done | bytes 786448 | tf_op jit(solution)/shard_map/reduce_scatter | solution.py:172
  503.7 63.5 %all-gather.15.cloned.1.call-done = bf16[2048,768]{1,0:T(8,128)(2,1)} async-done(((bf16[512,768]{1,0:T(8,128)(2,1)}), bf16[2048,768]{1,0:T(8,128)(2,1)}) %all-gather.15.cloned.1.call-update) | async-done | bytes 3145744 | tf_op jit(solution)/shard_map/all_gather | solution.py:164
  573.9 86.7 %while.147 = (s32[]{:T(128)}, bf16[4,512,3,64]{1,3,2,0:T(8,128)(2,1)}, s32[4]{0:T(128)S(1)}, s32[]{:T(128)}, s32[]{:T(128)}, /*index=5*/bf16[2048,3,64]{0,2,1:T(...) while((s32[]{:T(128)}, ...), condition=%wide.region_15.16_spmd, body=%wide.region_12.15_spmd.sunk | while | flops 830616576 | bytes 29271236 | solution.py:113
  665.5 107.4 %while.148 = (s32[]{:T(128)}, bf16[4,512,3,64]{1,3,2,0:T(8,128)(2,1)S(1)}, f32[4,3,512]{2,1,0:T(4,128)S(1)}, s32[4]{0:T(128)S(1)}, s32[]{:T(128)}, /*index=5*/s3...) while((s32[]{:T(128)}, ...), condition=%wide.region_23.24_spmd, body=%wide.region_20.23_spmd.sunk | while | flops 849487360 | bytes 43998412 | solution.py:113
  777.4 59.0 %reduce-scatter.19.cloned.1.call-done = bf16[512,768]{1,0:T(8,128)(2,1)} async-done(((bf16[2048,768]{1,0:T(8,128)(2,1)}), bf16[512,768]{1,0:T(8,128)(2,1)}) %reduce-scatter.19.cloned.1.call-update) | async-done | bytes 786448 | tf_op jit(solution)/shard_map/reduce_scatter | solution.py:172
  842.0 63.0 %all-gather.21.cloned.1.call-done = bf16[2048,768]{1,0:T(8,128)(2,1)} async-done(((bf16[512,768]{1,0:T(8,128)(2,1)}), bf16[2048,768]{1,0:T(8,128)(2,1)}) %all-gather.21.cloned.1.call-update) | async-done | bytes 3145744 | tf_op jit(solution)/shard_map/all_gather | solution.py:164
  912.5 56.1 %all-gather.19.cloned.1.call-done = bf16[2048,768]{1,0:T(8,128)(2,1)} async-done(((bf16[512,768]{1,0:T(8,128)(2,1)}), bf16[2048,768]{1,0:T(8,128)(2,1)}) %all-gather.19.cloned.1.call-update) | async-done | bytes 3145744 | tf_op jit(solution)/shard_map/all_gather | solution.py:168
  984.3 59.0 %reduce-scatter.21.cloned.1.call-done = bf16[512,768]{1,0:T(8,128)(2,1)} async-done(((bf16[2048,768]{1,0:T(8,128)(2,1)}), bf16[512,768]{1,0:T(8,128)(2,1)}) %reduce-scatter.21.cloned.1.call-update) | async-done | bytes 786448 | tf_op jit(solution)/shard_map/reduce_scatter | solution.py:185
  1050.0 63.6 %all-gather.23.cloned.1.call-done = bf16[2048,768]{1,0:T(8,128)(2,1)} async-done(((bf16[512,768]{1,0:T(8,128)(2,1)}), bf16[2048,768]{1,0:T(8,128)(2,1)}) %all-gather.23.cloned.1.call-update) | async-done | bytes 3145744 | tf_op jit(solution)/shard_map/all_gather | solution.py:168
  1119.0 182.7 %while.150 = (s32[]{:T(128)}, f32[2048,3,64]{0,2,1:T(8,128)}, f32[2048,3,64]{0,2,1:T(8,128)}, f32[4,512,3,64]{1,0,3,2:T(4,128)}, s32[4]{0:T(128)S(1)}, /*index=5...) while((s32[]{:T(128)}, f32[2048,3,64]{0,2,1:T(8,128)}, ...), condition=%wide.region_32.33_spmd.clone, body=%wide.region_30.32_spmd.clone.sunk | while | flops 2068850176 | bytes 151985584 | solution.py:155
  1315.6 58.5 %reduce-scatter.23.cloned.1.call-done = bf16[512,768]{1,0:T(8,128)(2,1)} async-done(((bf16[2048,768]{1,0:T(8,128)(2,1)}), bf16[512,768]{1,0:T(8,128)(2,1)}) %reduce-scatter.23.cloned.1.call-update) | async-done | bytes 786448 | tf_op jit(solution)/shard_map/reduce_scatter | solution.py:185
  1378.4 63.6 %all-gather.17.cloned.1.call-done = bf16[2048,768]{1,0:T(8,128)(2,1)} async-done(((bf16[512,768]{1,0:T(8,128)(2,1)}), bf16[2048,768]{1,0:T(8,128)(2,1)}) %all-gather.17.cloned.1.call-update) | async-done | bytes 3145744 | tf_op jit(solution)/shard_map/all_gather | solution.py:164
  1451.9 58.4 %reduce-scatter.17.cloned.1.call-done = bf16[512,768]{1,0:T(8,128)(2,1)} async-done(((bf16[2048,768]{1,0:T(8,128)(2,1)}), bf16[512,768]{1,0:T(8,128)(2,1)}) %reduce-scatter.17.cloned.1.call-update) | async-done | bytes 786448 | tf_op jit(solution)/shard_map/reduce_scatter | solution.py:172
  1515.2 60.1 %all-gather.27.cloned.1.call-done = bf16[2048,768]{1,0:T(8,128)(2,1)} async-done(((bf16[512,768]{1,0:T(8,128)(2,1)}), bf16[2048,768]{1,0:T(8,128)(2,1)}) %all-gather.27.cloned.1.call-update) | async-done | bytes 3145744 | tf_op jit(solution)/shard_map/all_gather | solution.py:164
  1582.8 56.7 %all-gather.25.cloned.1.call-done = bf16[2048,768]{1,0:T(8,128)(2,1)} async-done(((bf16[512,768]{1,0:T(8,128)(2,1)}), bf16[2048,768]{1,0:T(8,128)(2,1)}) %all-gather.25.cloned.1.call-update) | async-done | bytes 3145744 | tf_op jit(solution)/shard_map/all_gather | solution.py:168
  1654.8 59.0 %reduce-scatter.27.cloned.1.call-done = bf16[512,768]{1,0:T(8,128)(2,1)} async-done(((bf16[2048,768]{1,0:T(8,128)(2,1)}), bf16[512,768]{1,0:T(8,128)(2,1)}) %reduce-scatter.27.cloned.1.call-update) | async-done | bytes 786448 | tf_op jit(solution)/shard_map/reduce_scatter | solution.py:185
  1720.5 63.6 %all-gather.29.cloned.1.call-done = bf16[2048,768]{1,0:T(8,128)(2,1)} async-done(((bf16[512,768]{1,0:T(8,128)(2,1)}), bf16[2048,768]{1,0:T(8,128)(2,1)}) %all-gather.29.cloned.1.call-update) | async-done | bytes 3145744 | tf_op jit(solution)/shard_map/all_gather | solution.py:168
  1789.5 191.2 %while.151 = (s32[]{:T(128)}, f32[2048,3,64]{0,2,1:T(8,128)}, f32[2048,3,64]{0,2,1:T(8,128)}, f32[4,512,3,64]{1,0,3,2:T(4,128)}, s32[4]{0:T(128)S(1)}, /*index=5...) while((s32[]{:T(128)}, f32[2048,3,64]{0,2,1:T(8,128)}, ...), condition=%wide.region_48.49_spmd.clone, body=%wide.region_46.48_spmd.clone.sunk | while | flops 2068850176 | bytes 142548304 | solution.py:155
  2098.2 149.6 %all-reduce.5.cloned.1.call-done = (f32[2,768,3,192]{1,3,2,0:T(8,128)}, f32[2,192,768]{2,1,0:T(8,128)}, f32[2,768,768]{2,1,0:T(8,128)}, f32[2,768,768]{2,1,0:T(8,128)}) async-done(((f32[2,768,3,192]{1,3,2,0:T(8,128)}, f32[2,192,768]{2,1,0:T(8,128)}, f32[2,768,768]{2,1,0:T(8,128)}, f32[2,768,768]{2,1,0:T(8,128)}), (f32[2,768,3,192]{1,3,2,0:T(8,128)}, f32[2,192,768]{2,1,0:T(8,128)}, f32[2,768,768]{2,1,0:T(8,128)}, ...) | async-done | bytes 14155792 | tf_op jit(solution)/shard_map/psum | solution.py:427
  (774 shorter events, 1022.4 us)
Async XLA Ops:
  7.2 73.8 %all-gather.11.cloned.1.call-start = ((), (), s32[]{:S(2)}) async-start(), calls=%async_computation.10 | async-start | bytes 3932160 | tf_op jit(solution)/shard_map/all_gather | solution.py:164
  14.7 288.3 %reduce-scatter.11.cloned.1.call-start = ((), (), s32[]{:S(2)}) async-start(), calls=%async_computation.11 | async-start | bytes 3932160 | tf_op jit(solution)/shard_map/reduce_scatter | solution.py:172
  185.9 174.8 %reduce-scatter.25.cloned.1.call-start = ((), (), s32[]{:S(2)}) async-start(), calls=%async_computation.24 | async-start | bytes 3932160 | tf_op jit(solution)/shard_map/reduce_scatter | solution.py:172
  301.7 129.4 %all-gather.13.cloned.1.call-start = ((), (), s32[]{:S(2)}) async-start(), calls=%async_computation.12 | async-start | bytes 3932160 | tf_op jit(solution)/shard_map/all_gather | solution.py:164
  303.0 196.6 %copy-start.56 = (f32[768]{0:T(1024)}, f32[768]{0:T(1024)S(1)}, u32[]{:S(2)}) copy-start(f32[768]{0:T(1024)S(1)} %get-tuple-element.1157) | copy-start | bytes 9220
  367.4 132.2 %reduce-scatter.13.cloned.1.call-start = ((), (), s32[]{:S(2)}) async-start(), calls=%async_computation.13 | async-start | bytes 3932160 | tf_op jit(solution)/shard_map/reduce_scatter | solution.py:172
  440.5 126.7 %all-gather.15.cloned.1.call-start = ((), (), s32[]{:S(2)}) async-start(), calls=%async_computation.14 | async-start | bytes 3932160 | tf_op jit(solution)/shard_map/all_gather | solution.py:164
  503.6 273.9 %reduce-scatter.15.cloned.1.call-start = ((), (), s32[]{:S(2)}) async-start(), calls=%async_computation.15 | async-start | bytes 3932160 | tf_op jit(solution)/shard_map/reduce_scatter | solution.py:172
  665.4 171.1 %reduce-scatter.19.cloned.1.call-start = ((), (), s32[]{:S(2)}) async-start(), calls=%async_computation.18 | async-start | bytes 3932160 | tf_op jit(solution)/shard_map/reduce_scatter | solution.py:172
  777.4 127.6 %all-gather.21.cloned.1.call-start = ((), (), s32[]{:S(2)}) async-start(), calls=%async_computation.20 | async-start | bytes 3932160 | tf_op jit(solution)/shard_map/all_gather | solution.py:164
  841.3 127.3 %all-gather.19.cloned.1.call-start = ((), (), s32[]{:S(2)}) async-start(), calls=%async_computation.19 | async-start | bytes 3932160 | tf_op jit(solution)/shard_map/all_gather | solution.py:168
  841.9 126.7 %copy-start.105 = (f32[768]{0:T(1024)S(1)}, f32[768]{0:T(1024)}, u32[]{:S(2)}) copy-start(f32[768]{0:T(1024)} %get-tuple-element.1167) | copy-start | bytes 9220
  841.9 201.4 %reduce-scatter.21.cloned.1.call-start = ((), (), s32[]{:S(2)}) async-start(), calls=%async_computation.21 | async-start | bytes 3932160 | tf_op jit(solution)/shard_map/reduce_scatter | solution.py:185
  984.3 129.4 %all-gather.23.cloned.1.call-start = ((), (), s32[]{:S(2)}) async-start(), calls=%async_computation.22 | async-start | bytes 3932160 | tf_op jit(solution)/shard_map/all_gather | solution.py:168
  1050.0 324.1 %reduce-scatter.23.cloned.1.call-start = ((), (), s32[]{:S(2)}) async-start(), calls=%async_computation.23 | async-start | bytes 3932160 | tf_op jit(solution)/shard_map/reduce_scatter | solution.py:185
  1315.0 127.0 %all-gather.17.cloned.1.call-start = ((), (), s32[]{:S(2)}) async-start(), calls=%async_computation.16 | async-start | bytes 3932160 | tf_op jit(solution)/shard_map/all_gather | solution.py:164
  1315.6 126.4 %copy-start.106 = (f32[768]{0:T(1024)S(1)}, f32[768]{0:T(1024)}, u32[]{:S(2)}) copy-start(f32[768]{0:T(1024)} %get-tuple-element.1167) | copy-start | bytes 9220
  1378.3 132.0 %reduce-scatter.17.cloned.1.call-start = ((), (), s32[]{:S(2)}) async-start(), calls=%async_computation.17 | async-start | bytes 3932160 | tf_op jit(solution)/shard_map/reduce_scatter | solution.py:172
  1451.3 124.0 %all-gather.27.cloned.1.call-start = ((), (), s32[]{:S(2)}) async-start(), calls=%async_computation.26 | async-start | bytes 3932160 | tf_op jit(solution)/shard_map/all_gather | solution.py:164
  1451.8 187.6 %all-gather.25.cloned.1.call-start = ((), (), s32[]{:S(2)}) async-start(), calls=%async_computation.25 | async-start | bytes 3932160 | tf_op jit(solution)/shard_map/all_gather | solution.py:168
  1515.1 198.7 %reduce-scatter.27.cloned.1.call-start = ((), (), s32[]{:S(2)}) async-start(), calls=%async_computation.27 | async-start | bytes 3932160 | tf_op jit(solution)/shard_map/reduce_scatter | solution.py:185
  1654.8 129.4 %all-gather.29.cloned.1.call-start = ((), (), s32[]{:S(2)}) async-start(), calls=%async_computation.28 | async-start | bytes 3932160 | tf_op jit(solution)/shard_map/all_gather | solution.py:168
  1720.4 333.5 %reduce-scatter.29.cloned.1.call-start = ((), (), s32[]{:S(2)}) async-start(), calls=%async_computation.29 | async-start | bytes 3932160 | tf_op jit(solution)/shard_map/reduce_scatter | solution.py:185
  1992.0 255.8 %all-reduce.5.cloned.1.call-start = ((), (), s32[]{:S(2)}) async-start(), calls=%async_computation.30 | async-start | bytes 28311552 | tf_op jit(solution)/shard_map/psum | solution.py:427
  (151 other events, 3026.6 us)
Sparse Core Ops, SparseCore 0:
  14.8 66.1 all-gather.10
  186.0 58.8 reduce-scatter.10
  301.8 58.9 reduce-scatter.24
  367.5 63.5 all-gather.12
  440.6 58.8 reduce-scatter.12
  503.7 63.5 all-gather.14
  665.5 58.9 reduce-scatter.14
  777.5 58.9 reduce-scatter.18
  841.4 63.5 all-gather.20
  906.4 62.1 all-gather.18
  984.4 58.8 reduce-scatter.20
  1050.1 63.5 all-gather.22
  1315.1 58.8 reduce-scatter.22
  1378.4 63.5 all-gather.16
  1451.4 58.8 reduce-scatter.16
  1511.8 63.5 all-gather.26
  1577.3 62.1 all-gather.24
  1654.9 58.8 reduce-scatter.26
  1720.6 63.5 all-gather.28
  1992.1 58.8 reduce-scatter.28
  2056.2 191.4 all-reduce.4
where the time goes:
time: 2280 us; the launch traced here: 2270 us
  waiting for transfers between devices  1180 us (52%)
  matrix products  538 us (24%)
  other arithmetic  280 us (12%)
  local copies, waits for them, and re-layouts  137 us (6%)
  blocking collectives  64.4 us (3%)
  loops' own time  50.3 us (2%)
    all_gather x6, waiting for transfers between devices, gather_normed(): return lax.all_gather(normed, 'narrow', axis=0, tiled=True)  376 us
    all_gather x4, waiting for transfers between devices, gather_grads(): return lax.all_gather(grads_in, 'narrow', axis=0, tiled=True)  240 us
    reduce_scatter x6, waiting for transfers between devices, branch_sum(): lax.psum_scatter(jnp.dot(full_rows, weight, preferred_element_type=jnp.fl...  234 us
    reduce_scatter x4, waiting for transfers between devices, input_sum(): lax.psum_scatter(lax.dot_general(grad_full, weight, CONTRACT_COLS, prefer...  176 us
    psum x1, waiting for transfers between devices, per_device(): lax.psum((stacked[0], stacked[1], stacked[2], stacked[3], stacked[4], sta...  150 us
    dot_general x16, matrix products, one_block(): jnp.einsum('hqk,khd->qhd', chances, values, preferred_element_type=jnp.fl...  110 us
    dot_general x16, matrix products, masked_scores(): jnp.einsum('qhd,khd->hqk', query_block, keys_all, preferred_element_type=...  72.5 us
    dynamic_update_slice x16, local copies, waits for them, and re-layouts, attend_backward(): lax.scan(one_block, (zero_keys, zero_keys), (offsets, log_totals))  72.1 us
  transfers between devices with their start and end apart: 21, of which 18 were waited for; matrix products, arithmetic and copies ran while one was open for 12% of the time, Pallas kernels for 0%

commit v1 on v0

v1 whole, which is shorter than its diff:
```python
import functools
import math

import jax
import jax.numpy as jnp
from jax import lax
from jax.experimental import pallas as pl
from jax.experimental.pallas import tpu as pltpu
from jax.sharding import PartitionSpec as P

HEAD_DIM = 64
LEN = 1024
EPSILON = 1e-05
D = 768
QUARTERS = 4
HALF = 256
ROWS = 512
PIECE = 96
HEADS_COLS = 192
PARTS = 576
PACK = 224
MASKED = -1e30
BF = jnp.bfloat16
F32 = jnp.float32
NT = (((1,), (1,)), ((), ()))
TN = (((0,), (0,)), ((), ()))
VMEM_LIMIT = 56 * 1024 * 1024


def dot(a, b):
    return jnp.dot(a, b, preferred_element_type=F32)


def dot_nt(a, b):
    return lax.dot_general(a, b, NT, preferred_element_type=F32)


def dot_tn(a, b):
    return lax.dot_general(a, b, TN, preferred_element_type=F32)


def norm_parts(values):
    center = values - jnp.mean(values, axis=-1, keepdims=True)
    inverse = lax.rsqrt(jnp.mean(center * center, axis=-1, keepdims=True) + EPSILON)
    return center * inverse, inverse


def norm_backward(grad_in, unit_rows, inverse, gain):
    scaled = grad_in * gain
    return inverse * (
        scaled
        - jnp.mean(scaled, axis=-1, keepdims=True)
        - unit_rows * jnp.mean(scaled * unit_rows, axis=-1, keepdims=True)
    )


def swap_halves(u):
    lane = lax.broadcasted_iota(jnp.int32, u.shape, 1)
    return jnp.where((lane & 63) < 32, pltpu.roll(u, 96, axis=1), pltpu.roll(u, 32, axis=1))


def rot(u, cosine, sine):
    return u * cosine + swap_halves(u) * sine


def unrot(u, cosine, sine):
    return u * cosine - swap_halves(u) * sine


HOLDS = [(kb, flip ^ core) for core in (0, 1) for kb in (0, 2) for flip in (0, 2, 4, 6)]


def piece_copies(refs, idx, sems, place):
    w8, z = idx[0], idx[1]
    copies = []
    for (kb, flip), ref in zip(HOLDS, refs):
        for kk in range(2):
            k = kb + kk
            for source, target in place(ref.at[kk], k, (z - k) & 3, w8 ^ flip):
                copies.append(pltpu.make_async_copy(source, target, sems.at[len(copies)]))
    return copies


def rows_at(start, size, unit):
    return pl.ds(pl.multiple_of(start, unit), size)


def mixer_copies(refs, idx, sems, weights):
    def place(src, k, zq, wq):
        return [(src, weights.at[zq, rows_at(wq * PIECE, PIECE, 32)])]

    return piece_copies(refs, idx, sems, place)


def up_down_copies(refs, idx, sems, ups, downs):
    def place(src, k, zq, wq):
        rows = rows_at(wq * PIECE, PIECE, 32)
        return [
            (src.at[pl.ds(0, PIECE)], ups.at[k, rows]),
            (src.at[pl.ds(PIECE, PIECE)], downs.at[k, rows]),
        ]

    return piece_copies(refs, idx, sems, place)


def packed_copies(refs, idx, sems, packed):
    def place(src, k, zq, wq):
        return [(src.at[pl.ds(2 * PIECE, 32)], packed.at[zq, wq])]

    return piece_copies(refs, idx, sems, place)


def unpack_output(packed, weights):
    for zq in range(QUARTERS):
        for chip in range(4):
            for part in range(2):
                for s in range(3):
                    row = HEADS_COLS * zq + 48 * chip + 16 * s
                    weights[row : row + 16, 384 * part : 384 * part + 384] = packed[
                        zq, 2 * chip + part, 16 * (s // 2) : 16 * (s // 2) + 16, 384 * (s % 2) : 384 * (s % 2) + 384
                    ]


def any_spec():
    return pl.BlockSpec(memory_space=pl.ANY)


def vmem_spec():
    return pl.BlockSpec(memory_space=pltpu.VMEM)


def smem_spec():
    return pl.BlockSpec(memory_space=pltpu.SMEM)


def kernel_call(body, in_specs, out_shape, out_specs, scratch, args, flops, moved, aliases=None, name=None):
    return pl.pallas_call(
        body,
        in_specs=in_specs,
        out_specs=out_specs,
        out_shape=out_shape,
        scratch_shapes=scratch,
        input_output_aliases=aliases or {},
        compiler_params=pltpu.CompilerParams(vmem_limit_bytes=VMEM_LIMIT),
        cost_estimate=pl.CostEstimate(flops=int(flops), bytes_accessed=int(moved), transcendentals=0),
        name=name,
    )(*args)


def sds(shape, dtype):
    return jax.ShapeDtypeStruct(shape, dtype)


def project_body(idx, x, gain, shift, bias, cosine, sine, *rest):
    pieces, (h1, q, kv0, kv1, weights, wide, sems) = rest[:16], rest[16:]
    copies = mixer_copies(pieces, idx, sems, weights)
    for copy in copies:
        copy.start()

    def norm_rows(i, carry):
        rows = rows_at(i * 128, 128, 128)
        unit, _ = norm_parts(x[rows])
        h1[rows] = (unit * gain[...] + shift[...]).astype(BF)
        return carry

    lax.fori_loop(0, 4, norm_rows, 0)
    for copy in copies:
        copy.wait()
    for zq in range(QUARTERS):
        k = (idx[1] - zq) & 3
        p = dot(h1[...], weights[zq]) + bias[k]
        for part in range(3):
            col = D * part + HEADS_COLS * zq
            wide[:, col : col + HEADS_COLS] = p[:, HEADS_COLS * part : HEADS_COLS * (part + 1)]
    for half, kv in ((0, kv0), (1, kv1)):
        rows = slice(HALF * half, HALF * (half + 1))
        for j in range(6):
            cols = slice(128 * j, 128 * (j + 1))
            q[rows, cols] = (rot(wide[rows, cols], cosine[rows], sine[rows]) * 0.125).astype(BF)
            kcols = slice(D + 128 * j, D + 128 * (j + 1))
            kv[:, cols] = rot(wide[rows, kcols], cosine[rows], sine[rows]).astype(BF)
        kv[:, D:] = wide[rows, 2 * D :].astype(BF)


def project(idx, x, gain, shift, bias, cosine, sine, pieces):
    return kernel_call(
        project_body,
        [smem_spec()] + [vmem_spec()] * 6 + [any_spec()] * 16,
        [sds((ROWS, D), BF), sds((ROWS, D), BF), sds((HALF, 2 * D), BF), sds((HALF, 2 * D), BF)],
        [vmem_spec()] * 4,
        [
            pltpu.VMEM((QUARTERS, D, PARTS), BF),
            pltpu.VMEM((ROWS, 3 * D), F32),
            pltpu.SemaphoreType.DMA((32,)),
        ],
        (idx, x, gain, shift, bias, cosine, sine, *pieces),
        2 * ROWS * D * 3 * D,
        8e6,
        name="project",
    )


def load_keys(idx, own, near, far, far_near, kvn, kvc, kvr, sems):
    clean = idx[2] == 1
    waits = []
    for half in range(2):
        rows = pl.ds(HALF * half, HALF)
        copy = pltpu.make_async_copy(own[half], kvn.at[rows], sems.at[half])
        copy.start()
        waits.append(copy)
        for base, target, when_clean, when_noisy in ((2, kvc, own, near), (4, kvr, far, far_near)):
            sem = sems.at[base + half]
            a = pltpu.make_async_copy(when_clean[half], target.at[rows], sem)
            b = pltpu.make_async_copy(when_noisy[half], target.at[rows], sem)
            pl.when(clean)(a.start)
            pl.when(jnp.logical_not(clean))(b.start)
            waits.append(a)
    return waits


TILES = {
    0: [(0, [("c", 0, True)]), (1, [("c", 1, True), ("c", 0, False), ("r", 0, False), ("r", 1, False)])],
    1: [(1, [("c", 1, True), ("r", 0, False)]), (0, [("c", 0, True), ("c", 1, False), ("r", 0, False)])],
}


def attend_body(idx, q, kv0, kv1, c0, c1, r0, r1, n0, n1, o, lse, kvn, kvc, kvr, bias, bias_n, lcol, sems):
    waits = load_keys(idx, (kv0, kv1), (c0, c1), (r0, r1), (n0, n1), kvn, kvc, kvr, sems)
    clean, level = idx[2], idx[4]
    qi = lax.shift_right_logical(lax.broadcasted_iota(jnp.int32, (HALF, HALF), 0), level)
    ki = lax.shift_right_logical(lax.broadcasted_iota(jnp.int32, (HALF, HALF), 1), level)
    bias[...] = jnp.where(ki < qi + clean, 0.0, MASKED)
    same = jnp.where(ki == qi, 0, 1) + clean
    bias_n[...] = jnp.where(same[:128, :128] == 0, 0.0, MASKED)
    lcol[...] = jnp.zeros_like(lcol)
    for copy in waits:
        copy.wait()
    keys = {"c": kvc, "r": kvr}

    def run(tiles):
        def pair(hp, carry):
            off = pl.multiple_of(hp * 128, 128)
            cols = pl.ds(off, 128)
            vcols = pl.ds(pl.multiple_of(D + off, 128), 128)
            low_lane = lax.broadcasted_iota(jnp.int32, (HALF, 128), 1) < 64
            lane = lax.broadcasted_iota(jnp.int32, (HALF, 128), 1)
            ones = jnp.ones((HALF, 128), BF)
            for half, sources in tiles:
                rows = slice(HALF * half, HALF * (half + 1))
                q2 = q[rows, cols]
                sides = []
                for side in range(2):
                    qm = jnp.where(low_lane if side == 0 else jnp.logical_not(low_lane), q2, jnp.zeros_like(q2))
                    scores = []
                    for which, kh, diagonal in sources:
                        s = dot_nt(qm, keys[which][HALF * kh : HALF * (kh + 1), cols])
                        scores.append(s + bias[...] if diagonal else s)
                    own = [
                        dot_nt(qm[128 * t : 128 * (t + 1)], kvn[HALF * half + 128 * t : HALF * half + 128 * (t + 1), cols])
                        + bias_n[...]
                        for t in range(2)
                    ]
                    top = functools.reduce(jnp.maximum, [jnp.max(s, axis=-1, keepdims=True) for s in scores])
                    top = jnp.maximum(
                        top, jnp.concatenate([jnp.max(s, axis=-1, keepdims=True) for s in own], axis=0)
                    )
                    total = jnp.concatenate(
                        [
                            dot(
                                jnp.exp(own[t] - top[128 * t : 128 * (t + 1)]).astype(BF),
                                jnp.concatenate(
                                    [
                                        kvn[HALF * half + 128 * t : HALF * half + 128 * (t + 1), vcols],
                                        ones[:128],
                                    ],
                                    axis=1,
                                ),
                            )
                            for t in range(2)
                        ],
                        axis=0,
                    )
                    for s, (which, kh, diagonal) in zip(scores, sources):
                        v2 = jnp.concatenate([keys[which][HALF * kh : HALF * (kh + 1), vcols], ones], axis=1)
                        total = total + dot(jnp.exp(s - top).astype(BF), v2)
                    count = total[:, 128:]
                    sides.append((total[:, :128] / count, top + jnp.log(count)))
                o[rows, cols] = jnp.where(low_lane, sides[0][0], sides[1][0]).astype(BF)
                lcol[rows] = jnp.where(
                    lane == 2 * hp, sides[0][1], jnp.where(lane == 2 * hp + 1, sides[1][1], lcol[rows])
                )
            return carry

        lax.fori_loop(0, 6, pair, 0)

    for zl in range(2):
        pl.when(idx[3] == zl)(functools.partial(run, TILES[zl]))
    across = jnp.transpose(lcol[...])
    for head in range(12):
        lse[head] = across[head : head + 1]


def attend(idx, q, keys):
    return kernel_call(
        attend_body,
        [smem_spec(), vmem_spec()] + [any_spec()] * 8,
        [sds((ROWS, D), BF), sds((12, 1, ROWS), F32)],
        [vmem_spec()] * 2,
        [
            pltpu.VMEM((ROWS, 2 * D), BF),
            pltpu.VMEM((ROWS, 2 * D), BF),
            pltpu.VMEM((ROWS, 2 * D), BF),
            pltpu.VMEM((HALF, HALF), F32),
            pltpu.VMEM((128, 128), F32),
            pltpu.VMEM((ROWS, 128), F32),
            pltpu.SemaphoreType.DMA((6,)),
        ],
        (idx, q, *keys),
        12e9,
        6e6,
        name="attend",
    )


def feed_body(idx, x, o, gain, shift, out_bias, down_bias, up_bias, *rest):
    pieces, (x2, x1, h2, g, gp, ups, downs, packed, outw, sems, sems_o) = rest[:16], rest[16:]
    first = packed_copies(pieces, idx, sems_o, packed)
    later = up_down_copies(pieces, idx, sems, ups, downs)
    for copy in first + later:
        copy.start()
    for copy in first:
        copy.wait()
    unpack_output(packed, outw)
    x1[...] = x[...] + (dot(o[...], outw[...]) + out_bias[...])

    def norm_rows(i, carry):
        rows = rows_at(i * 128, 128, 128)
        unit, _ = norm_parts(x1[rows])
        h2[rows] = (unit * gain[...] + shift[...]).astype(BF)
        x2[rows] = x1[rows] + down_bias[...]
        return carry

    lax.fori_loop(0, 4, norm_rows, 0)
    for copy in later:
        copy.wait()

    def hidden(k, carry):
        for n in range(3):
            cols = slice(256 * n, 256 * (n + 1))
            u = dot(h2[...], ups[k, :, cols]) + up_bias[k, :, cols]
            uu = u * u
            t = jnp.tanh(0.7978845608028654 * u * (1.0 + 0.044715 * uu))
            half_t = 0.5 + 0.5 * t
            g[k, :, cols] = (u * half_t).astype(BF)
            slope = half_t + (0.5 * 0.7978845608028654) * u * (1.0 - t * t) * (1.0 + 0.134145 * uu)
            gp[k, :, cols] = slope.astype(BF)
        x2[...] += dot(g[k], downs[k])
        return carry

    lax.fori_loop(0, QUARTERS, hidden, 0)


WEIGHT_SCRATCH = [
    ((QUARTERS, D, D), BF),
    ((QUARTERS, D, D), BF),
    ((QUARTERS, 8, 32, D), BF),
    ((D, D), BF),
]


def feed(idx, x, o, gain, shift, out_bias, down_bias, up_bias, pieces):
    return kernel_call(
        feed_body,
        [smem_spec()] + [vmem_spec()] * 7 + [any_spec()] * 16,
        [
            sds((ROWS, D), F32),
            sds((ROWS, D), F32),
            sds((ROWS, D), BF),
            sds((QUARTERS, ROWS, D), BF),
            sds((QUARTERS, ROWS, D), BF),
        ],
        [vmem_spec()] * 5,
        [pltpu.VMEM(s, t) for s, t in WEIGHT_SCRATCH]
        + [pltpu.SemaphoreType.DMA((64,)), pltpu.SemaphoreType.DMA((32,))],
        (idx, x, o, gain, shift, out_bias, down_bias, up_bias, *pieces),
        2 * ROWS * D * D * 9,
        25e6,
        name="feed",
    )


def feed_back_body(idx, e, x1, gp, gain, *rest):
    pieces, (dm, dz, e1, da, do, small, ups, downs, packed, outw, dh2, hidden_sums, sems, sems_o) = rest[:16], rest[16:]
    first = packed_copies(pieces, idx, sems_o, packed)
    later = up_down_copies(pieces, idx, sems, ups, downs)
    for copy in later + first:
        copy.start()
    dm[...] = e[...].astype(BF)
    small[4:5] = jnp.sum(dm[...].astype(F32), axis=0, keepdims=True)
    dh2[...] = jnp.zeros_like(dh2)
    for copy in later:
        copy.wait()

    def hidden(k, carry):
        zq = (idx[1] - k) & 3
        for n in range(3):
            cols = slice(256 * n, 256 * (n + 1))
            part = (dot_nt(dm[...], downs[k, cols]) * gp[k, :, cols].astype(F32)).astype(BF)
            dz[k, :, cols] = part
            hidden_sums[zq, :, cols] = jnp.sum(part.astype(F32), axis=0, keepdims=True)
        dh2[...] += dot_nt(dz[k], ups[k])
        return carry

    lax.fori_loop(0, QUARTERS, hidden, 0)
    for copy in first:
        copy.wait()
    unpack_output(packed, outw)
    for zq in range(QUARTERS):
        small[zq : zq + 1] = hidden_sums[zq]
    small[5:8] = jnp.zeros((3, D), F32)

    def norm_rows(i, carry):
        rows = rows_at(i * 128, 128, 128)
        unit, inverse = norm_parts(x1[rows])
        grad = dh2[rows]
        up = e[rows] + norm_backward(grad, unit, inverse, gain[...])
        e1[rows] = up
        low = up.astype(BF)
        da[rows] = low
        small[5:6] += jnp.sum(low.astype(F32), axis=0, keepdims=True)
        small[6:7] += jnp.sum(grad * unit, axis=0, keepdims=True)
        small[7:8] += jnp.sum(grad, axis=0, keepdims=True)
        return carry

    lax.fori_loop(0, 4, norm_rows, 0)
    do[...] = dot_nt(da[...], outw[...]).astype(BF)


def feed_back(idx, e, x1, gp, gain, pieces):
    return kernel_call(
        feed_back_body,
        [smem_spec()] + [vmem_spec()] * 4 + [any_spec()] * 16,
        [
            sds((ROWS, D), BF),
            sds((QUARTERS, ROWS, D), BF),
            sds((ROWS, D), F32),
            sds((ROWS, D), BF),
            sds((ROWS, D), BF),
            sds((8, D), F32),
        ],
        [vmem_spec()] * 6,
        [pltpu.VMEM(s, t) for s, t in WEIGHT_SCRATCH]
        + [pltpu.VMEM((ROWS, D), F32), pltpu.VMEM((QUARTERS, 1, D), F32), pltpu.SemaphoreType.DMA((64,)), pltpu.SemaphoreType.DMA((32,))],
        (idx, e, x1, gp, gain, *pieces),
        2 * ROWS * D * D * 9,
        25e6,
        name="feed_back",
    )


def spread(idx, keep, send, source, k, wq, rows, sem):
    w8, mine = idx[0], idx[2]
    j = (wq >> 1) ^ (w8 >> 1)
    a = pltpu.make_async_copy(source, keep.at[j, k, rows], sem)
    b = pltpu.make_async_copy(source, send.at[j, k, rows], sem)
    pl.when((wq & 1) == mine)(a.start)
    pl.when((wq & 1) != mine)(b.start)
    return a


def feed_grads_body(idx, g, dm, h2, dz, o, da, keep, send, flipped, turned, d_up, d_down, d_out, sems):
    waits = []
    flipped[...] = jnp.transpose(o[...])
    turned[...] = dot(flipped[...], da[...]).astype(BF)
    for zq in range(QUARTERS):
        for chip in range(4):
            for part in range(2):
                for s in range(4):
                    rows, cols = slice(16 * (s // 2), 16 * (s // 2) + 16), slice(384 * (s % 2), 384 * (s % 2) + 384)
                    if s == 3:
                        block = jnp.zeros((16, 384), BF)
                    else:
                        row = HEADS_COLS * zq + 48 * chip + 16 * s
                        block = turned[row : row + 16, 384 * part : 384 * part + 384]
                    d_out[zq, 2 * chip + part, rows, cols] = block
    for zq in range(QUARTERS):
        k = (idx[1] - zq) & 3
        for wq in range(8):
            sem = sems.at[len(waits)]
            waits.append(spread(idx, keep, send, d_out.at[zq, wq], k, wq, pl.ds(2 * PIECE, 32), sem))
    for k in range(QUARTERS):
        flipped[...] = jnp.transpose(g[k])
        d_down[k] = dot(flipped[...], dm[...]).astype(BF)
        for wq in range(8):
            sem = sems.at[len(waits)]
            source = d_down.at[k, pl.ds(PIECE * wq, PIECE)]
            waits.append(spread(idx, keep, send, source, k, wq, pl.ds(PIECE, PIECE), sem))
    flipped[...] = jnp.transpose(h2[...])
    for k in range(QUARTERS):
        d_up[k] = dot(flipped[...], dz[k]).astype(BF)
        for wq in range(8):
            sem = sems.at[len(waits)]
            source = d_up.at[k, pl.ds(PIECE * wq, PIECE)]
            waits.append(spread(idx, keep, send, source, k, wq, pl.ds(0, PIECE), sem))
    for copy in waits:
        copy.wait()


def feed_grads(idx, g, dm, h2, dz, o, da):
    return kernel_call(
        feed_grads_body,
        [smem_spec()] + [vmem_spec()] * 6,
        [sds((4, QUARTERS, PACK, D), BF)] * 2,
        [any_spec()] * 2,
        [
            pltpu.VMEM((D, ROWS), BF),
            pltpu.VMEM((D, D), BF),
            pltpu.VMEM((QUARTERS, D, D), BF),
            pltpu.VMEM((QUARTERS, D, D), BF),
            pltpu.VMEM((QUARTERS, 8, 32, D), BF),
            pltpu.SemaphoreType.DMA((96,)),
        ],
        (idx, g, dm, h2, dz, o, da),
        2 * ROWS * D * D * 9,
        25e6,
        name="feed_grads",
    )


def attend_back_body(
    idx, q, do, o, lse, kv0, kv1, c0, c1, r0, r1, n0, n1, dq, dn, dc0, dc1, dr0, dr1, kvn, kvc, kvr, bias, bias_n, dcol, drow, sems
):
    waits = load_keys(idx, (kv0, kv1), (c0, c1), (r0, r1), (n0, n1), kvn, kvc, kvr, sems)
    clean, level = idx[2], idx[4]
    ki = lax.shift_right_logical(lax.broadcasted_iota(jnp.int32, (HALF, HALF), 0), level)
    qi = lax.shift_right_logical(lax.broadcasted_iota(jnp.int32, (HALF, HALF), 1), level)
    bias[...] = jnp.where(ki < qi + clean, 0.0, MASKED)
    same = jnp.where(ki == qi, 0, 1) + clean
    bias_n[...] = jnp.where(same[:128, :128] == 0, 0.0, MASKED)
    dcol[...] = jnp.zeros_like(dcol)

    def products(hp, carry):
        cols = pl.ds(pl.multiple_of(hp * 128, 128), 128)
        lane = lax.broadcasted_iota(jnp.int32, (ROWS, 128), 1)
        both = do[:, cols].astype(F32) * o[:, cols].astype(F32)
        first = jnp.sum(jnp.where(lane < 64, both, 0.0), axis=-1, keepdims=True)
        second = jnp.sum(jnp.where(lane < 64, 0.0, both), axis=-1, keepdims=True)
        dcol[...] = jnp.where(lane == 2 * hp, first, jnp.where(lane == 2 * hp + 1, second, dcol[...]))
        return carry

    lax.fori_loop(0, 6, products, 0)
    across = jnp.transpose(dcol[...])
    for head in range(12):
        drow[head] = across[head : head + 1]
    for copy in waits:
        copy.wait()
    keys = {"c": kvc, "r": kvr}
    outs = {("c", 0): dc0, ("c", 1): dc1, ("r", 0): dr0, ("r", 1): dr1}

    def run(tiles):
        by_key = {}
        for half, sources in tiles:
            for which, kh, diagonal in sources:
                by_key.setdefault((which, kh), []).append((half, diagonal))

        def pair(hp, carry):
            off = pl.multiple_of(hp * 128, 128)
            cols = pl.ds(off, 128)
            vcols = pl.ds(pl.multiple_of(D + off, 128), 128)

            def lows(n):
                low_lane = lax.broadcasted_iota(jnp.int32, (n, 128), 1) < 64
                return low_lane, jnp.logical_not(low_lane)

            def masked(v, side):
                return jnp.where(lows(v.shape[0])[side], v, jnp.zeros_like(v))

            def tile(k2, v2, qrow, n, bias_here):
                dk = dv = dqs = None
                q2, g2 = q[qrow : qrow + n, cols], do[qrow : qrow + n, cols]
                for side in range(2):
                    qm, gm, km = masked(q2, side), masked(g2, side), masked(k2, side)
                    head = 2 * hp + side
                    s = dot_nt(k2, qm)
                    if bias_here is not None:
                        s = s + bias_here
                    p = jnp.exp(s - lse[head, :, qrow : qrow + n])
                    dp = dot_nt(v2, gm)
                    ds = (p * (dp - drow[head, :, qrow : qrow + n])).astype(BF)
                    parts = (dot(ds, qm), dot(p.astype(BF), gm), dot_tn(ds, km))
                    if dk is None:
                        dk, dv, dqs = parts
                    else:
                        dk, dv, dqs = dk + parts[0], dv + parts[1], dqs + parts[2]
                return dk, dv, dqs

            dq_half = [None, None]
            for half in range(2):
                pieces = []
                for t in range(2):
                    row = HALF * half + 128 * t
                    dk, dv, dqs = tile(kvn[row : row + 128, cols], kvn[row : row + 128, vcols], row, 128, bias_n[...])
                    dn[row : row + 128, cols] = dk.astype(BF)
                    dn[row : row + 128, vcols] = dv.astype(BF)
                    pieces.append(dqs)
                dq_half[half] = jnp.concatenate(pieces, axis=0)
            for key in (("c", 0), ("c", 1), ("r", 0), ("r", 1)):
                if key not in by_key:
                    outs[key][:, cols] = jnp.zeros((HALF, 128), BF)
                    outs[key][:, vcols] = jnp.zeros((HALF, 128), BF)
                    continue
                krow = HALF * key[1]
                k2 = keys[key[0]][krow : krow + HALF, cols]
                v2 = keys[key[0]][krow : krow + HALF, vcols]
                total_k = total_v = None
                for half, diagonal in by_key[key]:
                    dk, dv, dqs = tile(k2, v2, HALF * half, HALF, bias[...] if diagonal else None)
                    total_k = dk if total_k is None else total_k + dk
                    total_v = dv if total_v is None else total_v + dv
                    dq_half[half] = dq_half[half] + dqs
                outs[key][:, cols] = total_k.astype(BF)
                outs[key][:, vcols] = total_v.astype(BF)
            for half in range(2):
                dq[HALF * half : HALF * (half + 1), cols] = dq_half[half] * 0.125
            return carry

        lax.fori_loop(0, 6, pair, 0)

    for zl in range(2):
        pl.when(idx[3] == zl)(functools.partial(run, TILES[zl]))


def attend_back(idx, q, do, o, lse, keys):
    return kernel_call(
        attend_back_body,
        [smem_spec()] + [vmem_spec()] * 4 + [any_spec()] * 8,
        [sds((ROWS, D), F32), sds((ROWS, 2 * D), BF)] + [sds((HALF, 2 * D), BF)] * 4,
        [vmem_spec()] * 6,
        [
            pltpu.VMEM((ROWS, 2 * D), BF),
            pltpu.VMEM((ROWS, 2 * D), BF),
            pltpu.VMEM((ROWS, 2 * D), BF),
            pltpu.VMEM((HALF, HALF), F32),
            pltpu.VMEM((128, 128), F32),
            pltpu.VMEM((ROWS, 128), F32),
            pltpu.VMEM((12, 1, ROWS), F32),
            pltpu.SemaphoreType.DMA((6,)),
        ],
        (idx, q, do, o, lse, *keys),
        30e9,
        12e6,
        name="attend_back",
    )


def project_back_body(idx, dq, dn, dc0, dc1, tc0, tc1, tr0, tr1, cosine, sine, x, e1, gain, *rest):
    pieces, (dpz, e, small, weights, wide, sems) = rest[:16], rest[16:]
    copies = mixer_copies(pieces, idx, sems, weights)
    for copy in copies:
        copy.start()
    noisy = idx[2] == 0
    for half, (dc, tc, tr) in enumerate(((dc0, tc0, tr0), (dc1, tc1, tr1))):
        rows = slice(HALF * half, HALF * (half + 1))
        for j in range(6):
            cols = slice(128 * j, 128 * (j + 1))
            wide[rows, cols] = unrot(dq[rows, cols], cosine[rows], sine[rows])

        def total(cols, half_rows=rows, dc=dc, tc=tc, tr=tr):
            summed = dc[:, cols].astype(F32) + tc[:, cols].astype(F32) + tr[:, cols].astype(F32)
            return jnp.where(noisy, dn[half_rows, cols].astype(F32), summed)

        for j in range(6):
            cols = slice(128 * j, 128 * (j + 1))
            wide[rows, D + 128 * j : D + 128 * (j + 1)] = unrot(total(cols), cosine[rows], sine[rows])
        wide[rows, 2 * D :] = total(slice(D, 2 * D))
    for copy in copies:
        copy.wait()
    small[...] = jnp.zeros_like(small)
    for zq in range(QUARTERS):
        for part in range(3):
            col = D * part + HEADS_COLS * zq
            dpz[zq, :, HEADS_COLS * part : HEADS_COLS * (part + 1)] = wide[:, col : col + HEADS_COLS].astype(BF)
        small[zq : zq + 1, :PARTS] = jnp.sum(dpz[zq].astype(F32), axis=0, keepdims=True)
        piece = dot_nt(dpz[zq], weights[zq])
        if zq == 0:
            e[...] = piece
        else:
            e[...] += piece

    def norm_rows(i, carry):
        rows = rows_at(i * 128, 128, 128)
        unit, inverse = norm_parts(x[rows])
        grad = e[rows]
        small[4:5] += jnp.sum(grad * unit, axis=0, keepdims=True)
        small[5:6] += jnp.sum(grad, axis=0, keepdims=True)
        e[rows] = e1[rows] + norm_backward(grad, unit, inverse, gain[...])
        return carry

    lax.fori_loop(0, 4, norm_rows, 0)


def project_back(idx, dq, dn, dc, tc, tr, cosine, sine, x, e1, gain, pieces):
    return kernel_call(
        project_back_body,
        [smem_spec()] + [vmem_spec()] * 13 + [any_spec()] * 16,
        [sds((QUARTERS, ROWS, PARTS), BF), sds((ROWS, D), F32), sds((8, D), F32)],
        [vmem_spec()] * 3,
        [
            pltpu.VMEM((QUARTERS, D, PARTS), BF),
            pltpu.VMEM((ROWS, 3 * D), F32),
            pltpu.SemaphoreType.DMA((32,)),
        ],
        (idx, dq, dn, *dc, *tc, *tr, cosine, sine, x, e1, gain, *pieces),
        2 * ROWS * D * 3 * D,
        12e6,
        name="project_back",
    )


def project_grads_body(idx, h1, dpz, keep, send, flipped, stage, sems):
    waits = []
    flipped[...] = jnp.transpose(h1[...])
    for zq in range(QUARTERS):
        k = (idx[1] - zq) & 3
        stage[zq] = dot(flipped[...], dpz[zq]).astype(BF)
        for wq in range(8):
            sem = sems.at[len(waits)]
            source = stage.at[zq, pl.ds(PIECE * wq, PIECE)]
            waits.append(spread(idx, keep, send, source, k, wq, pl.ds(0, PIECE), sem))
    for copy in waits:
        copy.wait()


def project_grads(idx, h1, dpz):
    return kernel_call(
        project_grads_body,
        [smem_spec()] + [vmem_spec()] * 2,
        [sds((4, QUARTERS, PIECE, PARTS), BF)] * 2,
        [any_spec()] * 2,
        [
            pltpu.VMEM((D, ROWS), BF),
            pltpu.VMEM((QUARTERS, D, PARTS), BF),
            pltpu.SemaphoreType.DMA((32,)),
        ],
        (idx, h1, dpz),
        2 * ROWS * D * 3 * D,
        9e6,
        name="project_grads",
    )


def finish_mixer_body(layer, filled, idx, *rest):
    pieces, rest = rest[:8], rest[8:]
    if filled:
        rest = rest[1:]
    out, stage, sem = rest
    for flip, piece in enumerate(pieces):
        stage[rows_at((idx[0] ^ flip) * PIECE, PIECE, 32)] = piece[...].astype(F32)
    copy = pltpu.make_async_copy(stage, out.at[layer], sem)
    copy.start()
    copy.wait()


def finish_mixer(idx, layer, layers, pieces, before):
    filled = before is not None
    return kernel_call(
        functools.partial(finish_mixer_body, layer, filled),
        [smem_spec()] + [vmem_spec()] * 8 + [any_spec()] * filled,
        sds((layers, D, PARTS), F32),
        any_spec(),
        [pltpu.VMEM((D, PARTS), F32), pltpu.SemaphoreType.DMA],
        (idx, *pieces) + ((before,) if filled else ()),
        1e6,
        4e6,
        aliases={9: 0} if filled else None,
        name="finish_mixer",
    )


def finish_feed_body(layer, filled, idx, *rest):
    pieces, rest = rest[:8], rest[8:]
    if filled:
        rest = rest[3:]
    up, down, out, up_s, down_s, out_s, sems = rest
    for flip, piece in enumerate(pieces):
        wq = idx[0] ^ flip
        rows = rows_at(wq * PIECE, PIECE, 32)
        up_s[rows] = piece[:PIECE].astype(F32)
        down_s[rows] = piece[PIECE : 2 * PIECE].astype(F32)
        cols = pl.ds(pl.multiple_of((wq & 1) * 384, 128), 384)
        for s in range(3):
            row = 2 * PIECE + 16 * (s // 2)
            block = piece[row : row + 16, 384 * (s % 2) : 384 * (s % 2) + 384]
            out_s[rows_at((wq >> 1) * 48 + 16 * s, 16, 16), cols] = block.astype(F32)
    copies = [
        pltpu.make_async_copy(stage, whole.at[layer], sems.at[i])
        for i, (stage, whole) in enumerate(((up_s, up), (down_s, down), (out_s, out)))
    ]
    for copy in copies:
        copy.start()
    for copy in copies:
        copy.wait()


def finish_feed(idx, layer, layers, pieces, before):
    filled = before is not None
    return kernel_call(
        functools.partial(finish_feed_body, layer, filled),
        [smem_spec()] + [vmem_spec()] * 8 + [any_spec()] * (3 * filled),
        [sds((layers, D, D), F32), sds((layers, D, D), F32), sds((layers, HEADS_COLS, D), F32)],
        [any_spec()] * 3,
        [
            pltpu.VMEM((D, D), F32),
            pltpu.VMEM((D, D), F32),
            pltpu.VMEM((HEADS_COLS, D), F32),
            pltpu.SemaphoreType.DMA((3,)),
        ],
        (idx, *pieces) + (tuple(before) if filled else ()),
        1e6,
        8e6,
        aliases={9: 0, 10: 1, 11: 2} if filled else None,
        name="finish_feed",
    )


def flip_wide(x, bit):
    return lax.ppermute(x, "wide", [(i, i ^ bit) for i in range(lax.axis_size("wide"))])


def shift_narrow(x, k):
    return lax.ppermute(x, "narrow", [(i, (i + k) % QUARTERS) for i in range(QUARTERS)])


def gather_pieces(piece):
    r = [piece] + [shift_narrow(piece, k) for k in range(1, QUARTERS)]
    p, q = jnp.stack(r[:2]), jnp.stack(r[2:])
    px, qy = flip_wide(p, 2), flip_wide(q, 4)
    py, qx = flip_wide(p, 4), flip_wide(q, 2)
    pxy, qxy = flip_wide(px, 4), flip_wide(qy, 2)
    here = [p, px, py, pxy, q, qx, qy, qxy]
    return here + [flip_wide(x, 1) for x in here]


def added(*terms):
    return functools.reduce(jnp.add, [t.astype(F32) for t in terms]).astype(BF)


def reduce_pieces(keep, send):
    got = flip_wide(send, 1)

    def both(js, ks):
        return added(keep[js, ks], got[js, ks])

    first, second = slice(0, 2), slice(2, 4)
    px = flip_wide(both(slice(1, 4, 2), first), 2)
    qy = flip_wide(both(slice(2, 4), second), 4)
    p = added(both(slice(0, 4, 2), first), px)
    q = added(both(slice(0, 2), second), qy)
    p = added(p[0], flip_wide(p[1], 4))
    q = added(q[0], flip_wide(q[1], 2))
    bit = 8
    while bit < lax.axis_size("wide"):
        p, q = added(p, flip_wide(p, bit)), added(q, flip_wide(q, bit))
        bit *= 2
    total = added(p[0], shift_narrow(p[1], -1), shift_narrow(q[0], -2), shift_narrow(q[1], -3))
    x, y = flip_wide(total, 2), flip_wide(total, 4)
    here = [total, x, y, flip_wide(x, 4)]
    there = [flip_wide(t, 1) for t in here]
    return [t for pair in zip(here, there) for t in pair]


def reduce_small(values):
    bit = 1
    while bit < lax.axis_size("wide"):
        values = values + flip_wide(values, bit)
        bit *= 2
    for bit in (1, 2):
        values = values + lax.ppermute(values, "narrow", [(i, i ^ bit) for i in range(QUARTERS)])
    return values


def device_pairs(move):
    pairs = []
    for w in range(lax.axis_size("wide")):
        for z in range(QUARTERS):
            target = move(w, z)
            if target is not None:
                pairs.append((w * QUARTERS + z, target[0] * QUARTERS + target[1]))
    return pairs


BOTH = ("wide", "narrow")


def relocate(rows):
    first = device_pairs(lambda w, z: ((w & ~1) | (z >> 1), ((w & 1) << 1) | (z & 1)))
    second = device_pairs(lambda w, z: ((w & ~1) | (z >> 1), ((w & 1) << 1) | (1 - (z & 1))))
    return lax.ppermute(rows[:HALF], BOTH, first), lax.ppermute(rows[HALF:], BOTH, second)


def between_chips(x, low_from):
    pairs = device_pairs(lambda w, z: (w, z ^ 1) if (w & 1) and (z & 1) in low_from else None)
    return lax.ppermute(x, BOTH, pairs)


def within_chip(x, source):
    pairs = [(i, i ^ 1) for i in range(lax.axis_size("wide")) if (i & 1) == source]
    return lax.ppermute(x, "wide", pairs)


def per_device(
    tokens,
    block_size,
    norm_gain,
    norm_shift,
    mixer_weight,
    mixer_bias,
    output_weight,
    output_bias,
    up_weight,
    up_bias,
    down_weight,
    cotangent,
):
    layers = norm_gain.shape[0]
    w, z = lax.axis_index("wide"), lax.axis_index("narrow")
    w8, core, low = w & 7, w & 1, z & 1
    sizes = jnp.where((z >> 1) == core, block_size, flip_wide(block_size, 1))[0]
    level = 2 + (sizes >= 8).astype(jnp.int32) + (sizes >= 16).astype(jnp.int32)
    idx = jnp.stack([w8, z, core, low, level, w8, w8, w8]).astype(jnp.int32)

    bases = jnp.where(low == 0, jnp.array([0, 768]), jnp.array([512, 256]))
    position = (bases[:, None] + jnp.arange(HALF)[None, :]).reshape(ROWS).astype(F32)
    halfway = HEAD_DIM // 2
    frequency = jnp.exp(jnp.arange(halfway, dtype=F32) * (-math.log(10000.0) / halfway))
    angle = position[:, None] * frequency[None, :]
    cosine = jnp.tile(jnp.cos(angle), (1, 4))
    sine = jnp.sin(angle)
    sine = jnp.concatenate([-sine, sine, -sine, sine], axis=1)

    def bias_pieces(layer):
        return mixer_bias[layer].reshape(PARTS), up_bias[layer]

    biases = jnp.concatenate([t for layer in range(layers) for t in bias_pieces(layer)])
    biases = jnp.stack([biases] + [shift_narrow(biases, k) for k in range(1, QUARTERS)])
    width = PARTS + D
    mixer_biases = [biases[:, None, width * layer : width * layer + PARTS] for layer in range(layers)]
    up_biases = [biases[:, None, width * layer + PARTS : width * (layer + 1)] for layer in range(layers)]

    def rows_of(weight, layer, start, count):
        return lax.dynamic_slice_in_dim(weight[layer], start, count, 0)

    def packed_output(layer):
        block = rows_of(output_weight, layer, (w8 >> 1) * 48, 48)
        block = lax.dynamic_slice_in_dim(block, core * 384, 384, 1).reshape(3, 16, 384)
        block = jnp.concatenate([block, jnp.zeros((1, 16, 384), BF)]).reshape(2, 2, 16, 384)
        return block.transpose(0, 2, 1, 3).reshape(32, D)

    mixer_pieces, feed_pieces = [], []
    for layer in range(layers):
        piece = rows_of(mixer_weight, layer, w8 * PIECE, PIECE).reshape(PIECE, PARTS)
        mixer_pieces.append(gather_pieces(piece))
        piece = jnp.concatenate(
            [
                rows_of(up_weight, layer, w8 * PIECE, PIECE),
                rows_of(down_weight, layer, w8 * PIECE, PIECE),
                packed_output(layer),
            ]
        )
        feed_pieces.append(gather_pieces(piece))

    x = jnp.concatenate(relocate(tokens)).astype(F32)
    e = jnp.concatenate(relocate(cotangent)).astype(F32)

    stores = []
    for layer in range(layers):
        gain, shift, bias = norm_gain[layer], norm_shift[layer], output_bias[layer]
        h1, q, kv0, kv1 = project(
            idx, x, gain[0:1], shift[0:1], mixer_biases[layer], cosine, sine, mixer_pieces[layer]
        )
        far = (between_chips(kv0, (0, 1)), between_chips(kv1, (1,)))
        near = (within_chip(kv0, 1), within_chip(kv1, 1))
        far_near = (within_chip(far[0], 1), within_chip(far[1], 1))
        keys = (kv0, kv1, *near, *far, *far_near)
        o, lse = attend(idx, q, keys)
        x2, x1, h2, g, gp = feed(
            idx, x, o, gain[1:2], shift[1:2], bias[0:1], bias[1:2], up_biases[layer], feed_pieces[layer]
        )
        stores.append((x, h1, q, keys, o, lse, x1, h2, g, gp))
        x = x2
    block_out = jnp.concatenate(relocate(x.astype(BF)))

    mixer_out, feed_out = None, None
    smalls = [None] * layers
    for layer in reversed(range(layers)):
        x, h1, q, keys, o, lse, x1, h2, g, gp = stores[layer]
        gain = norm_gain[layer]
        dm, dz, e1, da, do, small_feed = feed_back(idx, e, x1, gp, gain[1:2], feed_pieces[layer])
        dq, dn, dc0, dc1, dr0, dr1 = attend_back(idx, q, do, o, lse, keys)
        tc = (within_chip(dc0, 0), within_chip(dc1, 0))
        tr = (within_chip(dr0, 0), within_chip(dr1, 0))
        tr = (between_chips(added(dr0, tr[0]), (0, 1)), between_chips(added(dr1, tr[1]), (0,)))
        feed_grad = reduce_pieces(*feed_grads(idx, g, dm, h2, dz, o, da))
        dpz, e, small_mixer = project_back(
            idx, dq, dn, (dc0, dc1), tc, tr, cosine, sine, x, e1, gain[0:1], mixer_pieces[layer]
        )
        mixer_grad = reduce_pieces(*project_grads(idx, h1, dpz))
        feed_out = finish_feed(idx, layer, layers, feed_grad, feed_out)
        mixer_out = finish_mixer(idx, layer, layers, mixer_grad, mixer_out)
        smalls[layer] = reduce_small(jnp.concatenate([small_feed, small_mixer]))
    tokens_grad = jnp.concatenate(relocate(e.astype(BF)))

    small = jnp.stack(smalls)
    up_bias_grad = lax.dynamic_index_in_dim(small[:, 0:4], z, 1, keepdims=False)
    mixer_bias_grad = lax.dynamic_index_in_dim(small[:, 8:12, :PARTS], z, 1, keepdims=False)
    return (
        block_out,
        tokens_grad,
        jnp.stack([small[:, 12], small[:, 6]], axis=1),
        jnp.stack([small[:, 13], small[:, 7]], axis=1),
        mixer_out.reshape(layers, D, 3, HEADS_COLS),
        mixer_bias_grad.reshape(layers, 3, HEADS_COLS),
        feed_out[2],
        jnp.stack([small[:, 5], small[:, 4]], axis=1),
        feed_out[0],
        up_bias_grad,
        feed_out[1],
    )


def solution(mesh):
    rows = P(("wide", "narrow"), None)
    quarters = (
        P(None, None, None, "narrow"),
        P(None, None, "narrow"),
        P(None, "narrow", None),
        P(),
        P(None, None, "narrow"),
        P(None, "narrow"),
        P(None, "narrow", None),
    )
    return jax.shard_map(
        per_device,
        mesh=mesh,
        in_specs=(rows, P("wide"), P(), P()) + quarters + (rows,),
        out_specs=(rows, rows, P(), P()) + quarters,
        check_vma=False,
    )
```

time: 2280 us -> 905 us (0.40)
  waiting for transfers between devices: 1180 us -> 310 us
  matrix products: 538 us -> 0 us
  Pallas kernels: 0 us -> 272 us
  other arithmetic: 280 us -> 36.8 us
  starting transfers between devices: 0.87 us -> 230 us
  local copies, waits for them, and re-layouts: 137 us -> 45.1 us
  blocking collectives: 64.4 us -> 0 us
  loops' own time: 50.3 us -> 0 us
    all_gather x10 -> x0, waiting for transfers between devices: 616 us -> none  [the longest x6 376 us: gather_normed(): return lax.all_gather(normed, 'narrow', axis=0, tiled=True)]
    dot_general x90 -> x0, matrix products: 470 us -> none  [the longest x16 110 us: one_block(): jnp.einsum('hqk,khd->qhd', chances, values, preferred_element_type=jnp.fl...]
    reduce_scatter x10 -> x0, waiting for transfers between devices: 411 us -> none  [the longest x6 234 us: branch_sum(): lax.psum_scatter(jnp.dot(full_rows, weight, preferred_element_type=jnp.fl...]
    ppermute x0 -> x174, waiting for transfers between devices: none -> 310 us  [the longest x111 206 us: flip_wide(): lax.ppermute(x, 'wide', [(i, i ^ bit) for i in range(lax.axis_size('wide'...]
    pallas_call x0 -> x20, Pallas kernels: none -> 272 us  [kernel_call(): pl.pallas_call(body, in_specs=in_specs, out_specs=out_specs, out_shape=ou...]
    ppermute x0 -> x174, starting transfers between devices: none -> 230 us  [the longest x111 103 us: flip_wide(): lax.ppermute(x, 'wide', [(i, i ^ bit) for i in range(lax.axis_size('wide'...]
    psum x1 -> x0, waiting for transfers between devices: 150 us -> none  [per_device(): lax.psum((stacked[0], stacked[1], stacked[2], stacked[3], stacked[4], sta...]
    select_n x72 -> x1, other arithmetic: 95.3 us -> 0.01 us  [per_device(): bases = jnp.where(low == 0, jnp.array([0, 768]), jnp.array([512, 256]))]
  transfers between devices with their start and end apart: 21 -> 174, of which waited for: 18 -> 43; matrix products, arithmetic and copies ran while one was open for 12% -> 8% of each run, Pallas kernels for 0% -> 15%
where the time goes in v1:
time: 905 us; the launch traced here: 898 us
  waiting for transfers between devices  310 us (34%)
  Pallas kernels  272 us (30%)
  starting transfers between devices  230 us (25%)
  local copies, waits for them, and re-layouts  45.1 us (5%)
  other arithmetic  36.8 us (4%)
    pallas_call x20, Pallas kernels, kernel_call(): pl.pallas_call(body, in_specs=in_specs, out_specs=out_specs, out_shape=ou...  272 us
    ppermute x111, waiting for transfers between devices, flip_wide(): lax.ppermute(x, 'wide', [(i, i ^ bit) for i in range(lax.axis_size('wide'...  206 us
    ppermute x111, starting transfers between devices, flip_wide(): lax.ppermute(x, 'wide', [(i, i ^ bit) for i in range(lax.axis_size('wide'...  103 us
    ppermute x27, waiting for transfers between devices, shift_narrow(): lax.ppermute(x, 'narrow', [(i, (i + k) % QUARTERS) for i in range(QUARTER...  92.2 us
    ppermute x16, starting transfers between devices, within_chip(): return lax.ppermute(x, 'wide', pairs)  43.8 us
    ppermute x27, starting transfers between devices, shift_narrow(): lax.ppermute(x, 'narrow', [(i, (i + k) % QUARTERS) for i in range(QUARTER...  40.6 us
    ppermute x4, starting transfers between devices, relocate(): lax.ppermute(rows[HALF:], BOTH, second)  23.2 us
    convert_element_type x28, other arithmetic, added(): return functools.reduce(jnp.add, [t.astype(F32) for t in terms]).astype(BF)  20.2 us
  transfers between devices with their start and end apart: 174, of which 43 were waited for; matrix products, arithmetic and copies ran while one was open for 8% of the time, Pallas kernels for 15%

profile of v1, /device:TPU:0, one launch (start us, length us, event | category | flops | bytes accessed | tf_op | source)
XLA Modules:
  0.0 898.0 jit_solution(12192927780111662543)
XLA Ops:
  79.9 18.9 %collective-permute-done.33 = bf16[224,768]{1,0:T(8,128)(2,1)S(1)} collective-permute-done((bf16[224,768]{1,0:T(8,128)(2,1)}, bf16[224,768]{1,0:T(8,128)(2,1)S(1)}, u32[]{:S(2)}, u32[]{:S(2)}) %collective-permute-start.33) | collective-permute-done | bytes 344096 | tf_op jit(solution)/shard_map/ppermute | solution.py:831
  101.2 20.5 %collective-permute-start.89 = (bf16[256,768]{1,0:T(8,128)(2,1)}, bf16[256,768]{1,0:T(8,128)(2,1)S(1)}, u32[]{:S(2)}, u32[]{:S(2)}) collective-permute-start(bf16[256,768]{1,0:T(8,128)(2,1)} %get-tuple-element.200), channel_id=1, source_target_pairs={{0,1},{1,0},{2,5},{3,4},{4,3},{5,2},{6,7},{7,6},{8,9},{9,8},{10,13... | collective-permute-start | bytes 1179656 | tf_op jit(solution)/shard_map/ppermute | solution.py:898
  204.2 12.8 %collective-permute-start.39 = (bf16[2,224,768]{2,1,0:T(8,128)(2,1)}, bf16[2,224,768]{2,1,0:T(8,128)(2,1)S(1)}, u32[]{:S(2)}, u32[]{:S(2)}) collective-permute-start(bf16[2,224,768]{2,1,0:T(8,128)(2,1)} %collective-permute-done.30.rest_1_), channel_id=1, source_target_pairs={{0,4},{4,0},{8,12},{12,8},{16,20},{20,16},{24,28},{28,24},{1,5},{5... | collective-permute-start | bytes 2064392 | tf_op jit(solution)/shard_map/ppermute | solution.py:827
  225.6 21.3 %attend.2 = (bf16[512,768]{1,0:T(8,128)(2,1)}, f32[12,1,512]{2,1,0:T(1,128)}) custom-call(s32[8]{0:T(128)} %stack.122.idx, bf16[512,768]{1,0:T(8,128)(2,1)} %get-tuple-element.77.q, bf16[256,1536]{1,0:T(8,128)(2,1)} %get-tuple-element.78.kv0, bf16[256,1536]{1,0:T(8,128)(2,1)} %get-tuple-element.79.kv1, bf16[256,1536]{1,0:T(8,128)(2,1)} %copy-done.97, ...), custom_call_target="tpu_custom_call" | custom-call | flops 12000000000 | bytes 6000000 | tf_op jit(solution)/shard_map/attend/pallas_call | solution.py:137
  249.0 20.1 %feed.2 = (f32[512,768]{1,0:T(8,128)}, f32[512,768]{1,0:T(8,128)}, bf16[512,768]{1,0:T(8,128)(2,1)}, bf16[4,512,768]{2,1,0:T(8,128)(2,1)}, bf16[4,512,768]{2,1,0:T(8,128)(2,1)}) custom-call(s32[8]{0:T(128)} %stack.122.idx, f32[512,768]{1,0:T(8,128)} %maximum_convert_fusion.x, bf16[512,768]{1,0:T(8,128)(2,1)} %get-tuple-element.80.o, ...), custom_call_target="tpu_custom_call" | custom-call | flops 5435817984 | bytes 25000000 | tf_op jit(solution)/shard_map/feed/pallas_call | solution.py:137
  284.6 14.3 %collective-permute-done.72.rest_3_ = bf16[2,224,768]{2,1,0:T(8,128)(2,1)} collective-permute-done((bf16[2,224,768]{2,1,0:T(8,128)(2,1)}, bf16[2,224,768]{2,1,0:T(8,128)(2,1)}, u32[]{:S(2)}, u32[]{:S(2)}) %collective-permute-start.72) | collective-permute-done | bytes 688160 | tf_op jit(solution)/shard_map/ppermute | solution.py:827
  308.9 20.9 %attend.3 = (bf16[512,768]{1,0:T(8,128)(2,1)}, f32[12,1,512]{2,1,0:T(1,128)}) custom-call(s32[8]{0:T(128)} %stack.122.idx, bf16[512,768]{1,0:T(8,128)(2,1)} %get-tuple-element.82.q, bf16[256,1536]{1,0:T(8,128)(2,1)} %get-tuple-element.83.kv0, bf16[256,1536]{1,0:T(8,128)(2,1)} %get-tuple-element.84.kv1, bf16[256,1536]{1,0:T(8,128)(2,1)} %copy-done.105, ...), custom_call_target="tpu_custom_call" | custom-call | flops 12000000000 | bytes 6000000 | tf_op jit(solution)/shard_map/attend/pallas_call | solution.py:137
  331.0 20.1 %feed.3 = (f32[512,768]{1,0:T(8,128)}, f32[512,768]{1,0:T(8,128)}, bf16[512,768]{1,0:T(8,128)(2,1)}, bf16[4,512,768]{2,1,0:T(8,128)(2,1)}, bf16[4,512,768]{2,1,0:T(8,128)(2,1)}) custom-call(s32[8]{0:T(128)} %stack.122.idx, f32[512,768]{1,0:T(8,128)} %get-tuple-element.81.x, bf16[512,768]{1,0:T(8,128)(2,1)} %get-tuple-element.85.o, ...), custom_call_target="tpu_custom_call" | custom-call | flops 5435817984 | bytes 25000000 | tf_op jit(solution)/shard_map/feed/pallas_call | solution.py:137
  351.1 18.4 %feed_back.2 = (bf16[512,768]{1,0:T(8,128)(2,1)}, bf16[4,512,768]{2,1,0:T(8,128)(2,1)}, f32[512,768]{1,0:T(8,128)}, bf16[512,768]{1,0:T(8,128)(2,1)}, bf16[512,768]{1,0:T(8,128)(2,1)}, /*index=5*/f32[8,768]{1,0:T(8,128)}) custom-call(s32[8]{0:T(128)} %stack.122.idx, f32[512,768]{1,0:T(8,128)} %maximum_convert_fusion.1.e, f32[512,768]{1,0:T(8,128)} %get-tuple-element.87.x1, ...), custom_call_target="tpu_custom_call" | custom-call | flops 5435817984 | bytes 25000000 | tf_op jit(solution)/shard_map/feed_back/pallas_call | solution.py:137
  369.6 28.9 %attend_back.2 = (f32[512,768]{1,0:T(8,128)}, bf16[512,1536]{1,0:T(8,128)(2,1)}, bf16[256,1536]{1,0:T(8,128)(2,1)}, bf16[256,1536]{1,0:T(8,128)(2,1)}, bf16[256,...) custom-call(s32[8]{0:T(128)} %stack.122.idx, bf16[512,768]{1,0:T(8,128)(2,1)} %get-tuple-element.82.q, ...), custom_call_target="tpu_custom_call" | custom-call | flops 30000001024 | bytes 12000000 | tf_op jit(solution)/shard_map/attend_back/pallas_call | solution.py:137
  410.0 14.3 %project_back.2 = (bf16[4,512,576]{2,1,0:T(8,128)(2,1)}, f32[512,768]{1,0:T(8,128)}, f32[8,768]{1,0:T(8,128)}) custom-call(s32[8]{0:T(128)} %stack.122.idx, f32[512,768]{1,0:T(8,128)} %get-tuple-element.91.dq, bf16[512,1536]{1,0:T(8,128)(2,1)} %get-tuple-element.92.dn, bf16[256,1536]{1,0:T(8,128)(2,1)} %get-tuple-element.93.dc0, ...), custom_call_target="tpu_custom_call" | custom-call | flops 1811939328 | bytes 12000000 | tf_op jit(solution)/shard_map/project_back/pallas_call | solution.py:137
  424.4 18.5 %feed_back.3 = (bf16[512,768]{1,0:T(8,128)(2,1)}, bf16[4,512,768]{2,1,0:T(8,128)(2,1)}, f32[512,768]{1,0:T(8,128)}, bf16[512,768]{1,0:T(8,128)(2,1)}, bf16[512,768]{1,0:T(8,128)(2,1)}, /*index=5*/f32[8,768]{1,0:T(8,128)}) custom-call(s32[8]{0:T(128)} %stack.122.idx, f32[512,768]{1,0:T(8,128)} %get-tuple-element.98.e, f32[512,768]{1,0:T(8,128)} %get-tuple-element.99.x1, ...), custom_call_target="tpu_custom_call" | custom-call | flops 5435817984 | bytes 25000000 | tf_op jit(solution)/shard_map/feed_back/pallas_call | solution.py:137
  442.8 28.9 %attend_back.3 = (f32[512,768]{1,0:T(8,128)}, bf16[512,1536]{1,0:T(8,128)(2,1)}, bf16[256,1536]{1,0:T(8,128)(2,1)}, bf16[256,1536]{1,0:T(8,128)(2,1)}, bf16[256,...) custom-call(s32[8]{0:T(128)} %stack.122.idx, bf16[512,768]{1,0:T(8,128)(2,1)} %get-tuple-element.77.q, ...), custom_call_target="tpu_custom_call" | custom-call | flops 30000001024 | bytes 12000000 | tf_op jit(solution)/shard_map/attend_back/pallas_call | solution.py:137
  471.7 19.7 %collective-permute-start.98 = (bf16[256,1536]{1,0:T(8,128)(2,1)}, bf16[256,1536]{1,0:T(8,128)(2,1)S(1)}, u32[]{:S(2)}, u32[]{:S(2)}) collective-permute-start(bf16[256,1536]{1,0:T(8,128)(2,1)} %get-tuple-element.107), channel_id=1, source_target_pairs={{0,4},{8,12},{16,20},{24,28},{1,5},{9,13},{17,21},{25,29},{2,6},{1... | collective-permute-start | bytes 2359304 | tf_op jit(solution)/shard_map/ppermute | solution.py:908
  491.5 11.6 %feed_grads.3 = (bf16[4,4,224,768]{3,2,1,0:T(8,128)(2,1)}, bf16[4,4,224,768]{3,2,1,0:T(8,128)(2,1)}) custom-call(s32[8]{0:T(128)} %stack.122.idx, bf16[4,512,768]{2,1,0:T(8,128)(2,1)} %get-tuple-element.130.g, bf16[512,768]{1,0:T(8,128)(2,1)} %get-tuple-element.131.dm, bf16[512,768]{1,0:T(8,128)(2,1)} %get-tuple-element.132.h2, ...), custom_call_target="tpu_custom_call" | custom-call | flops 5435817984 | bytes 25000000 | tf_op jit(solution)/shard_map/feed_grads/pallas_call | solution.py:137
  522.7 11.5 %feed_grads.2 = (bf16[4,4,224,768]{3,2,1,0:T(8,128)(2,1)}, bf16[4,4,224,768]{3,2,1,0:T(8,128)(2,1)}) custom-call(s32[8]{0:T(128)} %stack.122.idx, bf16[4,512,768]{2,1,0:T(8,128)(2,1)} %get-tuple-element.123.g, bf16[512,768]{1,0:T(8,128)(2,1)} %get-tuple-element.124.dm, bf16[512,768]{1,0:T(8,128)(2,1)} %get-tuple-element.125.h2, ...), custom_call_target="tpu_custom_call" | custom-call | flops 5435817984 | bytes 25000000 | tf_op jit(solution)/shard_map/feed_grads/pallas_call | solution.py:137
  541.2 15.0 %project_back.3 = (bf16[4,512,576]{2,1,0:T(8,128)(2,1)}, f32[512,768]{1,0:T(8,128)}, f32[8,768]{1,0:T(8,128)}) custom-call(s32[8]{0:T(128)} %stack.122.idx, f32[512,768]{1,0:T(8,128)} %get-tuple-element.103.dq, bf16[512,1536]{1,0:T(8,128)(2,1)} %get-tuple-element.104.dn, bf16[256,1536]{1,0:T(8,128)(2,1)} %get-tuple-element.105.dc0, ...), custom_call_target="tpu_custom_call" | custom-call | flops 1811939328 | bytes 12000000 | tf_op jit(solution)/shard_map/project_back/pallas_call | solution.py:137
  589.0 16.2 %collective-permute-done.131 = bf16[2,96,576]{2,1,0:T(8,128)(2,1)S(1)} collective-permute-done((bf16[2,96,576]{2,1,0:T(8,128)(2,1)S(1)}, bf16[2,96,576]{2,1,0:T(8,128)(2,1)S(1)}, u32[]{:S(2)}, u32[]{:S(2)}) %collective-permute-start.131) | collective-permute-done | bytes 221216 | tf_op jit(solution)/shard_map/ppermute | solution.py:827
  628.8 15.1 %collective-permute-done.116 = bf16[2,96,576]{2,1,0:T(8,128)(2,1)S(1)} collective-permute-done((bf16[2,96,576]{2,1,0:T(8,128)(2,1)S(1)}, bf16[2,96,576]{2,1,0:T(8,128)(2,1)S(1)}, u32[]{:S(2)}, u32[]{:S(2)}) %collective-permute-start.116) | collective-permute-done | bytes 221216 | tf_op jit(solution)/shard_map/ppermute | solution.py:827
  662.7 26.3 %collective-permute-done.119 = bf16[2,96,576]{2,1,0:T(8,128)(2,1)S(1)} collective-permute-done((bf16[2,96,576]{2,1,0:T(8,128)(2,1)S(1)}, bf16[2,96,576]{2,1,0:T(8,128)(2,1)S(1)}, u32[]{:S(2)}, u32[]{:S(2)}) %collective-permute-start.119) | collective-permute-done | bytes 221216 | tf_op jit(solution)/shard_map/ppermute | solution.py:827
  696.2 11.6 %collective-permute-done.161 = bf16[2,224,768]{2,1,0:T(8,128)(2,1)S(1)} collective-permute-done((bf16[2,224,768]{2,1,0:T(8,128)(2,1)S(1)}, bf16[2,224,768]{2,1,0:T(8,128)(2,1)S(1)}, u32[]{:S(2)}, u32[]{:S(2)}) %collective-permute-start.161) | collective-permute-done | bytes 688160 | tf_op jit(solution)/shard_map/ppermute | solution.py:827
  720.3 17.0 %collective-permute-done.148 = bf16[2,2,224,768]{3,2,1,0:T(8,128)(2,1)S(1)} collective-permute-done((bf16[2,2,224,768]{3,2,1,0:T(8,128)(2,1)S(1)}, bf16[2,2,224,768]{3,2,1,0:T(8,128)(2,1)S(1)}, u32[]{:S(2)}, u32[]{:S(2)}) %collective-permute-start.148) | collective-permute-done | bytes 1376288 | tf_op jit(solution)/shard_map/ppermute | solution.py:827
  786.3 15.7 %collective-permute-done.120 = bf16[96,576]{1,0:T(8,128)(2,1)S(1)} collective-permute-done((bf16[96,576]{1,0:T(8,128)(2,1)S(1)}, bf16[96,576]{1,0:T(8,128)(2,1)S(1)}, u32[]{:S(2)}, u32[]{:S(2)}) %collective-permute-start.120) | collective-permute-done | bytes 110624 | tf_op jit(solution)/shard_map/ppermute | solution.py:831
  803.6 20.6 %collective-permute-done.165 = bf16[224,768]{1,0:T(8,128)(2,1)S(1)} collective-permute-done((bf16[224,768]{1,0:T(8,128)(2,1)S(1)}, bf16[224,768]{1,0:T(8,128)(2,1)S(1)}, u32[]{:S(2)}, u32[]{:S(2)}) %collective-permute-start.165) | collective-permute-done | bytes 344096 | tf_op jit(solution)/shard_map/ppermute | solution.py:831
  (734 shorter events, 455.0 us)
Async XLA Ops:
  62.4 36.4 %collective-permute-start.33 = (bf16[224,768]{1,0:T(8,128)(2,1)}, bf16[224,768]{1,0:T(8,128)(2,1)S(1)}, u32[]{:S(2)}, u32[]{:S(2)}) collective-permute-start(bf16[224,768]{1,0:T(8,128)(2,1)} %get-tuple-element.214), channel_id=1, source_target_pairs={{0,2},{1,3},{2,0},{3,1},{4,6},{5,7},{6,4},{7,5},{8,10},{9,11},{10,... | collective-permute-start | bytes 1032200 | tf_op jit(solution)/shard_map/ppermute | solution.py:831
  62.4 38.7 %collective-permute-start.69 = (bf16[224,768]{1,0:T(8,128)(2,1)}, bf16[224,768]{1,0:T(8,128)(2,1)S(1)}, u32[]{:S(2)}, u32[]{:S(2)}) collective-permute-start(bf16[224,768]{1,0:T(8,128)(2,1)} %get-tuple-element.212), channel_id=1, source_target_pairs={{0,1},{1,2},{2,3},{3,0},{4,5},{5,6},{6,7},{7,4},{8,9},{9,10},{10,1... | collective-permute-start | bytes 1032200 | tf_op jit(solution)/shard_map/ppermute | solution.py:831
  64.5 57.2 %collective-permute-start.74 = (bf16[224,768]{1,0:T(8,128)(2,1)}, bf16[224,768]{1,0:T(8,128)(2,1)S(1)}, u32[]{:S(2)}, u32[]{:S(2)}) collective-permute-start(bf16[224,768]{1,0:T(8,128)(2,1)} %get-tuple-element.212), channel_id=1, source_target_pairs={{0,3},{1,0},{2,1},{3,2},{4,7},{5,4},{6,5},{7,6},{8,11},{9,8},{10,9... | collective-permute-start | bytes 1032200 | tf_op jit(solution)/shard_map/ppermute | solution.py:831
  69.3 66.5 %collective-permute-start.73 = (bf16[224,768]{1,0:T(8,128)(2,1)}, bf16[224,768]{1,0:T(8,128)(2,1)S(1)}, u32[]{:S(2)}, u32[]{:S(2)}) collective-permute-start(bf16[224,768]{1,0:T(8,128)(2,1)} %get-tuple-element.212), channel_id=1, source_target_pairs={{0,2},{1,3},{2,0},{3,1},{4,6},{5,7},{6,4},{7,5},{8,10},{9,11},{10,... | collective-permute-start | bytes 1032200 | tf_op jit(solution)/shard_map/ppermute | solution.py:831
  77.3 60.2 %collective-permute-start.2 = (bf16[256,768]{1,0:T(8,128)(2,1)}, bf16[256,768]{1,0:T(8,128)(2,1)S(1)}, u32[]{:S(2)}, u32[]{:S(2)}) collective-permute-start(bf16[256,768]{1,0:T(8,128)(2,1)} %get-tuple-element.204), channel_id=1, source_target_pairs={{0,1},{1,0},{2,5},{3,4},{4,3},{5,2},{6,7},{7,6},{8,9},{9,8},{10,13... | collective-permute-start | bytes 1179656 | tf_op jit(solution)/shard_map/ppermute | solution.py:898
  99.5 38.1 %collective-permute-start.1 = (bf16[256,768]{1,0:T(8,128)(2,1)}, bf16[256,768]{1,0:T(8,128)(2,1)S(1)}, u32[]{:S(2)}, u32[]{:S(2)}) collective-permute-start(bf16[256,768]{1,0:T(8,128)(2,1)} %get-tuple-element.203), channel_id=1, source_target_pairs={{0,0},{1,1},{2,4},{3,5},{4,2},{5,3},{6,6},{7,7},{8,8},{9,9},{10,12... | collective-permute-start | bytes 1179656 | tf_op jit(solution)/shard_map/ppermute | solution.py:898
  101.2 37.9 %collective-permute-start.89 = (bf16[256,768]{1,0:T(8,128)(2,1)}, bf16[256,768]{1,0:T(8,128)(2,1)S(1)}, u32[]{:S(2)}, u32[]{:S(2)}) collective-permute-start(bf16[256,768]{1,0:T(8,128)(2,1)} %get-tuple-element.200), channel_id=1, source_target_pairs={{0,1},{1,0},{2,5},{3,4},{4,3},{5,2},{6,7},{7,6},{8,9},{9,8},{10,13... | collective-permute-start | bytes 1179656 | tf_op jit(solution)/shard_map/ppermute | solution.py:898
  221.5 55.8 %collective-permute-start.70 = (bf16[2,224,768]{2,1,0:T(8,128)(2,1)S(1)}, bf16[2,224,768]{2,1,0:T(8,128)(2,1)}, u32[]{:S(2)}, u32[]{:S(2)}) collective-permute-start(bf16[2,224,768]{2,1,0:T(8,128)(2,1)S(1)} %pad_maximum_fusion.4.rest_0_), channel_id=1, source_target_pairs={{0,8},{4,12},{8,0},{12,4},{16,24},{20,28},{24,16},{28,20},{1,9},{5... | collective-permute-start | bytes 2064392 | tf_op jit(solution)/shard_map/ppermute | solution.py:827
  222.2 55.8 %collective-permute-start.71 = (bf16[2,224,768]{2,1,0:T(8,128)(2,1)S(1)}, bf16[2,224,768]{2,1,0:T(8,128)(2,1)}, u32[]{:S(2)}, u32[]{:S(2)}) collective-permute-start(bf16[2,224,768]{2,1,0:T(8,128)(2,1)S(1)} %pad_maximum_fusion.4.rest_0_), channel_id=1, source_target_pairs={{0,16},{4,20},{8,24},{12,28},{16,0},{20,4},{24,8},{28,12},{1,17},{... | collective-permute-start | bytes 2064392 | tf_op jit(solution)/shard_map/ppermute | solution.py:827
  247.5 33.6 %collective-permute-start.76 = (bf16[2,224,768]{2,1,0:T(8,128)(2,1)S(1)}, bf16[2,224,768]{2,1,0:T(8,128)(2,1)S(1)}, u32[]{:S(2)}, u32[]{:S(2)}) collective-permute-start(bf16[2,224,768]{2,1,0:T(8,128)(2,1)S(1)} %pad_maximum_fusion.5.rest_4_), channel_id=1, source_target_pairs={{0,16},{4,20},{8,24},{12,28},{16,0},{20,4},{24,8},{28,12},{1,17},{... | collective-permute-start | bytes 2064392 | tf_op jit(solution)/shard_map/ppermute | solution.py:827
  471.7 45.0 %collective-permute-start.98 = (bf16[256,1536]{1,0:T(8,128)(2,1)}, bf16[256,1536]{1,0:T(8,128)(2,1)S(1)}, u32[]{:S(2)}, u32[]{:S(2)}) collective-permute-start(bf16[256,1536]{1,0:T(8,128)(2,1)} %get-tuple-element.107), channel_id=1, source_target_pairs={{0,4},{8,12},{16,20},{24,28},{1,5},{9,13},{17,21},{25,29},{2,6},{1... | collective-permute-start | bytes 2359304 | tf_op jit(solution)/shard_map/ppermute | solution.py:908
  503.1 111.5 %collective-permute-start.159 = (bf16[4,4,224,768]{3,2,1,0:T(8,128)(2,1)}, bf16[4,4,224,768]{3,2,1,0:T(8,128)(2,1)}, u32[]{:S(2)}, u32[]{:S(2)}) collective-permute-start(bf16[4,4,224,768]{3,2,1,0:T(8,128)(2,1)} %get-tuple-element.136), channel_id=1, source_target_pairs={{0,4},{4,0},{8,12},{12,8},{16,20},{20,16},{24,28},{28,24},{1,5},{5... | collective-permute-start | bytes 16515080 | tf_op jit(solution)/shard_map/ppermute | solution.py:827
  516.7 42.6 %collective-permute-start.129 = (bf16[4,4,96,576]{3,2,1,0:T(8,128)(2,1)}, bf16[4,4,96,576]{3,2,1,0:T(8,128)(2,1)S(1)}, u32[]{:S(2)}, u32[]{:S(2)}) collective-permute-start(bf16[4,4,96,576]{3,2,1,0:T(8,128)(2,1)} %get-tuple-element.122), channel_id=1, source_target_pairs={{0,4},{4,0},{8,12},{12,8},{16,20},{20,16},{24,28},{28,24},{1,5},{5... | collective-permute-start | bytes 5308424 | tf_op jit(solution)/shard_map/ppermute | solution.py:827
  534.3 110.6 %collective-permute-start.144 = (bf16[4,4,224,768]{3,2,1,0:T(8,128)(2,1)}, bf16[4,4,224,768]{3,2,1,0:T(8,128)(2,1)}, u32[]{:S(2)}, u32[]{:S(2)}) collective-permute-start(bf16[4,4,224,768]{3,2,1,0:T(8,128)(2,1)} %get-tuple-element.129), channel_id=1, source_target_pairs={{0,4},{4,0},{8,12},{12,8},{16,20},{20,16},{24,28},{28,24},{1,5},{5... | collective-permute-start | bytes 16515080 | tf_op jit(solution)/shard_map/ppermute | solution.py:827
  624.6 33.1 %collective-permute-start.160 = (bf16[2,2,224,768]{3,2,1,0:T(8,128)(2,1)S(1)}, bf16[2,2,224,768]{3,2,1,0:T(8,128)(2,1)S(1)}, u32[]{:S(2)}, u32[]{:S(2)}) collective-permute-start(bf16[2,2,224,768]{3,2,1,0:T(8,128)(2,1)S(1)} %add_convert_fusion.4), channel_id=1, source_target_pairs={{0,8},{4,12},{8,0},{12,4},{16,24},{20,28},{24,16},{28,20},{1,9},{5... | collective-permute-start | bytes 4128776 | tf_op jit(solution)/shard_map/ppermute | solution.py:827
  626.5 114.4 %collective-permute-start.87 = (bf16[256,768]{1,0:T(8,128)(2,1)S(1)}, bf16[256,768]{1,0:T(8,128)(2,1)S(1)}, u32[]{:S(2)}, u32[]{:S(2)}) collective-permute-start(bf16[256,768]{1,0:T(8,128)(2,1)S(1)} %get-tuple-element.202), channel_id=1, source_target_pairs={{0,1},{1,0},{2,5},{3,4},{4,3},{5,2},{6,7},{7,6},{8,9},{9,8},{10,13... | collective-permute-start | bytes 1179656 | tf_op jit(solution)/shard_map/ppermute | solution.py:898
  643.9 97.0 %collective-permute-start.86 = (bf16[256,768]{1,0:T(8,128)(2,1)S(1)}, bf16[256,768]{1,0:T(8,128)(2,1)S(1)}, u32[]{:S(2)}, u32[]{:S(2)}) collective-permute-start(bf16[256,768]{1,0:T(8,128)(2,1)S(1)} %get-tuple-element.201), channel_id=1, source_target_pairs={{0,0},{1,1},{2,4},{3,5},{4,2},{5,3},{6,6},{7,7},{8,8},{9,9},{10,12... | collective-permute-start | bytes 1179656 | tf_op jit(solution)/shard_map/ppermute | solution.py:898
  646.6 42.7 %collective-permute-start.145 = (bf16[2,2,224,768]{3,2,1,0:T(8,128)(2,1)S(1)}, bf16[2,2,224,768]{3,2,1,0:T(8,128)(2,1)S(1)}, u32[]{:S(2)}, u32[]{:S(2)}) collective-permute-start(bf16[2,2,224,768]{3,2,1,0:T(8,128)(2,1)S(1)} %add_convert_fusion.10), channel_id=1, source_target_pairs={{0,8},{4,12},{8,0},{12,4},{16,24},{20,28},{24,16},{28,20},{1,9},{5... | collective-permute-start | bytes 4128776 | tf_op jit(solution)/shard_map/ppermute | solution.py:827
  660.4 33.1 %collective-permute-start.163 = (bf16[2,2,224,768]{3,2,1,0:T(8,128)(2,1)S(1)}, bf16[2,2,224,768]{3,2,1,0:T(8,128)(2,1)S(1)}, u32[]{:S(2)}, u32[]{:S(2)}) collective-permute-start(bf16[2,2,224,768]{3,2,1,0:T(8,128)(2,1)S(1)} %get-tuple-element.184), channel_id=1, source_target_pairs={{0,16},{4,20},{8,24},{12,28},{16,0},{20,4},{24,8},{28,12},{1,17},{... | collective-permute-start | bytes 4128776 | tf_op jit(solution)/shard_map/ppermute | solution.py:827
  689.0 61.2 %collective-permute-start.113 = (f32[16,768]{1,0:T(8,128)S(1)}, f32[16,768]{1,0:T(8,128)S(1)}, u32[]{:S(2)}, u32[]{:S(2)}) collective-permute-start(f32[16,768]{1,0:T(8,128)S(1)} %add.248), channel_id=1, source_target_pairs={{0,2},{1,3},{2,0},{3,1},{4,6},{5,7},{6,4},{7,5},{8,10},{9,11},{10,... | collective-permute-start | bytes 147464 | tf_op jit(solution)/shard_map/ppermute | solution.py:878
  693.5 43.7 %collective-permute-start.148 = (bf16[2,2,224,768]{3,2,1,0:T(8,128)(2,1)S(1)}, bf16[2,2,224,768]{3,2,1,0:T(8,128)(2,1)S(1)}, u32[]{:S(2)}, u32[]{:S(2)}) collective-permute-start(bf16[2,2,224,768]{3,2,1,0:T(8,128)(2,1)S(1)} %get-tuple-element.186), channel_id=1, source_target_pairs={{0,16},{4,20},{8,24},{12,28},{16,0},{20,4},{24,8},{28,12},{1,17},{... | collective-permute-start | bytes 4128776 | tf_op jit(solution)/shard_map/ppermute | solution.py:827
  774.8 49.3 %collective-permute-start.165 = (bf16[224,768]{1,0:T(8,128)(2,1)S(1)}, bf16[224,768]{1,0:T(8,128)(2,1)S(1)}, u32[]{:S(2)}, u32[]{:S(2)}) collective-permute-start(bf16[224,768]{1,0:T(8,128)(2,1)S(1)} %get-tuple-element.205), channel_id=1, source_target_pairs={{0,2},{1,3},{2,0},{3,1},{4,6},{5,7},{6,4},{7,5},{8,10},{9,11},{10,... | collective-permute-start | bytes 1032200 | tf_op jit(solution)/shard_map/ppermute | solution.py:831
  783.7 45.3 %collective-permute-start.147 = (bf16[224,768]{1,0:T(8,128)(2,1)S(1)}, bf16[224,768]{1,0:T(8,128)(2,1)S(1)}, u32[]{:S(2)}, u32[]{:S(2)}) collective-permute-start(bf16[224,768]{1,0:T(8,128)(2,1)S(1)} %slice_bitcast_fusion.14), channel_id=1, source_target_pairs={{0,3},{1,0},{2,1},{3,2},{4,7},{5,4},{6,5},{7,6},{8,11},{9,8},{10,9... | collective-permute-start | bytes 1032200 | tf_op jit(solution)/shard_map/ppermute | solution.py:831
  802.0 36.3 %collective-permute-start.150 = (bf16[224,768]{1,0:T(8,128)(2,1)S(1)}, bf16[224,768]{1,0:T(8,128)(2,1)S(1)}, u32[]{:S(2)}, u32[]{:S(2)}) collective-permute-start(bf16[224,768]{1,0:T(8,128)(2,1)S(1)} %get-tuple-element.207), channel_id=1, source_target_pairs={{0,2},{1,3},{2,0},{3,1},{4,6},{5,7},{6,4},{7,5},{8,10},{9,11},{10,... | collective-permute-start | bytes 1032200 | tf_op jit(solution)/shard_map/ppermute | solution.py:831
  (278 other events, 4431.9 us)

commit v2 on v1

v2 whole, which is shorter than its diff:
```python
import functools
import math

import jax
import jax.numpy as jnp
from jax import lax
from jax.experimental import pallas as pl
from jax.experimental.pallas import tpu as pltpu
from jax.sharding import PartitionSpec as P

HEAD_DIM = 64
LEN = 1024
EPSILON = 1e-05
D = 768
QUARTERS = 4
HALF = 256
ROWS = 512
PIECE = 96
HEADS_COLS = 192
PARTS = 576
PACK = 224
MASKED = -1e30
BF = jnp.bfloat16
F32 = jnp.float32
NT = (((1,), (1,)), ((), ()))
TN = (((0,), (0,)), ((), ()))
VMEM_LIMIT = 56 * 1024 * 1024


def dot(a, b):
    return jnp.dot(a, b, preferred_element_type=F32)


def dot_nt(a, b):
    return lax.dot_general(a, b, NT, preferred_element_type=F32)


def dot_tn(a, b):
    return lax.dot_general(a, b, TN, preferred_element_type=F32)


def norm_parts(values):
    center = values - jnp.mean(values, axis=-1, keepdims=True)
    inverse = lax.rsqrt(jnp.mean(center * center, axis=-1, keepdims=True) + EPSILON)
    return center * inverse, inverse


def norm_backward(grad_in, unit_rows, inverse, gain):
    scaled = grad_in * gain
    return inverse * (
        scaled
        - jnp.mean(scaled, axis=-1, keepdims=True)
        - unit_rows * jnp.mean(scaled * unit_rows, axis=-1, keepdims=True)
    )


def swap_halves(u):
    lane = lax.broadcasted_iota(jnp.int32, u.shape, 1)
    return jnp.where((lane & 63) < 32, pltpu.roll(u, 96, axis=1), pltpu.roll(u, 32, axis=1))


def rot(u, cosine, sine):
    return u * cosine + swap_halves(u) * sine


def unrot(u, cosine, sine):
    return u * cosine - swap_halves(u) * sine


ORDER = (0, 2, 1, 3)


def flips(idx):
    first, second = 2 + 2 * idx[2], 4 - 2 * idx[2]
    return [0, first, second, 6, 1, 1 ^ second, 1 ^ first, 7]


def piece_copies(refs, idx, sems, place):
    copies = []
    for flip, ref in zip(flips(idx), refs):
        for at, k in enumerate(ORDER):
            for source, target in place(ref.at[at], k, idx[1] ^ k, idx[0] ^ flip):
                copies.append(pltpu.make_async_copy(source, target, sems.at[len(copies)]))
    return copies


def rows_at(start, size, unit):
    return pl.ds(pl.multiple_of(start, unit), size)


def mixer_copies(refs, idx, sems, weights):
    def place(src, k, zq, wq):
        return [(src, weights.at[zq, rows_at(wq * PIECE, PIECE, 32)])]

    return piece_copies(refs, idx, sems, place)


def up_down_copies(refs, idx, sems, ups, downs):
    def place(src, k, zq, wq):
        rows = rows_at(wq * PIECE, PIECE, 32)
        return [
            (src.at[pl.ds(0, PIECE)], ups.at[k, rows]),
            (src.at[pl.ds(PIECE, PIECE)], downs.at[k, rows]),
        ]

    return piece_copies(refs, idx, sems, place)


def packed_copies(refs, idx, sems, packed):
    def place(src, k, zq, wq):
        return [(src.at[pl.ds(2 * PIECE, 32)], packed.at[zq, wq])]

    return piece_copies(refs, idx, sems, place)


def unpack_output(packed, weights):
    for zq in range(QUARTERS):
        for chip in range(4):
            for part in range(2):
                for s in range(3):
                    row = HEADS_COLS * zq + 48 * chip + 16 * s
                    weights[row : row + 16, 384 * part : 384 * part + 384] = packed[
                        zq, 2 * chip + part, 16 * (s // 2) : 16 * (s // 2) + 16, 384 * (s % 2) : 384 * (s % 2) + 384
                    ]


def any_spec():
    return pl.BlockSpec(memory_space=pl.ANY)


def vmem_spec():
    return pl.BlockSpec(memory_space=pltpu.VMEM)


def smem_spec():
    return pl.BlockSpec(memory_space=pltpu.SMEM)


def kernel_call(body, in_specs, out_shape, out_specs, scratch, args, flops, moved, aliases=None, name=None):
    return pl.pallas_call(
        body,
        in_specs=in_specs,
        out_specs=out_specs,
        out_shape=out_shape,
        scratch_shapes=scratch,
        input_output_aliases=aliases or {},
        compiler_params=pltpu.CompilerParams(vmem_limit_bytes=VMEM_LIMIT),
        cost_estimate=pl.CostEstimate(flops=1000, bytes_accessed=1000, transcendentals=0),
        name=name,
    )(*args)


def sds(shape, dtype):
    return jax.ShapeDtypeStruct(shape, dtype)


def project_body(idx, x, gain, shift, bias, cosine, sine, *rest):
    pieces, (h1, q, kv, weights, wide, sems) = rest[:8], rest[8:]
    copies = mixer_copies(pieces, idx, sems, weights)
    for copy in copies:
        copy.start()

    def norm_rows(i, carry):
        rows = rows_at(i * 128, 128, 128)
        unit, _ = norm_parts(x[rows])
        h1[rows] = (unit * gain[...] + shift[...]).astype(BF)
        return carry

    lax.fori_loop(0, 4, norm_rows, 0)
    for copy in copies:
        copy.wait()
    for zq in range(QUARTERS):
        p = dot(h1[...], weights[zq]) + bias[idx[1] ^ zq]
        for part in range(3):
            col = D * part + HEADS_COLS * zq
            wide[:, col : col + HEADS_COLS] = p[:, HEADS_COLS * part : HEADS_COLS * (part + 1)]
    for half in range(2):
        rows = slice(HALF * half, HALF * (half + 1))
        for j in range(6):
            cols = slice(128 * j, 128 * (j + 1))
            q[rows, cols] = (rot(wide[rows, cols], cosine[rows], sine[rows]) * 0.125).astype(BF)
            kcols = slice(D + 128 * j, D + 128 * (j + 1))
            kv[rows, cols] = rot(wide[rows, kcols], cosine[rows], sine[rows]).astype(BF)
        kv[rows, D:] = wide[rows, 2 * D :].astype(BF)


def project(idx, x, gain, shift, bias, cosine, sine, pieces):
    return kernel_call(
        project_body,
        [smem_spec()] + [vmem_spec()] * 6 + [any_spec()] * 8,
        [sds((ROWS, D), BF), sds((ROWS, D), BF), sds((ROWS, 2 * D), BF)],
        [vmem_spec()] * 3,
        [
            pltpu.VMEM((QUARTERS, D, PARTS), BF),
            pltpu.VMEM((ROWS, 3 * D), F32),
            pltpu.SemaphoreType.DMA((32,)),
        ],
        (idx, x, gain, shift, bias, cosine, sine, *pieces),
        2 * ROWS * D * 3 * D,
        8e6,
        name="project",
    )


def load_near(idx, own, near, kvn, kvc, sems):
    clean = idx[2] == 1
    copy = pltpu.make_async_copy(own, kvn, sems.at[0])
    copy.start()
    a = pltpu.make_async_copy(own, kvc, sems.at[1])
    b = pltpu.make_async_copy(near, kvc, sems.at[1])
    pl.when(clean)(a.start)
    pl.when(jnp.logical_not(clean))(b.start)
    return [copy, a]


def load_far(idx, far, far_near, kvr, sem):
    clean = idx[2] == 1
    a = pltpu.make_async_copy(far, kvr, sem)
    b = pltpu.make_async_copy(far_near, kvr, sem)
    pl.when(clean)(a.start)
    pl.when(jnp.logical_not(clean))(b.start)
    return a


NEAR_TILES = {0: [(0, [(0, True)]), (1, [(1, True), (0, False)])], 1: [(1, [(1, True)]), (0, [(0, True), (1, False)])]}
FAR_TILES = {0: [(1, [0, 1])], 1: [(1, [0]), (0, [0])]}


def set_masks(idx, bias, bias_n, query_dim):
    clean, level = idx[2], idx[4]
    qi = lax.shift_right_logical(lax.broadcasted_iota(jnp.int32, (HALF, HALF), query_dim), level)
    ki = lax.shift_right_logical(lax.broadcasted_iota(jnp.int32, (HALF, HALF), 1 - query_dim), level)
    bias[...] = jnp.where(ki < qi + clean, 0.0, MASKED)
    same = jnp.where(ki == qi, 0, 1) + clean
    bias_n[...] = jnp.where(same[:128, :128] == 0, 0.0, MASKED)


def lanes(rows):
    return lax.broadcasted_iota(jnp.int32, (rows, 128), 1)


def one_head(v, side):
    low_lane = lanes(v.shape[0]) < 64
    return jnp.where(low_lane if side == 0 else jnp.logical_not(low_lane), v, jnp.zeros_like(v))


def pair_cols(hp):
    off = pl.multiple_of(hp * 128, 128)
    return pl.ds(off, 128), pl.ds(pl.multiple_of(D + off, 128), 128)


def row_max(s):
    return jnp.max(s, axis=-1, keepdims=True)


def with_ones(v):
    return jnp.concatenate([v, jnp.ones_like(v)], axis=1)


def half_rows(half):
    return slice(HALF * half, HALF * (half + 1))


def attend_near_body(idx, q, own, near, acc, tops, counts, kvn, kvc, bias, bias_n, sems):
    waits = load_near(idx, own, near, kvn, kvc, sems)
    set_masks(idx, bias, bias_n, 0)
    tops[...] = jnp.zeros_like(tops)
    counts[...] = jnp.ones_like(counts)
    for copy in waits:
        copy.wait()

    def run(tiles):
        def pair(hp, carry):
            cols, vcols = pair_cols(hp)
            lane = lanes(HALF)
            for half, sources in tiles:
                rows = half_rows(half)
                q2 = q[rows, cols]
                sides = []
                for side in range(2):
                    qm = one_head(q2, side)
                    scores = []
                    for kh, diagonal in sources:
                        s = dot_nt(qm, kvc[half_rows(kh), cols])
                        scores.append(s + bias[...] if diagonal else s)
                    blocks = [slice(HALF * half + 128 * t, HALF * half + 128 * (t + 1)) for t in range(2)]
                    parts = [slice(128 * t, 128 * (t + 1)) for t in range(2)]
                    mine = [dot_nt(qm[part], kvn[block, cols]) + bias_n[...] for part, block in zip(parts, blocks)]
                    top = jnp.concatenate([row_max(s) for s in mine], axis=0)
                    for s in scores:
                        top = jnp.maximum(top, row_max(s))
                    total = jnp.concatenate(
                        [
                            dot(jnp.exp(s - top[part]).astype(BF), with_ones(kvn[block, vcols]))
                            for s, part, block in zip(mine, parts, blocks)
                        ],
                        axis=0,
                    )
                    for s, (kh, diagonal) in zip(scores, sources):
                        total = total + dot(jnp.exp(s - top).astype(BF), with_ones(kvc[half_rows(kh), vcols]))
                    sides.append((total[:, :128], top, total[:, 128:]))
                acc[rows, cols] = jnp.where(lane < 64, sides[0][0], sides[1][0])
                for target, at in ((tops, 1), (counts, 2)):
                    target[rows] = jnp.where(
                        lane == 2 * hp, sides[0][at], jnp.where(lane == 2 * hp + 1, sides[1][at], target[rows])
                    )
            return carry

        lax.fori_loop(0, 6, pair, 0)

    for zl in range(2):
        pl.when(idx[3] == zl)(functools.partial(run, NEAR_TILES[zl]))


def attend_near(idx, q, own, near):
    return kernel_call(
        attend_near_body,
        [smem_spec(), vmem_spec()] + [any_spec()] * 2,
        [sds((ROWS, D), F32), sds((ROWS, 128), F32), sds((ROWS, 128), F32)],
        [vmem_spec()] * 3,
        [
            pltpu.VMEM((ROWS, 2 * D), BF),
            pltpu.VMEM((ROWS, 2 * D), BF),
            pltpu.VMEM((HALF, HALF), F32),
            pltpu.VMEM((128, 128), F32),
            pltpu.SemaphoreType.DMA((2,)),
        ],
        (idx, q, own, near),
        8e9,
        6e6,
        name="attend_near",
    )


def attend_far_body(idx, q, far, far_near, acc, tops, counts, o, lse, kvr, last, sem):
    copy = load_far(idx, far, far_near, kvr, sem)
    last[...] = tops[...] + jnp.log(counts[...])
    copy.wait()

    def column(values, head):
        return jnp.sum(jnp.where(lanes(HALF) == head, values, 0.0), axis=-1, keepdims=True)

    def run(tiles):
        covered = [half for half, _ in tiles]

        def pair(hp, carry):
            cols, vcols = pair_cols(hp)
            lane = lanes(HALF)
            for half in range(2):
                rows = half_rows(half)
                if half in covered:
                    sources = dict(tiles)[half]
                    q2 = q[rows, cols]
                    sides = []
                    for side in range(2):
                        qm = one_head(q2, side)
                        scores = [dot_nt(qm, kvr[half_rows(kh), cols]) for kh in sources]
                        before = column(tops[rows], 2 * hp + side)
                        top = before
                        for s in scores:
                            top = jnp.maximum(top, row_max(s))
                        shrink = jnp.exp(before - top)
                        total = None
                        for s, kh in zip(scores, sources):
                            part = dot(jnp.exp(s - top).astype(BF), with_ones(kvr[half_rows(kh), vcols]))
                            total = part if total is None else total + part
                        count = column(counts[rows], 2 * hp + side) * shrink + total[:, 128:]
                        value = (acc[rows, cols] * shrink + total[:, :128]) / count
                        sides.append((value, top + jnp.log(count)))
                    last[rows] = jnp.where(
                        lane == 2 * hp, sides[0][1], jnp.where(lane == 2 * hp + 1, sides[1][1], last[rows])
                    )
                else:
                    sides = [(acc[rows, cols] / column(counts[rows], 2 * hp + side),) for side in range(2)]
                o[rows, cols] = jnp.where(lane < 64, sides[0][0], sides[1][0]).astype(BF)
            return carry

        lax.fori_loop(0, 6, pair, 0)

    for zl in range(2):
        pl.when(idx[3] == zl)(functools.partial(run, FAR_TILES[zl]))
    across = jnp.transpose(last[...])
    for head in range(12):
        lse[head] = across[head : head + 1]


def attend_far(idx, q, far, far_near, state):
    return kernel_call(
        attend_far_body,
        [smem_spec(), vmem_spec()] + [any_spec()] * 2 + [vmem_spec()] * 3,
        [sds((ROWS, D), BF), sds((12, 1, ROWS), F32)],
        [vmem_spec()] * 2,
        [
            pltpu.VMEM((ROWS, 2 * D), BF),
            pltpu.VMEM((ROWS, 128), F32),
            pltpu.SemaphoreType.DMA,
        ],
        (idx, q, far, far_near, *state),
        5e9,
        6e6,
        name="attend_far",
    )


def feed_body(idx, x, o, gain, shift, out_bias, down_bias, up_bias, *rest):
    pieces, (x2, x1, h2, g, gp, ups, downs, packed, outw, sems, sems_o) = rest[:8], rest[8:]
    first = packed_copies(pieces, idx, sems_o, packed)
    later = up_down_copies(pieces, idx, sems, ups, downs)
    for copy in first + later:
        copy.start()
    for copy in first:
        copy.wait()
    unpack_output(packed, outw)
    x1[...] = x[...] + (dot(o[...], outw[...]) + out_bias[...])

    def norm_rows(i, carry):
        rows = rows_at(i * 128, 128, 128)
        unit, _ = norm_parts(x1[rows])
        h2[rows] = (unit * gain[...] + shift[...]).astype(BF)
        x2[rows] = x1[rows] + down_bias[...]
        return carry

    lax.fori_loop(0, 4, norm_rows, 0)
    for copy in later:
        copy.wait()

    def hidden(k, carry):
        for n in range(3):
            cols = slice(256 * n, 256 * (n + 1))
            u = dot(h2[...], ups[k, :, cols]) + up_bias[k, :, cols]
            uu = u * u
            t = jnp.tanh(0.7978845608028654 * u * (1.0 + 0.044715 * uu))
            half_t = 0.5 + 0.5 * t
            g[k, :, cols] = (u * half_t).astype(BF)
            slope = half_t + (0.5 * 0.7978845608028654) * u * (1.0 - t * t) * (1.0 + 0.134145 * uu)
            gp[k, :, cols] = slope.astype(BF)
        x2[...] += dot(g[k], downs[k])
        return carry

    lax.fori_loop(0, QUARTERS, hidden, 0)


WEIGHT_SCRATCH = [
    ((QUARTERS, D, D), BF),
    ((QUARTERS, D, D), BF),
    ((QUARTERS, 8, 32, D), BF),
    ((D, D), BF),
]


def feed(idx, x, o, gain, shift, out_bias, down_bias, up_bias, pieces):
    return kernel_call(
        feed_body,
        [smem_spec()] + [vmem_spec()] * 7 + [any_spec()] * 8,
        [
            sds((ROWS, D), F32),
            sds((ROWS, D), F32),
            sds((ROWS, D), BF),
            sds((QUARTERS, ROWS, D), BF),
            sds((QUARTERS, ROWS, D), BF),
        ],
        [vmem_spec()] * 5,
        [pltpu.VMEM(s, t) for s, t in WEIGHT_SCRATCH]
        + [pltpu.SemaphoreType.DMA((64,)), pltpu.SemaphoreType.DMA((32,))],
        (idx, x, o, gain, shift, out_bias, down_bias, up_bias, *pieces),
        2 * ROWS * D * D * 9,
        25e6,
        name="feed",
    )


def feed_back_body(idx, e, x1, gp, gain, *rest):
    pieces, (dm, dz, e1, da, do, small, ups, downs, packed, outw, dh2, hidden_sums, sems, sems_o) = rest[:8], rest[8:]
    first = packed_copies(pieces, idx, sems_o, packed)
    later = up_down_copies(pieces, idx, sems, ups, downs)
    for copy in later + first:
        copy.start()
    dm[...] = e[...].astype(BF)
    small[4:5] = jnp.sum(dm[...].astype(F32), axis=0, keepdims=True)
    dh2[...] = jnp.zeros_like(dh2)
    for copy in later:
        copy.wait()

    def hidden(k, carry):
        zq = idx[1] ^ k
        for n in range(3):
            cols = slice(256 * n, 256 * (n + 1))
            part = (dot_nt(dm[...], downs[k, cols]) * gp[k, :, cols].astype(F32)).astype(BF)
            dz[k, :, cols] = part
            hidden_sums[zq, :, cols] = jnp.sum(part.astype(F32), axis=0, keepdims=True)
        dh2[...] += dot_nt(dz[k], ups[k])
        return carry

    lax.fori_loop(0, QUARTERS, hidden, 0)
    for copy in first:
        copy.wait()
    unpack_output(packed, outw)
    for zq in range(QUARTERS):
        small[zq : zq + 1] = hidden_sums[zq]
    small[5:8] = jnp.zeros((3, D), F32)

    def norm_rows(i, carry):
        rows = rows_at(i * 128, 128, 128)
        unit, inverse = norm_parts(x1[rows])
        grad = dh2[rows]
        up = e[rows] + norm_backward(grad, unit, inverse, gain[...])
        e1[rows] = up
        low = up.astype(BF)
        da[rows] = low
        small[5:6] += jnp.sum(low.astype(F32), axis=0, keepdims=True)
        small[6:7] += jnp.sum(grad * unit, axis=0, keepdims=True)
        small[7:8] += jnp.sum(grad, axis=0, keepdims=True)
        return carry

    lax.fori_loop(0, 4, norm_rows, 0)
    do[...] = dot_nt(da[...], outw[...]).astype(BF)


def feed_back(idx, e, x1, gp, gain, pieces):
    return kernel_call(
        feed_back_body,
        [smem_spec()] + [vmem_spec()] * 4 + [any_spec()] * 8,
        [
            sds((ROWS, D), BF),
            sds((QUARTERS, ROWS, D), BF),
            sds((ROWS, D), F32),
            sds((ROWS, D), BF),
            sds((ROWS, D), BF),
            sds((8, D), F32),
        ],
        [vmem_spec()] * 6,
        [pltpu.VMEM(s, t) for s, t in WEIGHT_SCRATCH]
        + [pltpu.VMEM((ROWS, D), F32), pltpu.VMEM((QUARTERS, 1, D), F32), pltpu.SemaphoreType.DMA((64,)), pltpu.SemaphoreType.DMA((32,))],
        (idx, e, x1, gp, gain, *pieces),
        2 * ROWS * D * D * 9,
        25e6,
        name="feed_back",
    )


def spread(idx, keep, send, source, k, wq, rows, sem):
    w8, mine = idx[0], idx[2]
    j = (wq >> 1) ^ (w8 >> 1)
    turned = ((j & 1) << 1) | (j >> 1)
    at = ((k & 1) << 1) | (k >> 1)
    here, there = jnp.where(mine == 1, j, turned), jnp.where(mine == 1, turned, j)
    a = pltpu.make_async_copy(source, keep.at[here, at, rows], sem)
    b = pltpu.make_async_copy(source, send.at[there, at, rows], sem)
    pl.when((wq & 1) == mine)(a.start)
    pl.when((wq & 1) != mine)(b.start)
    return a


def feed_grads_body(idx, g, dm, h2, dz, o, da, keep, send, flipped, turned, d_up, d_down, d_out, sems):
    waits = []
    flipped[...] = jnp.transpose(o[...])
    turned[...] = dot(flipped[...], da[...]).astype(BF)
    for zq in range(QUARTERS):
        for chip in range(4):
            for part in range(2):
                for s in range(4):
                    rows, cols = slice(16 * (s // 2), 16 * (s // 2) + 16), slice(384 * (s % 2), 384 * (s % 2) + 384)
                    if s == 3:
                        block = jnp.zeros((16, 384), BF)
                    else:
                        row = HEADS_COLS * zq + 48 * chip + 16 * s
                        block = turned[row : row + 16, 384 * part : 384 * part + 384]
                    d_out[zq, 2 * chip + part, rows, cols] = block
    for zq in range(QUARTERS):
        k = idx[1] ^ zq
        for wq in range(8):
            sem = sems.at[len(waits)]
            waits.append(spread(idx, keep, send, d_out.at[zq, wq], k, wq, pl.ds(2 * PIECE, 32), sem))
    for k in range(QUARTERS):
        flipped[...] = jnp.transpose(g[k])
        d_down[k] = dot(flipped[...], dm[...]).astype(BF)
        for wq in range(8):
            sem = sems.at[len(waits)]
            source = d_down.at[k, pl.ds(PIECE * wq, PIECE)]
            waits.append(spread(idx, keep, send, source, k, wq, pl.ds(PIECE, PIECE), sem))
    flipped[...] = jnp.transpose(h2[...])
    for k in range(QUARTERS):
        d_up[k] = dot(flipped[...], dz[k]).astype(BF)
        for wq in range(8):
            sem = sems.at[len(waits)]
            source = d_up.at[k, pl.ds(PIECE * wq, PIECE)]
            waits.append(spread(idx, keep, send, source, k, wq, pl.ds(0, PIECE), sem))
    for copy in waits:
        copy.wait()


def feed_grads(idx, g, dm, h2, dz, o, da):
    return kernel_call(
        feed_grads_body,
        [smem_spec()] + [vmem_spec()] * 6,
        [sds((4, QUARTERS, PACK, D), BF)] * 2,
        [any_spec()] * 2,
        [
            pltpu.VMEM((D, ROWS), BF),
            pltpu.VMEM((D, D), BF),
            pltpu.VMEM((QUARTERS, D, D), BF),
            pltpu.VMEM((QUARTERS, D, D), BF),
            pltpu.VMEM((QUARTERS, 8, 32, D), BF),
            pltpu.SemaphoreType.DMA((96,)),
        ],
        (idx, g, dm, h2, dz, o, da),
        2 * ROWS * D * D * 9,
        25e6,
        name="feed_grads",
    )


def back_tile(q, do, lse, drow, cols, hp, k2, v2, qrow, n, bias_here):
    q2, g2 = q[qrow : qrow + n, cols], do[qrow : qrow + n, cols]
    sums = None
    for side in range(2):
        qm, gm, km = one_head(q2, side), one_head(g2, side), one_head(k2, side)
        head = 2 * hp + side
        s = dot_nt(k2, qm)
        if bias_here is not None:
            s = s + bias_here
        p = jnp.exp(s - lse[head, :, qrow : qrow + n])
        dp = dot_nt(v2, gm)
        ds = (p * (dp - drow[head, :, qrow : qrow + n])).astype(BF)
        parts = (dot(ds, qm), dot(p.astype(BF), gm), dot_tn(ds, km))
        sums = parts if sums is None else tuple(a + b for a, b in zip(sums, parts))
    return sums


def attend_back_far_body(idx, q, do, o, lse, far, far_near, dq, dr, drow, kvr, dcol, sem):
    copy = load_far(idx, far, far_near, kvr, sem)
    dcol[...] = jnp.zeros_like(dcol)

    def products(hp, carry):
        cols, _ = pair_cols(hp)
        lane = lanes(ROWS)
        both = do[:, cols].astype(F32) * o[:, cols].astype(F32)
        first = jnp.sum(jnp.where(lane < 64, both, 0.0), axis=-1, keepdims=True)
        second = jnp.sum(jnp.where(lane < 64, 0.0, both), axis=-1, keepdims=True)
        dcol[...] = jnp.where(lane == 2 * hp, first, jnp.where(lane == 2 * hp + 1, second, dcol[...]))
        return carry

    lax.fori_loop(0, 6, products, 0)
    across = jnp.transpose(dcol[...])
    for head in range(12):
        drow[head] = across[head : head + 1]
    copy.wait()

    def run(tiles):
        def pair(hp, carry):
            cols, vcols = pair_cols(hp)
            dq_half = [None, None]
            for kh in range(2):
                keys = half_rows(kh)
                total = None
                for half, sources in tiles:
                    if kh in sources:
                        parts = back_tile(
                            q, do, lse, drow, cols, hp, kvr[keys, cols], kvr[keys, vcols], HALF * half, HALF, None
                        )
                        total = parts[:2] if total is None else (total[0] + parts[0], total[1] + parts[1])
                        dq_half[half] = parts[2] if dq_half[half] is None else dq_half[half] + parts[2]
                if total is None:
                    total = (jnp.zeros((HALF, 128), F32),) * 2
                dr[keys, cols] = total[0].astype(BF)
                dr[keys, vcols] = total[1].astype(BF)
            for half in range(2):
                part = dq_half[half]
                dq[half_rows(half), cols] = jnp.zeros((HALF, 128), F32) if part is None else part
            return carry

        lax.fori_loop(0, 6, pair, 0)

    for zl in range(2):
        pl.when(idx[3] == zl)(functools.partial(run, FAR_TILES[zl]))


def attend_back_far(idx, q, do, o, lse, far, far_near):
    return kernel_call(
        attend_back_far_body,
        [smem_spec()] + [vmem_spec()] * 4 + [any_spec()] * 2,
        [sds((ROWS, D), F32), sds((ROWS, 2 * D), BF), sds((12, 1, ROWS), F32)],
        [vmem_spec()] * 3,
        [
            pltpu.VMEM((ROWS, 2 * D), BF),
            pltpu.VMEM((ROWS, 128), F32),
            pltpu.SemaphoreType.DMA,
        ],
        (idx, q, do, o, lse, far, far_near),
        12e9,
        8e6,
        name="attend_back_far",
    )


def attend_back_near_body(idx, q, do, lse, drow, dq_far, own, near, dq, dn, dc, kvn, kvc, bias, bias_n, sems):
    waits = load_near(idx, own, near, kvn, kvc, sems)
    set_masks(idx, bias, bias_n, 1)
    for copy in waits:
        copy.wait()

    def run(tiles):
        def pair(hp, carry):
            cols, vcols = pair_cols(hp)
            dq_half = [None, None]
            for half in range(2):
                pieces = []
                for t in range(2):
                    rows = slice(HALF * half + 128 * t, HALF * half + 128 * (t + 1))
                    dk, dv, dqs = back_tile(
                        q, do, lse, drow, cols, hp, kvn[rows, cols], kvn[rows, vcols], rows.start, 128, bias_n[...]
                    )
                    dn[rows, cols] = dk.astype(BF)
                    dn[rows, vcols] = dv.astype(BF)
                    pieces.append(dqs)
                dq_half[half] = dq_far[half_rows(half), cols] + jnp.concatenate(pieces, axis=0)
            for kh in range(2):
                keys = half_rows(kh)
                total = None
                for half, sources in tiles:
                    if kh in dict(sources):
                        parts = back_tile(
                            q,
                            do,
                            lse,
                            drow,
                            cols,
                            hp,
                            kvc[keys, cols],
                            kvc[keys, vcols],
                            HALF * half,
                            HALF,
                            bias[...] if dict(sources)[kh] else None,
                        )
                        total = parts[:2] if total is None else (total[0] + parts[0], total[1] + parts[1])
                        dq_half[half] = dq_half[half] + parts[2]
                dc[keys, cols] = total[0].astype(BF)
                dc[keys, vcols] = total[1].astype(BF)
            for half in range(2):
                dq[half_rows(half), cols] = dq_half[half] * 0.125
            return carry

        lax.fori_loop(0, 6, pair, 0)

    for zl in range(2):
        pl.when(idx[3] == zl)(functools.partial(run, NEAR_TILES[zl]))


def attend_back_near(idx, q, do, lse, drow, dq_far, own, near):
    return kernel_call(
        attend_back_near_body,
        [smem_spec()] + [vmem_spec()] * 5 + [any_spec()] * 2,
        [sds((ROWS, D), F32), sds((ROWS, 2 * D), BF), sds((ROWS, 2 * D), BF)],
        [vmem_spec()] * 3,
        [
            pltpu.VMEM((ROWS, 2 * D), BF),
            pltpu.VMEM((ROWS, 2 * D), BF),
            pltpu.VMEM((HALF, HALF), F32),
            pltpu.VMEM((128, 128), F32),
            pltpu.SemaphoreType.DMA((2,)),
        ],
        (idx, q, do, lse, drow, dq_far, own, near),
        18e9,
        12e6,
        name="attend_back_near",
    )


def project_back_body(idx, dq, dn, dcr, got, far, cosine, sine, x, e1, gain, *rest):
    pieces, (dpz, e, small, weights, wide, sems) = rest[:8], rest[8:]
    copies = mixer_copies(pieces, idx, sems, weights)
    for copy in copies:
        copy.start()
    noisy = idx[2] == 0
    for half in range(2):
        rows = slice(HALF * half, HALF * (half + 1))
        for j in range(6):
            cols = slice(128 * j, 128 * (j + 1))
            wide[rows, cols] = unrot(dq[rows, cols], cosine[rows], sine[rows])

        def total(cols, at=rows):
            summed = dcr[at, cols].astype(F32) + got[at, cols].astype(F32) + far[at, cols].astype(F32)
            return jnp.where(noisy, dn[at, cols].astype(F32), summed)

        for j in range(6):
            cols = slice(128 * j, 128 * (j + 1))
            wide[rows, D + 128 * j : D + 128 * (j + 1)] = unrot(total(cols), cosine[rows], sine[rows])
        wide[rows, 2 * D :] = total(slice(D, 2 * D))
    for copy in copies:
        copy.wait()
    small[...] = jnp.zeros_like(small)
    for zq in range(QUARTERS):
        for part in range(3):
            col = D * part + HEADS_COLS * zq
            dpz[zq, :, HEADS_COLS * part : HEADS_COLS * (part + 1)] = wide[:, col : col + HEADS_COLS].astype(BF)
        small[zq : zq + 1, :PARTS] = jnp.sum(dpz[zq].astype(F32), axis=0, keepdims=True)
        piece = dot_nt(dpz[zq], weights[zq])
        if zq == 0:
            e[...] = piece
        else:
            e[...] += piece

    def norm_rows(i, carry):
        rows = rows_at(i * 128, 128, 128)
        unit, inverse = norm_parts(x[rows])
        grad = e[rows]
        small[4:5] += jnp.sum(grad * unit, axis=0, keepdims=True)
        small[5:6] += jnp.sum(grad, axis=0, keepdims=True)
        e[rows] = e1[rows] + norm_backward(grad, unit, inverse, gain[...])
        return carry

    lax.fori_loop(0, 4, norm_rows, 0)


def project_back(idx, dq, dn, dcr, got, far, cosine, sine, x, e1, gain, pieces):
    return kernel_call(
        project_back_body,
        [smem_spec()] + [vmem_spec()] * 10 + [any_spec()] * 8,
        [sds((QUARTERS, ROWS, PARTS), BF), sds((ROWS, D), F32), sds((8, D), F32)],
        [vmem_spec()] * 3,
        [
            pltpu.VMEM((QUARTERS, D, PARTS), BF),
            pltpu.VMEM((ROWS, 3 * D), F32),
            pltpu.SemaphoreType.DMA((32,)),
        ],
        (idx, dq, dn, dcr, got, far, cosine, sine, x, e1, gain, *pieces),
        2 * ROWS * D * 3 * D,
        12e6,
        name="project_back",
    )


def project_grads_body(idx, h1, dpz, keep, send, flipped, stage, sems):
    waits = []
    flipped[...] = jnp.transpose(h1[...])
    for zq in range(QUARTERS):
        k = idx[1] ^ zq
        stage[zq] = dot(flipped[...], dpz[zq]).astype(BF)
        for wq in range(8):
            sem = sems.at[len(waits)]
            source = stage.at[zq, pl.ds(PIECE * wq, PIECE)]
            waits.append(spread(idx, keep, send, source, k, wq, pl.ds(0, PIECE), sem))
    for copy in waits:
        copy.wait()


def project_grads(idx, h1, dpz):
    return kernel_call(
        project_grads_body,
        [smem_spec()] + [vmem_spec()] * 2,
        [sds((4, QUARTERS, PIECE, PARTS), BF)] * 2,
        [any_spec()] * 2,
        [
            pltpu.VMEM((D, ROWS), BF),
            pltpu.VMEM((QUARTERS, D, PARTS), BF),
            pltpu.SemaphoreType.DMA((32,)),
        ],
        (idx, h1, dpz),
        2 * ROWS * D * 3 * D,
        9e6,
        name="project_grads",
    )


def finish_mixer_body(layer, filled, idx, *rest):
    pieces, rest = rest[:8], rest[8:]
    if filled:
        rest = rest[1:]
    out, stage, sem = rest
    for flip, piece in zip(flips(idx), pieces):
        stage[rows_at((idx[0] ^ flip) * PIECE, PIECE, 32)] = piece[...].astype(F32)
    copy = pltpu.make_async_copy(stage, out.at[layer], sem)
    copy.start()
    copy.wait()


def finish_mixer(idx, layer, layers, pieces, before):
    filled = before is not None
    return kernel_call(
        functools.partial(finish_mixer_body, layer, filled),
        [smem_spec()] + [vmem_spec()] * 8 + [any_spec()] * filled,
        sds((layers, D, PARTS), F32),
        any_spec(),
        [pltpu.VMEM((D, PARTS), F32), pltpu.SemaphoreType.DMA],
        (idx, *pieces) + ((before,) if filled else ()),
        1e6,
        4e6,
        aliases={9: 0} if filled else None,
        name="finish_mixer",
    )


def finish_feed_body(layer, filled, idx, *rest):
    pieces, rest = rest[:8], rest[8:]
    if filled:
        rest = rest[3:]
    up, down, out, up_s, down_s, out_s, sems = rest
    for flip, piece in zip(flips(idx), pieces):
        wq = idx[0] ^ flip
        rows = rows_at(wq * PIECE, PIECE, 32)
        up_s[rows] = piece[:PIECE].astype(F32)
        down_s[rows] = piece[PIECE : 2 * PIECE].astype(F32)
        cols = pl.ds(pl.multiple_of((wq & 1) * 384, 128), 384)
        for s in range(3):
            row = 2 * PIECE + 16 * (s // 2)
            block = piece[row : row + 16, 384 * (s % 2) : 384 * (s % 2) + 384]
            out_s[rows_at((wq >> 1) * 48 + 16 * s, 16, 16), cols] = block.astype(F32)
    copies = [
        pltpu.make_async_copy(stage, whole.at[layer], sems.at[i])
        for i, (stage, whole) in enumerate(((up_s, up), (down_s, down), (out_s, out)))
    ]
    for copy in copies:
        copy.start()
    for copy in copies:
        copy.wait()


def finish_feed(idx, layer, layers, pieces, before):
    filled = before is not None
    return kernel_call(
        functools.partial(finish_feed_body, layer, filled),
        [smem_spec()] + [vmem_spec()] * 8 + [any_spec()] * (3 * filled),
        [sds((layers, D, D), F32), sds((layers, D, D), F32), sds((layers, HEADS_COLS, D), F32)],
        [any_spec()] * 3,
        [
            pltpu.VMEM((D, D), F32),
            pltpu.VMEM((D, D), F32),
            pltpu.VMEM((HEADS_COLS, D), F32),
            pltpu.SemaphoreType.DMA((3,)),
        ],
        (idx, *pieces) + (tuple(before) if filled else ()),
        1e6,
        8e6,
        aliases={9: 0, 10: 1, 11: 2} if filled else None,
        name="finish_feed",
    )


def pack_body(idx, ups, downs, outs, *rest):
    targets, (zeros, sems) = rest[:-2], rest[-2:]
    zeros[...] = jnp.zeros_like(zeros)
    rows = rows_at(idx[0] * PIECE, PIECE, 32)
    cols = pl.ds(pl.multiple_of(idx[2] * 384, 128), 384)
    copies = []
    for layer, target in enumerate(targets):
        moves = [
            (ups.at[layer, rows], target.at[pl.ds(0, PIECE)]),
            (downs.at[layer, rows], target.at[pl.ds(PIECE, PIECE)]),
        ]
        for s in range(4):
            place = target.at[pl.ds(2 * PIECE + 16 * (s // 2), 16), pl.ds(384 * (s % 2), 384)]
            if s == 3:
                moves.append((zeros, place))
            else:
                moves.append((outs.at[layer, rows_at((idx[0] >> 1) * 48 + 16 * s, 16, 16), cols], place))
        for source, place in moves:
            copies.append(pltpu.make_async_copy(source, place, sems.at[len(copies)]))
    for copy in copies:
        copy.start()
    for copy in copies:
        copy.wait()


def pack(idx, ups, downs, outs):
    layers = ups.shape[0]
    return kernel_call(
        pack_body,
        [smem_spec()] + [any_spec()] * 3,
        [sds((PACK, D), BF)] * layers,
        [vmem_spec()] * layers,
        [pltpu.VMEM((16, 384), BF), pltpu.SemaphoreType.DMA((6 * layers,))],
        (idx, ups, downs, outs),
        1e6,
        1e6,
        name="pack",
    )


def flip_wide(x, bit):
    return lax.ppermute(x, "wide", [(i, i ^ bit) for i in range(lax.axis_size("wide"))])


def flip_narrow(x, bit):
    return lax.ppermute(x, "narrow", [(i, i ^ bit) for i in range(QUARTERS)])


def first_axis(x):
    return lax.ppermute(x, "wide", [(i, i ^ (4 if i & 1 else 2)) for i in range(lax.axis_size("wide"))])


def second_axis(x):
    return lax.ppermute(x, "wide", [(i, i ^ (2 if i & 1 else 4)) for i in range(lax.axis_size("wide"))])


def gate_body(*refs):
    return None


def gate(tree):
    leaves, shape = jax.tree.flatten(tree)
    out = pl.pallas_call(
        gate_body,
        in_specs=[any_spec() for _ in leaves],
        out_specs=[any_spec() for _ in leaves],
        out_shape=[sds(x.shape, x.dtype) for x in leaves],
        input_output_aliases={i: i for i in range(len(leaves))},
        name="gate",
    )(*leaves)
    return jax.tree.unflatten(shape, out)


def gather_direct(piece):
    return [piece] + [flip_narrow(piece, k) for k in ORDER[1:]]


def gather_far(piece):
    return piece, flip_narrow(piece, 2)


def gather_near(pair):
    pair = jnp.stack(pair)
    return pair, flip_narrow(pair, 1)


def whole(parts):
    return jnp.stack(parts) if parts[0].ndim == 2 else jnp.concatenate(parts)


def gather_first(own):
    return own, first_axis(own)


def gather_second(parts):
    own, first = parts
    return [own, first, second_axis(own), second_axis(first)]


def gather_last(here):
    return here + [flip_wide(x, 1) for x in here]


def added(*terms):
    return functools.reduce(jnp.add, [t.astype(F32) for t in terms]).astype(BF)


def reduce_core(pair):
    keep, send = pair
    return keep, flip_wide(send, 1)


def reduce_first(pair):
    keep, got = pair
    return keep, got, first_axis(added(keep[2:], got[2:]))


def reduce_second(parts):
    keep, got, first = parts
    return keep, got, first, second_axis(added(keep[1], got[1], first[1]))


def reduce_near(parts):
    keep, got, first, second = parts
    total = added(keep[0], got[0], first[0], second)
    bit = 8
    while bit < lax.axis_size("wide"):
        total = added(total, flip_wide(total, bit))
        bit *= 2
    return total, flip_narrow(total[2:], 1)


def reduce_far(parts):
    total, near = parts
    return total, near, flip_narrow(added(total[1], near[1]), 2)


def spread_first(parts):
    total, near, far = parts
    return gather_first(added(total[0], near[0], far))


def device_pairs(move):
    pairs = []
    for w in range(lax.axis_size("wide")):
        for z in range(QUARTERS):
            target = move(w, z)
            if target is not None:
                pairs.append((w * QUARTERS + z, target[0] * QUARTERS + target[1]))
    return pairs


BOTH = ("wide", "narrow")


def relocate(rows):
    first = device_pairs(lambda w, z: ((w & ~1) | (z >> 1), ((w & 1) << 1) | (z & 1)))
    second = device_pairs(lambda w, z: ((w & ~1) | (z >> 1), ((w & 1) << 1) | (1 - (z & 1))))
    return lax.ppermute(rows[:HALF], BOTH, first), lax.ppermute(rows[HALF:], BOTH, second)


def between_chips(x):
    pairs = device_pairs(lambda w, z: (w, z ^ 1) if w & 1 else None)
    return lax.ppermute(x, BOTH, pairs)


def within_chip(x, source):
    pairs = [(i, i ^ 1) for i in range(lax.axis_size("wide")) if (i & 1) == source]
    return lax.ppermute(x, "wide", pairs)


def per_device(
    tokens,
    block_size,
    norm_gain,
    norm_shift,
    mixer_weight,
    mixer_bias,
    output_weight,
    output_bias,
    up_weight,
    up_bias,
    down_weight,
    cotangent,
):
    layers = norm_gain.shape[0]
    w, z = lax.axis_index("wide"), lax.axis_index("narrow")
    w8, core, low = w & 7, w & 1, z & 1
    sizes = jnp.where((z >> 1) == core, block_size, flip_wide(block_size, 1))[0]
    level = 2 + (sizes >= 8).astype(jnp.int32) + (sizes >= 16).astype(jnp.int32)
    idx = jnp.stack([w8, z, core, low, level, w8, w8, w8]).astype(jnp.int32)

    bases = jnp.where(low == 0, jnp.array([0, 768]), jnp.array([512, 256]))
    position = (bases[:, None] + jnp.arange(HALF)[None, :]).reshape(ROWS).astype(F32)
    halfway = HEAD_DIM // 2
    frequency = jnp.exp(jnp.arange(halfway, dtype=F32) * (-math.log(10000.0) / halfway))
    angle = position[:, None] * frequency[None, :]
    cosine = jnp.tile(jnp.cos(angle), (1, 4))
    sine = jnp.sin(angle)
    sine = jnp.concatenate([-sine, sine, -sine, sine], axis=1)

    def bias_pieces(layer):
        return mixer_bias[layer].reshape(PARTS), up_bias[layer]

    biases = jnp.concatenate([t for layer in range(layers) for t in bias_pieces(layer)])
    width = PARTS + D

    def bias_of(layer, start, size):
        at = width * layer + start
        by_flip = dict(zip(ORDER, biases))
        return jnp.stack([by_flip[k][at : at + size] for k in range(QUARTERS)])[:, None]

    def mixer_piece(layer):
        return lax.dynamic_slice_in_dim(mixer_weight[layer], w8 * PIECE, PIECE, 0).reshape(PIECE, PARTS)

    def run_project(layer, x, pieces):
        gain, shift = norm_gain[layer], norm_shift[layer]
        return project(idx, x, gain[0:1], shift[0:1], bias_of(layer, 0, PARTS), cosine, sine, pieces)

    def run_feed(layer, x, o, pieces):
        gain, shift, bias = norm_gain[layer], norm_shift[layer], output_bias[layer]
        return feed(
            idx, x, o, gain[1:2], shift[1:2], bias[0:1], bias[1:2], bias_of(layer, PARTS, D), pieces
        )

    mixer0 = gather_direct(mixer_piece(0))
    feed0, feed1 = pack(idx, up_weight, down_weight, output_weight)
    mixer0, tokens, feed0, biases = gate((mixer0, tokens, feed0, biases))
    mixer0 = gather_first(whole(mixer0))
    rows = relocate(tokens)
    mixer0, feed0, biases, mixer1 = gate((mixer0, feed0, biases, mixer_piece(1)))
    own, first = mixer0
    mixer0 = [own, first, second_axis(own), second_axis(first)]
    feed0, biases = gather_direct(feed0), gather_direct(biases)
    mixer0, rows, biases = gate((mixer0, rows, biases))
    mixer0 = gather_last(mixer0)
    x0 = jnp.concatenate(rows).astype(F32)
    h1_0, q_0, kv = run_project(0, x0, mixer0)
    own_0 = gate(kv)
    near_0, far = within_chip(own_0, 1), between_chips(own_0)
    near_0, q_0, feed0, mixer1 = gate((near_0, q_0, feed0, mixer1))
    own, first = gather_first(whole(feed0))
    state = attend_near(idx, q_0, own_0, near_0)
    state, far_0, own, first, mixer1, feed1 = gate((state, far, own, first, mixer1, feed1))
    far_near_0 = within_chip(far_0, 1)
    second = second_axis(own)
    mixer1 = gather_direct(mixer1)
    o_0, lse_0 = attend_far(idx, q_0, far_0, far_near_0, state)
    o_0, own, first, second, mixer1, feed1 = gate((o_0, own, first, second, mixer1, feed1))
    third = second_axis(first)
    others = [flip_wide(own, 1), flip_wide(first, 1), flip_wide(second, 1)]
    mixer1, feed1 = gather_first(whole(mixer1)), gather_far(feed1)
    third, others, o_0, mixer1, feed1 = gate((third, others, o_0, mixer1, feed1))
    feed0 = [own, first, second, third] + others + [flip_wide(third, 1)]
    mixer1, feed1 = gather_second(mixer1), gather_near(feed1)
    x1, x1_0, h2_0, g_0, gp_0 = run_feed(0, x0, o_0, feed0)
    x1, mixer1, feed1 = gate((x1, mixer1, feed1))
    mixer1 = gather_last(mixer1)
    own, first = gather_first(whole(feed1))
    h1_1, q_1, kv = run_project(1, x1, mixer1)
    own_1 = gate(kv)
    near_1, far = within_chip(own_1, 1), between_chips(own_1)
    near_1, q_1, own, first = gate((near_1, q_1, own, first))
    second = second_axis(own)
    state = attend_near(idx, q_1, own_1, near_1)
    state, far_1, own, first, second, cotangent = gate((state, far, own, first, second, cotangent))
    far_near_1 = within_chip(far_1, 1)
    third = second_axis(first)
    others = [flip_wide(own, 1), flip_wide(first, 1), flip_wide(second, 1)]
    e = relocate(cotangent)
    o_1, lse_1 = attend_far(idx, q_1, far_1, far_near_1, state)
    o_1, third, others, e = gate((o_1, third, others, e))
    feed1 = [own, first, second, third] + others + [flip_wide(third, 1)]
    x2, x1_1, h2_1, g_1, gp_1 = run_feed(1, x1, o_1, feed1)
    x_out = relocate(x2.astype(BF))

    e = jnp.concatenate(e).astype(F32)
    dm, dz, e1, da, do, small_feed1 = feed_back(idx, e, x1_1, gp_1, norm_gain[1, 1:2], feed1)
    g_feed1 = feed_grads(idx, g_1, dm, h2_1, dz, o_1, da)
    do, x_out, g_feed1 = gate((do, x_out, g_feed1))
    g_feed1 = reduce_core(g_feed1)
    dq, dr, drow = attend_back_far(idx, q_1, do, o_1, lse_1, far_1, far_near_1)
    dr, dq, g_feed1 = gate((dr, dq, g_feed1))
    far = between_chips(added(dr, within_chip(dr, 0)))
    g_feed1 = reduce_first(g_feed1)
    dq, dn, dc = attend_back_near(idx, q_1, do, lse_1, drow, dq, own_1, near_1)
    dc, far, g_feed1 = gate((dc, far, g_feed1))
    got = within_chip(dc, 0)
    g_feed1 = reduce_second(g_feed1)
    dpz, e, small_mixer1 = project_back(
        idx, dq, dn, dc, got, far, cosine, sine, x1, e1, norm_gain[1, 0:1], mixer1
    )
    dpz, e, g_feed1 = gate((dpz, e, g_feed1))
    g_feed1 = reduce_near(g_feed1)
    g_mixer1 = project_grads(idx, h1_1, dpz)
    e, g_mixer1 = gate((e, g_mixer1))
    g_mixer1 = reduce_core(g_mixer1)
    dm, dz, e1, da, do, small_feed0 = feed_back(idx, e, x1_0, gp_0, norm_gain[0, 1:2], feed0)
    dm, do, g_feed1, g_mixer1 = gate((dm, do, g_feed1, g_mixer1))
    g_feed1, g_mixer1 = reduce_far(g_feed1), reduce_first(g_mixer1)
    g_feed0 = feed_grads(idx, g_0, dm, h2_0, dz, o_0, da)
    do, g_feed1, g_mixer1, g_feed0 = gate((do, g_feed1, g_mixer1, g_feed0))
    g_feed1, g_mixer1, g_feed0 = spread_first(g_feed1), reduce_second(g_mixer1), reduce_core(g_feed0)
    dq, dr, drow = attend_back_far(idx, q_0, do, o_0, lse_0, far_0, far_near_0)
    dr, dq, g_feed1, g_mixer1, g_feed0 = gate((dr, dq, g_feed1, g_mixer1, g_feed0))
    far = between_chips(added(dr, within_chip(dr, 0)))
    g_feed0, g_mixer1 = reduce_first(g_feed0), reduce_near(g_mixer1)
    dq, dn, dc = attend_back_near(idx, q_0, do, lse_0, drow, dq, own_0, near_0)
    dc, far, g_feed0, g_mixer1 = gate((dc, far, g_feed0, g_mixer1))
    got = within_chip(dc, 0)
    g_feed0, g_mixer1 = reduce_second(g_feed0), reduce_far(g_mixer1)
    dpz, e, small_mixer0 = project_back(
        idx, dq, dn, dc, got, far, cosine, sine, x0, e1, norm_gain[0, 0:1], mixer0
    )
    dpz, g_feed0, g_feed1, g_mixer1 = gate((dpz, g_feed0, g_feed1, g_mixer1))
    g_feed0, g_feed1, g_mixer1 = reduce_near(g_feed0), gather_second(g_feed1), spread_first(g_mixer1)
    g_mixer0 = project_grads(idx, h1_0, dpz)
    smalls = jnp.concatenate([small_feed0, small_mixer0, small_feed1, small_mixer1])
    e, g_mixer0, g_feed1, g_mixer1, smalls = gate((e, g_mixer0, g_feed1, g_mixer1, smalls))
    g_mixer0 = reduce_core(g_mixer0)
    g_feed1, g_mixer1 = gather_last(g_feed1), gather_second(g_mixer1)
    smalls = smalls, flip_wide(smalls, 1)
    g_mixer0, g_feed1, g_mixer1, smalls, e = gate((g_mixer0, g_feed1, g_mixer1, smalls, e))
    g_mixer0, g_mixer1 = reduce_first(g_mixer0), gather_last(g_mixer1)
    rows = relocate(e.astype(BF))
    smalls = smalls[0] + smalls[1]
    smalls = smalls, first_axis(smalls)
    feed_out = finish_feed(idx, 1, layers, g_feed1, None)
    g_mixer0, g_feed0, g_mixer1, smalls = gate((g_mixer0, g_feed0, g_mixer1, smalls))
    g_mixer0, g_feed0 = reduce_second(g_mixer0), reduce_far(g_feed0)
    smalls = smalls[0] + smalls[1]
    smalls = smalls, second_axis(smalls)
    mixer_out = finish_mixer(idx, 1, layers, g_mixer1, None)
    g_mixer0, smalls, rows = gate((g_mixer0, smalls, rows))
    g_mixer0 = reduce_near(g_mixer0)
    smalls = smalls[0] + smalls[1]
    bit = 8
    while bit < lax.axis_size("wide"):
        smalls = smalls + flip_wide(smalls, bit)
        bit *= 2
    smalls = smalls, flip_narrow(smalls, 1)
    g_mixer0, g_feed0, smalls = gate((g_mixer0, g_feed0, smalls))
    g_mixer0, g_feed0 = reduce_far(g_mixer0), spread_first(g_feed0)
    smalls = smalls[0] + smalls[1]
    smalls = smalls, flip_narrow(smalls, 2)
    g_mixer0, g_feed0, smalls = gate((g_mixer0, g_feed0, smalls))
    g_mixer0, g_feed0 = spread_first(g_mixer0), gather_second(g_feed0)
    smalls = smalls[0] + smalls[1]
    g_mixer0, g_feed0 = gate((g_mixer0, g_feed0))
    g_mixer0, g_feed0 = gather_second(g_mixer0), gather_last(g_feed0)
    g_mixer0, feed_out, g_feed0 = gate((g_mixer0, feed_out, g_feed0))
    g_mixer0 = gather_last(g_mixer0)
    feed_out = finish_feed(idx, 0, layers, g_feed0, feed_out)
    mixer_out = finish_mixer(idx, 0, layers, g_mixer0, mixer_out)
    tokens_grad = jnp.concatenate(rows)
    x_out = jnp.concatenate(x_out)

    small = smalls.reshape(layers, 16, D)
    up_bias_grad = lax.dynamic_index_in_dim(small[:, 0:4], z, 1, keepdims=False)
    mixer_bias_grad = lax.dynamic_index_in_dim(small[:, 8:12, :PARTS], z, 1, keepdims=False)
    return (
        x_out,
        tokens_grad,
        jnp.stack([small[:, 12], small[:, 6]], axis=1),
        jnp.stack([small[:, 13], small[:, 7]], axis=1),
        mixer_out.reshape(layers, D, 3, HEADS_COLS),
        mixer_bias_grad.reshape(layers, 3, HEADS_COLS),
        feed_out[2],
        jnp.stack([small[:, 5], small[:, 4]], axis=1),
        feed_out[0],
        up_bias_grad,
        feed_out[1],
    )


def solution(mesh):
    rows = P(("wide", "narrow"), None)
    quarters = (
        P(None, None, None, "narrow"),
        P(None, None, "narrow"),
        P(None, "narrow", None),
        P(),
        P(None, None, "narrow"),
        P(None, "narrow"),
        P(None, "narrow", None),
    )
    return jax.shard_map(
        per_device,
        mesh=mesh,
        in_specs=(rows, P("wide"), P(), P()) + quarters + (rows,),
        out_specs=(rows, rows, P(), P()) + quarters,
        check_vma=False,
    )
```

time: 905 us -> 737 us (0.81)
  waiting for transfers between devices: 310 us -> 167 us
  starting transfers between devices: 230 us -> 128 us
  local copies, waits for them, and re-layouts: 45.1 us -> 71.1 us
  Pallas kernels: 272 us -> 296 us
  other arithmetic: 36.8 us -> 59.5 us
    ppermute x111 -> x38, waiting for transfers between devices: 206 us -> 8.48 us  [flip_wide(): lax.ppermute(x, 'wide', [(i, i ^ bit) for i in range(lax.axis_size('wide'...]
    ppermute x111 -> x38, starting transfers between devices: 103 us -> 15.1 us  [flip_wide(): lax.ppermute(x, 'wide', [(i, i ^ bit) for i in range(lax.axis_size('wide'...]
    ppermute x31 -> x58, waiting for transfers between devices: 103 us -> 149 us  [the longest x24 80.6 us: flip_narrow(): return lax.ppermute(x, 'narrow', [(i, i ^ bit) for i in range(QUARTERS)])]
    ppermute x31 -> x58, starting transfers between devices: 47.9 us -> 85.5 us  [the longest x24 47.8 us: flip_narrow(): return lax.ppermute(x, 'narrow', [(i, i ^ bit) for i in range(QUARTERS)])]
    unnamed x263 -> x336, local copies, waits for them, and re-layouts: 14.4 us -> 49.3 us
    ppermute x16 -> x8, starting transfers between devices: 43.8 us -> 13 us  [within_chip(): return lax.ppermute(x, 'wide', pairs)]
    pallas_call x20 -> x25, Pallas kernels: 272 us -> 296 us  [kernel_call(): pl.pallas_call(body, in_specs=in_specs, out_specs=out_specs, out_shape=ou...]
    convert_element_type x28 -> x22, other arithmetic: 20.2 us -> 39.7 us  [added(): return functools.reduce(jnp.add, [t.astype(F32) for t in terms]).astype(BF)]
  transfers between devices with their start and end apart: 174 -> 116, of which waited for: 43 -> 34; matrix products, arithmetic and copies ran while one was open for 8% -> 9% of each run, Pallas kernels for 15% -> 34%
where the time goes in v2:
time: 737 us; the launch traced here: 726 us
  Pallas kernels  296 us (40%)
  waiting for transfers between devices  167 us (23%)
  starting transfers between devices  128 us (17%)
  local copies, waits for them, and re-layouts  71.1 us (10%)
  other arithmetic  59.5 us (8%)
    pallas_call x25, Pallas kernels, kernel_call(): pl.pallas_call(body, in_specs=in_specs, out_specs=out_specs, out_shape=ou...  296 us
    ppermute x24, waiting for transfers between devices, flip_narrow(): return lax.ppermute(x, 'narrow', [(i, i ^ bit) for i in range(QUARTERS)])  80.6 us
    unnamed x336, local copies, waits for them, and re-layouts  49.3 us
    ppermute x24, starting transfers between devices, flip_narrow(): return lax.ppermute(x, 'narrow', [(i, i ^ bit) for i in range(QUARTERS)])  47.8 us
    ppermute x13, waiting for transfers between devices, first_axis(): lax.ppermute(x, 'wide', [(i, i ^ (4 if i & 1 else 2)) for i in range(lax....  42.7 us
    convert_element_type x22, other arithmetic, added(): return functools.reduce(jnp.add, [t.astype(F32) for t in terms]).astype(BF)  39.7 us
    ppermute x21, waiting for transfers between devices, second_axis(): lax.ppermute(x, 'wide', [(i, i ^ (2 if i & 1 else 4)) for i in range(lax....  25.6 us
    ppermute x21, starting transfers between devices, second_axis(): lax.ppermute(x, 'wide', [(i, i ^ (2 if i & 1 else 4)) for i in range(lax....  22.7 us
  transfers between devices with their start and end apart: 116, of which 34 were waited for; matrix products, arithmetic and copies ran while one was open for 9% of the time, Pallas kernels for 34%

profile of v2, /device:TPU:0, one launch (start us, length us, event | category | flops | bytes accessed | tf_op | source)
XLA Modules:
  0.0 726.4 jit_solution(14591233062067642176)
XLA Ops:
  81.0 9.4 %collective-permute-done.18.refs_4_ = bf16[224,768]{1,0:T(8,128)(2,1)S(1)} collective-permute-done((bf16[224,768]{1,0:T(8,128)(2,1)S(1)}, bf16[224,768]{1,0:T(8,128)(2,1)S(1)}, u32[]{:S(2)}, u32[]{:S(2)}) %collective-permute-start.18) | collective-permute-done | bytes 344096 | tf_op jit(solution)/shard_map/ppermute | solution.py:984
  90.4 12.3 %collective-permute-done.17.refs_3_ = bf16[224,768]{1,0:T(8,128)(2,1)S(1)} collective-permute-done((bf16[224,768]{1,0:T(8,128)(2,1)S(1)}, bf16[224,768]{1,0:T(8,128)(2,1)S(1)}, u32[]{:S(2)}, u32[]{:S(2)}) %collective-permute-start.17) | collective-permute-done | bytes 344096 | tf_op jit(solution)/shard_map/ppermute | solution.py:984
  105.3 18.2 %attend_near.2 = (f32[512,768]{1,0:T(8,128)}, f32[512,128]{1,0:T(8,128)}, f32[512,128]{1,0:T(8,128)}) custom-call(s32[8]{0:T(128)} %stack.146.idx, bf16[512,768]{1,0:T(8,128)(2,1)} %get-tuple-element.339.q, bf16[512,1536]{1,0:T(8,128)(2,1)} %gate.34.own, bf16[512,1536]{1,0:T(8,128)(2,1)} %get-tuple-element.340.near), custom_call_target="tpu_custom_call" | custom-call | flops 1000 | bytes 1000 | tf_op jit(solution)/shard_map/attend_near/pallas_call | solution.py:140
  133.8 8.4 %attend_far.2 = (bf16[512,768]{1,0:T(8,128)(2,1)}, f32[12,1,512]{2,1,0:T(1,128)}) custom-call(s32[8]{0:T(128)} %stack.146.idx, bf16[512,768]{1,0:T(8,128)(2,1)} %get-tuple-element.339.q, bf16[512,1536]{1,0:T(8,128)(2,1)} %get-tuple-element.350.far, bf16[512,1536]{1,0:T(8,128)(2,1)} %copy-done.33, f32[512,768]{1,0:T(8,128)} %get-tuple-element.351.acc, ...), custom_call_target="tpu_custom_call" | custom-call | flops 1000 | bytes 1000 | tf_op jit(solution)/shard_map/attend_far/pallas_call | solution.py:140
  149.7 15.7 %collective-permute-done.32.refs_8_ = bf16[224,768]{1,0:T(8,128)(2,1)S(1)} collective-permute-done((bf16[224,768]{1,0:T(8,128)(2,1)}, bf16[224,768]{1,0:T(8,128)(2,1)S(1)}, u32[]{:S(2)}, u32[]{:S(2)}) %collective-permute-start.32) | collective-permute-done | bytes 344096 | tf_op jit(solution)/shard_map/ppermute | solution.py:984
  182.8 20.1 %feed.2 = (f32[512,768]{1,0:T(8,128)}, f32[512,768]{1,0:T(8,128)}, bf16[512,768]{1,0:T(8,128)(2,1)}, bf16[4,512,768]{2,1,0:T(8,128)(2,1)}, bf16[4,512,768]{2,1,0:T(8,128)(2,1)}) custom-call(s32[8]{0:T(128)} %stack.146.idx, f32[512,768]{1,0:T(8,128)} %maximum_convert_fusion.x, bf16[512,768]{1,0:T(8,128)(2,1)} %get-tuple-element.368.o, ...), custom_call_target="tpu_custom_call" | custom-call | flops 1000 | bytes 1000 | tf_op jit(solution)/shard_map/feed/pallas_call | solution.py:140
  209.1 8.3 %project.3 = (bf16[512,768]{1,0:T(8,128)(2,1)}, bf16[512,768]{1,0:T(8,128)(2,1)}, bf16[512,1536]{1,0:T(8,128)(2,1)}) custom-call(s32[8]{0:T(128)} %stack.146.idx, f32[512,768]{1,0:T(8,128)} %get-tuple-element.378.x, f32[1,768]{1,0:T(1,128)} %get-tuple-element.703.gain, f32[1,768]{1,0:T(1,128)} %get-tuple-element.685.shift, ...), custom_call_target="tpu_custom_call" | custom-call | flops 1000 | bytes 1000 | tf_op jit(solution)/shard_map/project/pallas_call | solution.py:140
  222.3 15.0 %collective-permute-done.42.refs_3_ = bf16[4,224,768]{2,1,0:T(8,128)(2,1)S(1)} collective-permute-done((bf16[4,224,768]{2,1,0:T(8,128)(2,1)S(1)}, bf16[4,224,768]{2,1,0:T(8,128)(2,1)S(1)}, u32[]{:S(2)}, u32[]{:S(2)}) %collective-permute-start.42) | collective-permute-done | bytes 1376288 | tf_op jit(solution)/shard_map/ppermute | solution.py:988
  239.3 18.5 %attend_near.3 = (f32[512,768]{1,0:T(8,128)}, f32[512,128]{1,0:T(8,128)}, f32[512,128]{1,0:T(8,128)}) custom-call(s32[8]{0:T(128)} %stack.146.idx, bf16[512,768]{1,0:T(8,128)(2,1)} %get-tuple-element.387.q, bf16[512,1536]{1,0:T(8,128)(2,1)} %gate.40.own, bf16[512,1536]{1,0:T(8,128)(2,1)} %get-tuple-element.388.near), custom_call_target="tpu_custom_call" | custom-call | flops 1000 | bytes 1000 | tf_op jit(solution)/shard_map/attend_near/pallas_call | solution.py:140
  275.4 8.4 %attend_far.3 = (bf16[512,768]{1,0:T(8,128)(2,1)}, f32[12,1,512]{2,1,0:T(1,128)}) custom-call(s32[8]{0:T(128)} %stack.146.idx, bf16[512,768]{1,0:T(8,128)(2,1)} %get-tuple-element.387.q, bf16[512,1536]{1,0:T(8,128)(2,1)} %get-tuple-element.394.far, bf16[512,1536]{1,0:T(8,128)(2,1)} %copy-done.34, f32[512,768]{1,0:T(8,128)} %get-tuple-element.395.acc, ...), custom_call_target="tpu_custom_call" | custom-call | flops 1000 | bytes 1000 | tf_op jit(solution)/shard_map/attend_far/pallas_call | solution.py:140
  298.0 20.1 %feed.3 = (f32[512,768]{1,0:T(8,128)}, f32[512,768]{1,0:T(8,128)}, bf16[512,768]{1,0:T(8,128)(2,1)}, bf16[4,512,768]{2,1,0:T(8,128)(2,1)}, bf16[4,512,768]{2,1,0:T(8,128)(2,1)}) custom-call(s32[8]{0:T(128)} %stack.146.idx, f32[512,768]{1,0:T(8,128)} %get-tuple-element.378.x, bf16[512,768]{1,0:T(8,128)(2,1)} %get-tuple-element.405.o, ...), custom_call_target="tpu_custom_call" | custom-call | flops 1000 | bytes 1000 | tf_op jit(solution)/shard_map/feed/pallas_call | solution.py:140
  322.7 18.4 %feed_back.2 = (bf16[512,768]{1,0:T(8,128)(2,1)}, bf16[4,512,768]{2,1,0:T(8,128)(2,1)}, f32[512,768]{1,0:T(8,128)}, bf16[512,768]{1,0:T(8,128)(2,1)}, bf16[512,768]{1,0:T(8,128)(2,1)}, /*index=5*/f32[8,768]{1,0:T(8,128)}) custom-call(s32[8]{0:T(128)} %stack.146.idx, f32[512,768]{1,0:T(8,128)} %maximum_convert_fusion.1.e, f32[512,768]{1,0:T(8,128)} %get-tuple-element.410.x1, ...), custom_call_target="tpu_custom_call" | custom-call | flops 1000 | bytes 1000 | tf_op jit(solution)/shard_map/feed_back/pallas_call | solution.py:140
  341.1 11.6 %feed_grads.2 = (bf16[4,4,224,768]{3,2,1,0:T(8,128)(2,1)}, bf16[4,4,224,768]{3,2,1,0:T(8,128)(2,1)}) custom-call(s32[8]{0:T(128)} %stack.146.idx, bf16[4,512,768]{2,1,0:T(8,128)(2,1)} %get-tuple-element.414.g, bf16[512,768]{1,0:T(8,128)(2,1)} %get-tuple-element.415.dm, bf16[512,768]{1,0:T(8,128)(2,1)} %get-tuple-element.416.h2, ...), custom_call_target="tpu_custom_call" | custom-call | flops 1000 | bytes 1000 | tf_op jit(solution)/shard_map/feed_grads/pallas_call | solution.py:140
  356.8 11.3 %attend_back_far.2 = (f32[512,768]{1,0:T(8,128)}, bf16[512,1536]{1,0:T(8,128)(2,1)}, f32[12,1,512]{2,1,0:T(1,128)}) custom-call(s32[8]{0:T(128)} %stack.146.idx, bf16[512,768]{1,0:T(8,128)(2,1)} %get-tuple-element.387.q, bf16[512,768]{1,0:T(8,128)(2,1)} %get-tuple-element.423.do, bf16[512,768]{1,0:T(8,128)(2,1)} %get-tuple-element.405.o, ...), custom_call_target="tpu_custom_call" | custom-call | flops 1000 | bytes 1000 | tf_op jit(solution)/shard_map/attend_back_far/pallas_call | solution.py:140
  377.3 22.5 %attend_back_near.2 = (f32[512,768]{1,0:T(8,128)}, bf16[512,1536]{1,0:T(8,128)(2,1)}, bf16[512,1536]{1,0:T(8,128)(2,1)}) custom-call(s32[8]{0:T(128)} %stack.146.idx, bf16[512,768]{1,0:T(8,128)(2,1)} %get-tuple-element.387.q, bf16[512,768]{1,0:T(8,128)(2,1)} %get-tuple-element.423.do, f32[12,1,512]{2,1,0:T(1,128)} %get-tuple-element.424.lse, ...), custom_call_target="tpu_custom_call" | custom-call | flops 1000 | bytes 1000 | tf_op jit(solution)/shard_map/attend_back_near/pallas_call | solution.py:140
  415.0 14.5 %project_back.2 = (bf16[4,512,576]{2,1,0:T(8,128)(2,1)}, f32[512,768]{1,0:T(8,128)}, f32[8,768]{1,0:T(8,128)}) custom-call(s32[8]{0:T(128)} %stack.146.idx, f32[512,768]{1,0:T(8,128)} %get-tuple-element.431.dq, bf16[512,1536]{1,0:T(8,128)(2,1)} %get-tuple-element.432.dn, bf16[512,1536]{1,0:T(8,128)(2,1)} %get-tuple-element.437.dcr, ...), custom_call_target="tpu_custom_call" | custom-call | flops 1000 | bytes 1000 | tf_op jit(solution)/shard_map/project_back/pallas_call | solution.py:140
  443.5 18.5 %feed_back.3 = (bf16[512,768]{1,0:T(8,128)(2,1)}, bf16[4,512,768]{2,1,0:T(8,128)(2,1)}, f32[512,768]{1,0:T(8,128)}, bf16[512,768]{1,0:T(8,128)(2,1)}, bf16[512,768]{1,0:T(8,128)(2,1)}, /*index=5*/f32[8,768]{1,0:T(8,128)}) custom-call(s32[8]{0:T(128)} %stack.146.idx, f32[512,768]{1,0:T(8,128)} %get-tuple-element.450.e, f32[512,768]{1,0:T(8,128)} %get-tuple-element.451.x1, ...), custom_call_target="tpu_custom_call" | custom-call | flops 1000 | bytes 1000 | tf_op jit(solution)/shard_map/feed_back/pallas_call | solution.py:140
  469.8 11.6 %feed_grads.3 = (bf16[4,4,224,768]{3,2,1,0:T(8,128)(2,1)}, bf16[4,4,224,768]{3,2,1,0:T(8,128)(2,1)}) custom-call(s32[8]{0:T(128)} %stack.146.idx, bf16[4,512,768]{2,1,0:T(8,128)(2,1)} %get-tuple-element.466.g, bf16[512,768]{1,0:T(8,128)(2,1)} %get-tuple-element.467.dm, bf16[512,768]{1,0:T(8,128)(2,1)} %get-tuple-element.468.h2, ...), custom_call_target="tpu_custom_call" | custom-call | flops 1000 | bytes 1000 | tf_op jit(solution)/shard_map/feed_grads/pallas_call | solution.py:140
  491.9 11.3 %attend_back_far.3 = (f32[512,768]{1,0:T(8,128)}, bf16[512,1536]{1,0:T(8,128)(2,1)}, f32[12,1,512]{2,1,0:T(1,128)}) custom-call(s32[8]{0:T(128)} %stack.146.idx, bf16[512,768]{1,0:T(8,128)(2,1)} %get-tuple-element.339.q, bf16[512,768]{1,0:T(8,128)(2,1)} %get-tuple-element.473.do, bf16[512,768]{1,0:T(8,128)(2,1)} %get-tuple-element.368.o, ...), custom_call_target="tpu_custom_call" | custom-call | flops 1000 | bytes 1000 | tf_op jit(solution)/shard_map/attend_back_far/pallas_call | solution.py:140
  515.8 22.5 %attend_back_near.3 = (f32[512,768]{1,0:T(8,128)}, bf16[512,1536]{1,0:T(8,128)(2,1)}, bf16[512,1536]{1,0:T(8,128)(2,1)}) custom-call(s32[8]{0:T(128)} %stack.146.idx, bf16[512,768]{1,0:T(8,128)(2,1)} %get-tuple-element.339.q, bf16[512,768]{1,0:T(8,128)(2,1)} %get-tuple-element.473.do, f32[12,1,512]{2,1,0:T(1,128)} %get-tuple-element.474.lse, ...), custom_call_target="tpu_custom_call" | custom-call | flops 1000 | bytes 1000 | tf_op jit(solution)/shard_map/attend_back_near/pallas_call | solution.py:140
  551.9 14.4 %project_back.3 = (bf16[4,512,576]{2,1,0:T(8,128)(2,1)}, f32[512,768]{1,0:T(8,128)}, f32[8,768]{1,0:T(8,128)}) custom-call(s32[8]{0:T(128)} %stack.146.idx, f32[512,768]{1,0:T(8,128)} %get-tuple-element.487.dq, bf16[512,1536]{1,0:T(8,128)(2,1)} %get-tuple-element.488.dn, bf16[512,1536]{1,0:T(8,128)(2,1)} %get-tuple-element.497.dcr, ...), custom_call_target="tpu_custom_call" | custom-call | flops 1000 | bytes 1000 | tf_op jit(solution)/shard_map/project_back/pallas_call | solution.py:140
  601.2 13.9 %collective-permute-done.87.refs_4_ = bf16[2,224,768]{2,1,0:T(8,128)(2,1)S(1)} collective-permute-done((bf16[2,224,768]{2,1,0:T(8,128)(2,1)S(1)}, bf16[2,224,768]{2,1,0:T(8,128)(2,1)S(1)}, u32[]{:S(2)}, u32[]{:S(2)}) %collective-permute-start.87) | collective-permute-done | bytes 688160 | tf_op jit(solution)/shard_map/ppermute | solution.py:984
  647.5 10.3 %collective-permute-done.98.refs_4_ = bf16[224,768]{1,0:T(8,128)(2,1)S(1)} collective-permute-done((bf16[224,768]{1,0:T(8,128)(2,1)}, bf16[224,768]{1,0:T(8,128)(2,1)S(1)}, u32[]{:S(2)}, u32[]{:S(2)}) %collective-permute-start.98) | collective-permute-done | bytes 344096 | tf_op jit(solution)/shard_map/ppermute | solution.py:984
  660.3 9.7 %collective-permute-start.102 = (f32[32,768]{1,0:T(8,128)S(1)}, f32[32,768]{1,0:T(8,128)S(1)}, u32[]{:S(2)}, u32[]{:S(2)}) collective-permute-start(f32[32,768]{1,0:T(8,128)S(1)} %add.253.refs_5_), channel_id=1, source_target_pairs={{0,2},{1,3},{2,0},{3,1},{4,6},{5,7},{6,4},{7,5},{8,10},{9,11},{10,... | collective-permute-start | bytes 294920 | tf_op jit(solution)/shard_map/ppermute | solution.py:984
  (709 shorter events, 376.9 us)
Async XLA Ops:
  68.1 34.6 %collective-permute-start.16 = (bf16[512,1536]{1,0:T(8,128)(2,1)}, bf16[512,1536]{1,0:T(8,128)(2,1)}, u32[]{:S(2)}, u32[]{:S(2)}) collective-permute-start(bf16[512,1536]{1,0:T(8,128)(2,1)} %gate.34.own), channel_id=1, source_target_pairs={{4,0},{12,8},{20,16},{28,24},{5,1},{13,9},{21,17},{29,25},{6,2},{1... | collective-permute-start | bytes 4718600 | tf_op jit(solution)/shard_map/ppermute | solution.py:1107
  73.3 29.4 %collective-permute-start.17 = (bf16[224,768]{1,0:T(8,128)(2,1)S(1)}, bf16[224,768]{1,0:T(8,128)(2,1)S(1)}, u32[]{:S(2)}, u32[]{:S(2)}) collective-permute-start(bf16[224,768]{1,0:T(8,128)(2,1)S(1)} %copy-done.44), channel_id=1, source_target_pairs={{0,2},{1,3},{2,0},{3,1},{4,6},{5,7},{6,4},{7,5},{8,10},{9,11},{10,... | collective-permute-start | bytes 1032200 | tf_op jit(solution)/shard_map/ppermute | solution.py:984
  74.0 49.5 %collective-permute-start.20 = (bf16[512,1536]{1,0:T(8,128)(2,1)}, bf16[512,1536]{1,0:T(8,128)(2,1)S(1)}, u32[]{:S(2)}, u32[]{:S(2)}) collective-permute-start(bf16[512,1536]{1,0:T(8,128)(2,1)} %gate.34.own), channel_id=1, source_target_pairs={{4,5},{5,4},{6,7},{7,6},{12,13},{13,12},{14,15},{15,14},{20,21},{2... | collective-permute-start | bytes 4718600 | tf_op jit(solution)/shard_map/ppermute | solution.py:1102
  146.3 27.9 %collective-permute-start.28 = (bf16[4,224,768]{2,1,0:T(8,128)(2,1)}, bf16[4,224,768]{2,1,0:T(8,128)(2,1)S(1)}, u32[]{:S(2)}, u32[]{:S(2)}) collective-permute-start(bf16[4,224,768]{2,1,0:T(8,128)(2,1)} %get-tuple-element.360.rest_0_), channel_id=1, source_target_pairs={{0,4},{4,0},{8,12},{12,8},{16,20},{20,16},{24,28},{28,24},{1,5},{5... | collective-permute-start | bytes 4128776 | tf_op jit(solution)/shard_map/ppermute | solution.py:980
  146.8 27.4 %collective-permute-start.30 = (bf16[4,224,768]{2,1,0:T(8,128)(2,1)}, bf16[4,224,768]{2,1,0:T(8,128)(2,1)S(1)}, u32[]{:S(2)}, u32[]{:S(2)}) collective-permute-start(bf16[4,224,768]{2,1,0:T(8,128)(2,1)} %get-tuple-element.361.rest_2_), channel_id=1, source_target_pairs={{0,4},{4,0},{8,12},{12,8},{16,20},{20,16},{24,28},{28,24},{1,5},{5... | collective-permute-start | bytes 4128776 | tf_op jit(solution)/shard_map/ppermute | solution.py:980
  146.8 28.2 %collective-permute-start.29 = (bf16[4,224,768]{2,1,0:T(8,128)(2,1)}, bf16[4,224,768]{2,1,0:T(8,128)(2,1)}, u32[]{:S(2)}, u32[]{:S(2)}) collective-permute-start(bf16[4,224,768]{2,1,0:T(8,128)(2,1)} %get-tuple-element.359.rest_1_), channel_id=1, source_target_pairs={{0,4},{4,0},{8,12},{12,8},{16,20},{20,16},{24,28},{28,24},{1,5},{5... | collective-permute-start | bytes 4128776 | tf_op jit(solution)/shard_map/ppermute | solution.py:980
  147.3 27.7 %collective-permute-start.27 = (bf16[4,224,768]{2,1,0:T(8,128)(2,1)}, bf16[4,224,768]{2,1,0:T(8,128)(2,1)}, u32[]{:S(2)}, u32[]{:S(2)}) collective-permute-start(bf16[4,224,768]{2,1,0:T(8,128)(2,1)} %get-tuple-element.359.rest_1_), channel_id=1, source_target_pairs={{0,16},{4,12},{8,24},{12,4},{16,0},{20,28},{24,8},{28,20},{1,17},{... | collective-permute-start | bytes 4128776 | tf_op jit(solution)/shard_map/ppermute | solution.py:992
  178.7 24.3 %collective-permute-start.36 = (bf16[2,224,768]{2,1,0:T(8,128)(2,1)S(1)}, bf16[2,224,768]{2,1,0:T(8,128)(2,1)S(1)}, u32[]{:S(2)}, u32[]{:S(2)}) collective-permute-start(bf16[2,224,768]{2,1,0:T(8,128)(2,1)S(1)} %pad_maximum_fusion.3.refs_5_), channel_id=1, source_target_pairs={{0,1},{1,0},{2,3},{3,2},{4,5},{5,4},{6,7},{7,6},{8,9},{9,8},{10,11... | collective-permute-start | bytes 2064392 | tf_op jit(solution)/shard_map/ppermute | solution.py:984
  178.8 24.1 %collective-permute-start.34 = (bf16[4,96,576]{2,1,0:T(8,128)(2,1)}, bf16[4,96,576]{2,1,0:T(8,128)(2,1)S(1)}, u32[]{:S(2)}, u32[]{:S(2)}) collective-permute-start(bf16[4,96,576]{2,1,0:T(8,128)(2,1)} %get-tuple-element.374.refs_1_), channel_id=1, source_target_pairs={{0,16},{4,12},{8,24},{12,4},{16,0},{20,28},{24,8},{28,20},{1,17},{... | collective-permute-start | bytes 1327112 | tf_op jit(solution)/shard_map/ppermute | solution.py:992
  179.8 23.1 %collective-permute-start.35 = (bf16[4,96,576]{2,1,0:T(8,128)(2,1)}, bf16[4,96,576]{2,1,0:T(8,128)(2,1)S(1)}, u32[]{:S(2)}, u32[]{:S(2)}) collective-permute-start(bf16[4,96,576]{2,1,0:T(8,128)(2,1)} %get-tuple-element.375.refs_2_), channel_id=1, source_target_pairs={{0,16},{4,12},{8,24},{12,4},{16,0},{20,28},{24,8},{28,20},{1,17},{... | collective-permute-start | bytes 1327112 | tf_op jit(solution)/shard_map/ppermute | solution.py:992
  220.5 37.4 %collective-permute-start.43 = (bf16[512,1536]{1,0:T(8,128)(2,1)}, bf16[512,1536]{1,0:T(8,128)(2,1)}, u32[]{:S(2)}, u32[]{:S(2)}) collective-permute-start(bf16[512,1536]{1,0:T(8,128)(2,1)} %gate.40.own), channel_id=1, source_target_pairs={{4,5},{5,4},{6,7},{7,6},{12,13},{13,12},{14,15},{15,14},{20,21},{2... | collective-permute-start | bytes 4718600 | tf_op jit(solution)/shard_map/ppermute | solution.py:1102
  263.6 20.2 %collective-permute-start.47 = (bf16[4,224,768]{2,1,0:T(8,128)(2,1)S(1)}, bf16[4,224,768]{2,1,0:T(8,128)(2,1)S(1)}, u32[]{:S(2)}, u32[]{:S(2)}) collective-permute-start(bf16[4,224,768]{2,1,0:T(8,128)(2,1)S(1)} %copy-done.4), channel_id=1, source_target_pairs={{0,4},{4,0},{8,12},{12,8},{16,20},{20,16},{24,28},{28,24},{1,5},{5... | collective-permute-start | bytes 4128776 | tf_op jit(solution)/shard_map/ppermute | solution.py:980
  319.7 33.0 %collective-permute-start.54 = (bf16[256,768]{1,0:T(8,128)(2,1)S(1)}, bf16[256,768]{1,0:T(8,128)(2,1)S(1)}, u32[]{:S(2)}, u32[]{:S(2)}) collective-permute-start(bf16[256,768]{1,0:T(8,128)(2,1)S(1)} %get-tuple-element.658), channel_id=1, source_target_pairs={{0,1},{1,0},{2,5},{3,4},{4,3},{5,2},{6,7},{7,6},{8,9},{9,8},{10,13... | collective-permute-start | bytes 1179656 | tf_op jit(solution)/shard_map/ppermute | solution.py:1097
  320.5 32.2 %collective-permute-start.53 = (bf16[256,768]{1,0:T(8,128)(2,1)S(1)}, bf16[256,768]{1,0:T(8,128)(2,1)S(1)}, u32[]{:S(2)}, u32[]{:S(2)}) collective-permute-start(bf16[256,768]{1,0:T(8,128)(2,1)S(1)} %get-tuple-element.659), channel_id=1, source_target_pairs={{0,0},{1,1},{2,4},{3,5},{4,2},{5,3},{6,6},{7,7},{8,8},{9,9},{10,12... | collective-permute-start | bytes 1179656 | tf_op jit(solution)/shard_map/ppermute | solution.py:1097
  373.9 33.1 %collective-permute-start.58 = (bf16[2,4,224,768]{3,2,1,0:T(8,128)(2,1)S(1)}, bf16[2,4,224,768]{3,2,1,0:T(8,128)(2,1)S(1)}, u32[]{:S(2)}, u32[]{:S(2)}) collective-permute-start(bf16[2,4,224,768]{3,2,1,0:T(8,128)(2,1)S(1)} %add_convert_fusion.1), channel_id=1, source_target_pairs={{0,8},{4,20},{8,0},{12,28},{16,24},{20,4},{24,16},{28,12},{1,9},{5... | collective-permute-start | bytes 8257544 | tf_op jit(solution)/shard_map/ppermute | solution.py:988
  375.5 31.6 %collective-permute-start.57 = (bf16[512,1536]{1,0:T(8,128)(2,1)S(1)}, bf16[512,1536]{1,0:T(8,128)(2,1)}, u32[]{:S(2)}, u32[]{:S(2)}) collective-permute-start(bf16[512,1536]{1,0:T(8,128)(2,1)S(1)} %add_convert_fusion.3), channel_id=1, source_target_pairs={{4,5},{5,4},{6,7},{7,6},{12,13},{13,12},{14,15},{15,14},{20,21},{2... | collective-permute-start | bytes 4718600 | tf_op jit(solution)/shard_map/ppermute | solution.py:1102
  438.2 23.9 %collective-permute-start.62 = (bf16[4,4,96,576]{3,2,1,0:T(8,128)(2,1)}, bf16[4,4,96,576]{3,2,1,0:T(8,128)(2,1)S(1)}, u32[]{:S(2)}, u32[]{:S(2)}) collective-permute-start(bf16[4,4,96,576]{3,2,1,0:T(8,128)(2,1)} %get-tuple-element.460), channel_id=1, source_target_pairs={{0,4},{4,0},{8,12},{12,8},{16,20},{20,16},{24,28},{28,24},{1,5},{5... | collective-permute-start | bytes 5308424 | tf_op jit(solution)/shard_map/ppermute | solution.py:980
  441.6 20.4 %collective-permute-start.61 = (bf16[2,224,768]{2,1,0:T(8,128)(2,1)S(1)}, bf16[2,224,768]{2,1,0:T(8,128)(2,1)S(1)}, u32[]{:S(2)}, u32[]{:S(2)}) collective-permute-start(bf16[2,224,768]{2,1,0:T(8,128)(2,1)S(1)} %slice.484), channel_id=1, source_target_pairs={{0,1},{1,0},{2,3},{3,2},{4,5},{5,4},{6,7},{7,6},{8,9},{9,8},{10,11... | collective-permute-start | bytes 2064392 | tf_op jit(solution)/shard_map/ppermute | solution.py:984
  509.4 33.1 %collective-permute-start.70 = (bf16[2,4,224,768]{3,2,1,0:T(8,128)(2,1)S(1)}, bf16[2,4,224,768]{3,2,1,0:T(8,128)(2,1)S(1)}, u32[]{:S(2)}, u32[]{:S(2)}) collective-permute-start(bf16[2,4,224,768]{3,2,1,0:T(8,128)(2,1)S(1)} %add_convert_fusion), channel_id=1, source_target_pairs={{0,8},{4,20},{8,0},{12,28},{16,24},{20,4},{24,16},{28,12},{1,9},{5... | collective-permute-start | bytes 8257544 | tf_op jit(solution)/shard_map/ppermute | solution.py:988
  512.4 30.1 %collective-permute-start.69 = (bf16[512,1536]{1,0:T(8,128)(2,1)}, bf16[512,1536]{1,0:T(8,128)(2,1)}, u32[]{:S(2)}, u32[]{:S(2)}) collective-permute-start(bf16[512,1536]{1,0:T(8,128)(2,1)} %add_convert_fusion.2), channel_id=1, source_target_pairs={{4,5},{5,4},{6,7},{7,6},{12,13},{13,12},{14,15},{15,14},{20,21},{2... | collective-permute-start | bytes 4718600 | tf_op jit(solution)/shard_map/ppermute | solution.py:1102
  515.7 22.6 %collective-permute-start.71 = (bf16[2,96,576]{2,1,0:T(8,128)(2,1)S(1)}, bf16[2,96,576]{2,1,0:T(8,128)(2,1)S(1)}, u32[]{:S(2)}, u32[]{:S(2)}) collective-permute-start(bf16[2,96,576]{2,1,0:T(8,128)(2,1)S(1)} %slice.485), channel_id=1, source_target_pairs={{0,1},{1,0},{2,3},{3,2},{4,5},{5,4},{6,7},{7,6},{8,9},{9,8},{10,11... | collective-permute-start | bytes 663560 | tf_op jit(solution)/shard_map/ppermute | solution.py:984
  592.5 25.7 %collective-permute-start.86 = (bf16[2,4,96,576]{3,2,1,0:T(8,128)(2,1)S(1)}, bf16[2,4,96,576]{3,2,1,0:T(8,128)(2,1)S(1)}, u32[]{:S(2)}, u32[]{:S(2)}) collective-permute-start(bf16[2,4,96,576]{3,2,1,0:T(8,128)(2,1)S(1)} %add_convert_fusion.6), channel_id=1, source_target_pairs={{0,8},{4,20},{8,0},{12,28},{16,24},{20,4},{24,16},{28,12},{1,9},{5... | collective-permute-start | bytes 2654216 | tf_op jit(solution)/shard_map/ppermute | solution.py:988
  627.6 30.3 %collective-permute-start.98 = (bf16[224,768]{1,0:T(8,128)(2,1)}, bf16[224,768]{1,0:T(8,128)(2,1)S(1)}, u32[]{:S(2)}, u32[]{:S(2)}) collective-permute-start(bf16[224,768]{1,0:T(8,128)(2,1)} %fusion.11), channel_id=1, source_target_pairs={{0,2},{1,3},{2,0},{3,1},{4,6},{5,7},{6,4},{7,5},{8,10},{9,11},{10,... | collective-permute-start | bytes 1032200 | tf_op jit(solution)/shard_map/ppermute | solution.py:984
  636.6 21.2 %collective-permute-start.97 = (bf16[2,96,576]{2,1,0:T(8,128)(2,1)S(1)}, bf16[2,96,576]{2,1,0:T(8,128)(2,1)S(1)}, u32[]{:S(2)}, u32[]{:S(2)}) collective-permute-start(bf16[2,96,576]{2,1,0:T(8,128)(2,1)S(1)} %slice.489), channel_id=1, source_target_pairs={{0,1},{1,0},{2,3},{3,2},{4,5},{5,4},{6,7},{7,6},{8,9},{9,8},{10,11... | collective-permute-start | bytes 663560 | tf_op jit(solution)/shard_map/ppermute | solution.py:984
  (257 other events, 1730.6 us)

commit v3 on v2

--- a/solution.py
+++ b/solution.py
@@ -1073,9 +1073,33 @@
     return total, near, flip_narrow(added(total[1], near[1]), 2)
 
 
+def both_axes(x):
+    return flip_wide(x, 6)
+
+
+def gather_plane(own):
+    return [own, first_axis(own), second_axis(own), both_axes(own)]
+
+
 def spread_first(parts):
     total, near, far = parts
     return gather_first(added(total[0], near[0], far))
+
+
+def reduce_plane(pair):
+    keep, got = pair
+    moves = (second_axis, first_axis, both_axes)
+    return [keep, got] + [move(added(keep[i + 1], got[i + 1])) for i, move in enumerate(moves)]
+
+
+def reduce_narrow(parts):
+    keep, got, *others = parts
+    total = added(keep[0], got[0], *others)
+    bit = 8
+    while bit < lax.axis_size("wide"):
+        total = added(total, flip_wide(total, bit))
+        bit *= 2
+    return [total] + [flip_narrow(total[i], ORDER[i]) for i in range(1, QUARTERS)]
 
 
 def device_pairs(move):
@@ -1145,8 +1169,7 @@
 
     def bias_of(layer, start, size):
         at = width * layer + start
-        by_flip = dict(zip(ORDER, biases))
-        return jnp.stack([by_flip[k][at : at + size] for k in range(QUARTERS)])[:, None]
+        return jnp.stack([b[at : at + size] for b in biases])[:, None]
 
     def mixer_piece(layer):
         return lax.dynamic_slice_in_dim(mixer_weight[layer], w8 * PIECE, PIECE, 0).reshape(PIECE, PARTS)
@@ -1163,21 +1186,23 @@
 
     mixer0 = gather_direct(mixer_piece(0))
     feed0, feed1 = pack(idx, up_weight, down_weight, output_weight)
+    biases = [biases] + [flip_narrow(biases, k) for k in (1, 2, 3)]
     mixer0, tokens, feed0, biases = gate((mixer0, tokens, feed0, biases))
     mixer0 = gather_first(whole(mixer0))
     rows = relocate(tokens)
-    mixer0, feed0, biases, mixer1 = gate((mixer0, feed0, biases, mixer_piece(1)))
+    mixer0, feed0 = gate((mixer0, feed0))
     own, first = mixer0
     mixer0 = [own, first, second_axis(own), second_axis(first)]
-    feed0, biases = gather_direct(feed0), gather_direct(biases)
-    mixer0, rows, biases = gate((mixer0, rows, biases))
+    feed0 = gather_far(feed0)
+    mixer0, rows, feed0 = gate((mixer0, rows, feed0))
     mixer0 = gather_last(mixer0)
+    feed0 = gather_near(feed0)
     x0 = jnp.concatenate(rows).astype(F32)
     h1_0, q_0, kv = run_project(0, x0, mixer0)
-    own_0 = gate(kv)
+    own_0, feed0 = gate((kv, feed0))
     near_0, far = within_chip(own_0, 1), between_chips(own_0)
-    near_0, q_0, feed0, mixer1 = gate((near_0, q_0, feed0, mixer1))
     own, first = gather_first(whole(feed0))
+    mixer1 = mixer_piece(1)
     state = attend_near(idx, q_0, own_0, near_0)
     state, far_0, own, first, mixer1, feed1 = gate((state, far, own, first, mixer1, feed1))
     far_near_0 = within_chip(far_0, 1)
@@ -1187,29 +1212,29 @@
     o_0, own, first, second, mixer1, feed1 = gate((o_0, own, first, second, mixer1, feed1))
     third = second_axis(first)
     others = [flip_wide(own, 1), flip_wide(first, 1), flip_wide(second, 1)]
-    mixer1, feed1 = gather_first(whole(mixer1)), gather_far(feed1)
+    feed1 = gather_far(feed1)
     third, others, o_0, mixer1, feed1 = gate((third, others, o_0, mixer1, feed1))
     feed0 = [own, first, second, third] + others + [flip_wide(third, 1)]
-    mixer1, feed1 = gather_second(mixer1), gather_near(feed1)
+    mixer1, feed1 = gather_plane(whole(mixer1)), gather_near(feed1)
     x1, x1_0, h2_0, g_0, gp_0 = run_feed(0, x0, o_0, feed0)
     x1, mixer1, feed1 = gate((x1, mixer1, feed1))
     mixer1 = gather_last(mixer1)
     own, first = gather_first(whole(feed1))
     h1_1, q_1, kv = run_project(1, x1, mixer1)
-    own_1 = gate(kv)
+    own_1, own, first = gate((kv, own, first))
     near_1, far = within_chip(own_1, 1), between_chips(own_1)
-    near_1, q_1, own, first = gate((near_1, q_1, own, first))
     second = second_axis(own)
     state = attend_near(idx, q_1, own_1, near_1)
-    state, far_1, own, first, second, cotangent = gate((state, far, own, first, second, cotangent))
+    state, far_1, own, first, second = gate((state, far, own, first, second))
     far_near_1 = within_chip(far_1, 1)
     third = second_axis(first)
     others = [flip_wide(own, 1), flip_wide(first, 1), flip_wide(second, 1)]
+    o_1, lse_1 = attend_far(idx, q_1, far_1, far_near_1, state)
+    o_1, third, others, cotangent = gate((o_1, third, others, cotangent))
     e = relocate(cotangent)
-    o_1, lse_1 = attend_far(idx, q_1, far_1, far_near_1, state)
-    o_1, third, others, e = gate((o_1, third, others, e))
     feed1 = [own, first, second, third] + others + [flip_wide(third, 1)]
     x2, x1_1, h2_1, g_1, gp_1 = run_feed(1, x1, o_1, feed1)
+    x2, e = gate((x2, e))
     x_out = relocate(x2.astype(BF))
 
     e = jnp.concatenate(e).astype(F32)
@@ -1235,60 +1260,71 @@
     g_mixer1 = reduce_core(g_mixer1)
     dm, dz, e1, da, do, small_feed0 = feed_back(idx, e, x1_0, gp_0, norm_gain[0, 1:2], feed0)
     dm, do, g_feed1, g_mixer1 = gate((dm, do, g_feed1, g_mixer1))
-    g_feed1, g_mixer1 = reduce_far(g_feed1), reduce_first(g_mixer1)
+    g_feed1, g_mixer1 = reduce_far(g_feed1), reduce_plane(g_mixer1)
     g_feed0 = feed_grads(idx, g_0, dm, h2_0, dz, o_0, da)
     do, g_feed1, g_mixer1, g_feed0 = gate((do, g_feed1, g_mixer1, g_feed0))
-    g_feed1, g_mixer1, g_feed0 = spread_first(g_feed1), reduce_second(g_mixer1), reduce_core(g_feed0)
+    g_mixer1, g_feed0 = reduce_narrow(g_mixer1), reduce_core(g_feed0)
+    g_feed1 = spread_first(g_feed1)
     dq, dr, drow = attend_back_far(idx, q_0, do, o_0, lse_0, far_0, far_near_0)
     dr, dq, g_feed1, g_mixer1, g_feed0 = gate((dr, dq, g_feed1, g_mixer1, g_feed0))
     far = between_chips(added(dr, within_chip(dr, 0)))
-    g_feed0, g_mixer1 = reduce_first(g_feed0), reduce_near(g_mixer1)
+    g_feed0, g_feed1 = reduce_first(g_feed0), gather_second(g_feed1)
     dq, dn, dc = attend_back_near(idx, q_0, do, lse_0, drow, dq, own_0, near_0)
-    dc, far, g_feed0, g_mixer1 = gate((dc, far, g_feed0, g_mixer1))
+    dc, far, g_feed0, g_feed1 = gate((dc, far, g_feed0, g_feed1))
     got = within_chip(dc, 0)
-    g_feed0, g_mixer1 = reduce_second(g_feed0), reduce_far(g_mixer1)
+    g_feed0 = reduce_second(g_feed0)
+    total, *others = g_mixer1
+    g_mixer1 = gather_first(added(total[0], *others))
     dpz, e, small_mixer0 = project_back(
         idx, dq, dn, dc, got, far, cosine, sine, x0, e1, norm_gain[0, 0:1], mixer0
     )
-    dpz, g_feed0, g_feed1, g_mixer1 = gate((dpz, g_feed0, g_feed1, g_mixer1))
-    g_feed0, g_feed1, g_mixer1 = reduce_near(g_feed0), gather_second(g_feed1), spread_first(g_mixer1)
+    e, dpz, g_feed0, g_mixer1 = gate((e, dpz, g_feed0, g_mixer1))
+    g_feed0 = reduce_near(g_feed0)
     g_mixer0 = project_grads(idx, h1_0, dpz)
     smalls = jnp.concatenate([small_feed0, small_mixer0, small_feed1, small_mixer1])
-    e, g_mixer0, g_feed1, g_mixer1, smalls = gate((e, g_mixer0, g_feed1, g_mixer1, smalls))
+    g_mixer0, smalls, g_feed0, g_feed1, g_mixer1, e = gate((g_mixer0, smalls, g_feed0, g_feed1, g_mixer1, e))
     g_mixer0 = reduce_core(g_mixer0)
-    g_feed1, g_mixer1 = gather_last(g_feed1), gather_second(g_mixer1)
     smalls = smalls, flip_wide(smalls, 1)
-    g_mixer0, g_feed1, g_mixer1, smalls, e = gate((g_mixer0, g_feed1, g_mixer1, smalls, e))
-    g_mixer0, g_mixer1 = reduce_first(g_mixer0), gather_last(g_mixer1)
+    g_mixer0, smalls, e = gate((g_mixer0, smalls, e))
+    g_mixer0 = reduce_plane(g_mixer0)
     rows = relocate(e.astype(BF))
     smalls = smalls[0] + smalls[1]
     smalls = smalls, first_axis(smalls)
+    g_feed1 = gather_last(g_feed1)
     feed_out = finish_feed(idx, 1, layers, g_feed1, None)
-    g_mixer0, g_feed0, g_mixer1, smalls = gate((g_mixer0, g_feed0, g_mixer1, smalls))
-    g_mixer0, g_feed0 = reduce_second(g_mixer0), reduce_far(g_feed0)
+    g_mixer0, g_feed0, smalls, feed_out, rows, g_mixer1 = gate((g_mixer0, g_feed0, smalls, feed_out, rows, g_mixer1))
+    keep, got, *others = g_mixer0
+    total = added(keep[0], got[0], *others)
+    bit = 8
+    while bit < lax.axis_size("wide"):
+        total = added(total, flip_wide(total, bit))
+        bit *= 2
+    g_mixer0 = total, flip_narrow(total[2:], 1)
+    g_feed0 = reduce_far(g_feed0)
     smalls = smalls[0] + smalls[1]
     smalls = smalls, second_axis(smalls)
-    mixer_out = finish_mixer(idx, 1, layers, g_mixer1, None)
-    g_mixer0, smalls, rows = gate((g_mixer0, smalls, rows))
-    g_mixer0 = reduce_near(g_mixer0)
+    g_mixer1 = gather_second(g_mixer1)
+    g_mixer0, g_feed0, smalls, g_mixer1 = gate((g_mixer0, g_feed0, smalls, g_mixer1))
+    g_mixer0, g_feed0 = reduce_far(g_mixer0), spread_first(g_feed0)
     smalls = smalls[0] + smalls[1]
     bit = 8
     while bit < lax.axis_size("wide"):
         smalls = smalls + flip_wide(smalls, bit)
         bit *= 2
     smalls = smalls, flip_narrow(smalls, 1)
-    g_mixer0, g_feed0, smalls = gate((g_mixer0, g_feed0, smalls))
-    g_mixer0, g_feed0 = reduce_far(g_mixer0), spread_first(g_feed0)
+    g_mixer1 = gather_last(g_mixer1)
+    mixer_out = finish_mixer(idx, 1, layers, g_mixer1, None)
+    g_mixer0, g_feed0, smalls, mixer_out = gate((g_mixer0, g_feed0, smalls, mixer_out))
+    g_mixer0, g_feed0 = spread_first(g_mixer0), gather_second(g_feed0)
     smalls = smalls[0] + smalls[1]
     smalls = smalls, flip_narrow(smalls, 2)
     g_mixer0, g_feed0, smalls = gate((g_mixer0, g_feed0, smalls))
-    g_mixer0, g_feed0 = spread_first(g_mixer0), gather_second(g_feed0)
+    g_mixer0 = gather_second(g_mixer0)
     smalls = smalls[0] + smalls[1]
-    g_mixer0, g_feed0 = gate((g_mixer0, g_feed0))
-    g_mixer0, g_feed0 = gather_second(g_mixer0), gather_last(g_feed0)
-    g_mixer0, feed_out, g_feed0 = gate((g_mixer0, feed_out, g_feed0))
+    g_feed0 = gather_last(g_feed0)
+    feed_out = finish_feed(idx, 0, layers, g_feed0, feed_out)
+    g_mixer0, feed_out = gate((g_mixer0, feed_out))
     g_mixer0 = gather_last(g_mixer0)
-    feed_out = finish_feed(idx, 0, layers, g_feed0, feed_out)
     mixer_out = finish_mixer(idx, 0, layers, g_mixer0, mixer_out)
     tokens_grad = jnp.concatenate(rows)
     x_out = jnp.concatenate(x_out)

time: 737 us -> 695 us (0.943)
  waiting for transfers between devices: 167 us -> 140 us
  starting transfers between devices: 128 us -> 115 us
    ppermute x24, waiting for transfers between devices: 80.6 us -> 61.5 us  [flip_narrow(): return lax.ppermute(x, 'narrow', [(i, i ^ bit) for i in range(QUARTERS)])]
    ppermute x24, starting transfers between devices: 47.8 us -> 32.7 us  [flip_narrow(): return lax.ppermute(x, 'narrow', [(i, i ^ bit) for i in range(QUARTERS)])]
    ppermute x21 -> x20, waiting for transfers between devices: 25.6 us -> 17.2 us  [second_axis(): lax.ppermute(x, 'wide', [(i, i ^ (2 if i & 1 else 4)) for i in range(lax....]
    ppermute x38 -> x41, starting transfers between devices: 15.1 us -> 22.3 us  [flip_wide(): lax.ppermute(x, 'wide', [(i, i ^ bit) for i in range(lax.axis_size('wide'...]
    unnamed x336 -> x337, local copies, waits for them, and re-layouts: 49.3 us -> 53.3 us
    convert_element_type x22 -> x19, other arithmetic: 39.7 us -> 36.1 us  [added(): return functools.reduce(jnp.add, [t.astype(F32) for t in terms]).astype(BF)]
    ppermute x21 -> x20, starting transfers between devices: 22.7 us -> 21.4 us  [second_axis(): lax.ppermute(x, 'wide', [(i, i ^ (2 if i & 1 else 4)) for i in range(lax....]
  transfers between devices with their start and end apart: 116 -> 118, of which waited for: 34 -> 37; matrix products, arithmetic and copies ran while one was open for 9% -> 9% of each run, Pallas kernels for 34% -> 42%
where the time goes in v3:
time: 695 us; the launch traced here: 684 us
  Pallas kernels  295 us (42%)
  waiting for transfers between devices  140 us (20%)
  starting transfers between devices  115 us (17%)
  local copies, waits for them, and re-layouts  74.7 us (11%)
  other arithmetic  55.5 us (8%)
    pallas_call x25, Pallas kernels, kernel_call(): pl.pallas_call(body, in_specs=in_specs, out_specs=out_specs, out_shape=ou...  295 us
    ppermute x24, waiting for transfers between devices, flip_narrow(): return lax.ppermute(x, 'narrow', [(i, i ^ bit) for i in range(QUARTERS)])  61.5 us
    unnamed x337, local copies, waits for them, and re-layouts  53.3 us
    ppermute x13, waiting for transfers between devices, first_axis(): lax.ppermute(x, 'wide', [(i, i ^ (4 if i & 1 else 2)) for i in range(lax....  42.8 us
    convert_element_type x19, other arithmetic, added(): return functools.reduce(jnp.add, [t.astype(F32) for t in terms]).astype(BF)  36.1 us
    ppermute x24, starting transfers between devices, flip_narrow(): return lax.ppermute(x, 'narrow', [(i, i ^ bit) for i in range(QUARTERS)])  32.7 us
    ppermute x41, starting transfers between devices, flip_wide(): lax.ppermute(x, 'wide', [(i, i ^ bit) for i in range(lax.axis_size('wide'...  22.3 us
    ppermute x20, starting transfers between devices, second_axis(): lax.ppermute(x, 'wide', [(i, i ^ (2 if i & 1 else 4)) for i in range(lax....  21.4 us
  transfers between devices with their start and end apart: 118, of which 37 were waited for; matrix products, arithmetic and copies ran while one was open for 9% of the time, Pallas kernels for 42%

profile of v3, /device:TPU:0, one launch (start us, length us, event | category | flops | bytes accessed | tf_op | source)
XLA Modules:
  0.0 684.1 jit_solution(10312866424860930233)
XLA Ops:
  43.1 23.1 %collective-permute-done.12.refs_7_ = bf16[224,768]{1,0:T(8,128)(2,1)S(1)} collective-permute-done((bf16[224,768]{1,0:T(8,128)(2,1)}, bf16[224,768]{1,0:T(8,128)(2,1)S(1)}, u32[]{:S(2)}, u32[]{:S(2)}) %collective-permute-start.12) | collective-permute-done | bytes 344096 | tf_op jit(solution)/shard_map/ppermute | solution.py:984
  75.0 8.2 %project.2 = (bf16[512,768]{1,0:T(8,128)(2,1)}, bf16[512,768]{1,0:T(8,128)(2,1)}, bf16[512,1536]{1,0:T(8,128)(2,1)}) custom-call(s32[8]{0:T(128)} %stack.140.idx, f32[512,768]{1,0:T(8,128)} %maximum_convert_fusion.x, f32[1,768]{1,0:T(1,128)} %get-tuple-element.675.gain, f32[1,768]{1,0:T(1,128)} %get-tuple-element.655.shift, ...), custom_call_target="tpu_custom_call" | custom-call | flops 1000 | bytes 1000 | tf_op jit(solution)/shard_map/project/pallas_call | solution.py:140
  93.0 18.1 %attend_near.2 = (f32[512,768]{1,0:T(8,128)}, f32[512,128]{1,0:T(8,128)}, f32[512,128]{1,0:T(8,128)}) custom-call(s32[8]{0:T(128)} %stack.140.idx, bf16[512,768]{1,0:T(8,128)(2,1)} %get-tuple-element.315.q, bf16[512,1536]{1,0:T(8,128)(2,1)} %get-tuple-element.319.own, bf16[512,1536]{1,0:T(8,128)(2,1)} %collective-permute-done.18.near), custom_call_target="tpu_custom_call" | custom-call | flops 1000 | bytes 1000 | tf_op jit(solution)/shard_map/attend_near/pallas_call | solution.py:140
  120.9 8.4 %attend_far.2 = (bf16[512,768]{1,0:T(8,128)(2,1)}, f32[12,1,512]{2,1,0:T(1,128)}) custom-call(s32[8]{0:T(128)} %stack.140.idx, bf16[512,768]{1,0:T(8,128)(2,1)} %get-tuple-element.315.q, bf16[512,1536]{1,0:T(8,128)(2,1)} %get-tuple-element.326.far, bf16[512,1536]{1,0:T(8,128)(2,1)} %copy-done.29, f32[512,768]{1,0:T(8,128)} %get-tuple-element.327.acc, ...), custom_call_target="tpu_custom_call" | custom-call | flops 1000 | bytes 1000 | tf_op jit(solution)/shard_map/attend_far/pallas_call | solution.py:140
  137.8 15.3 %collective-permute-done.30.refs_10_ = bf16[224,768]{1,0:T(8,128)(2,1)S(1)} collective-permute-done((bf16[224,768]{1,0:T(8,128)(2,1)}, bf16[224,768]{1,0:T(8,128)(2,1)S(1)}, u32[]{:S(2)}, u32[]{:S(2)}) %collective-permute-start.30) | collective-permute-done | bytes 344096 | tf_op jit(solution)/shard_map/ppermute | solution.py:984
  166.4 20.0 %feed.2 = (f32[512,768]{1,0:T(8,128)}, f32[512,768]{1,0:T(8,128)}, bf16[512,768]{1,0:T(8,128)(2,1)}, bf16[4,512,768]{2,1,0:T(8,128)(2,1)}, bf16[4,512,768]{2,1,0:T(8,128)(2,1)}) custom-call(s32[8]{0:T(128)} %stack.140.idx, f32[512,768]{1,0:T(8,128)} %maximum_convert_fusion.x, bf16[512,768]{1,0:T(8,128)(2,1)} %get-tuple-element.344.o, ...), custom_call_target="tpu_custom_call" | custom-call | flops 1000 | bytes 1000 | tf_op jit(solution)/shard_map/feed/pallas_call | solution.py:140
  197.2 8.2 %project.3 = (bf16[512,768]{1,0:T(8,128)(2,1)}, bf16[512,768]{1,0:T(8,128)(2,1)}, bf16[512,1536]{1,0:T(8,128)(2,1)}) custom-call(s32[8]{0:T(128)} %stack.140.idx, f32[512,768]{1,0:T(8,128)} %get-tuple-element.356.x, f32[1,768]{1,0:T(1,128)} %get-tuple-element.674.gain, f32[1,768]{1,0:T(1,128)} %get-tuple-element.656.shift, ...), custom_call_target="tpu_custom_call" | custom-call | flops 1000 | bytes 1000 | tf_op jit(solution)/shard_map/project/pallas_call | solution.py:140
  217.1 18.5 %attend_near.3 = (f32[512,768]{1,0:T(8,128)}, f32[512,128]{1,0:T(8,128)}, f32[512,128]{1,0:T(8,128)}) custom-call(s32[8]{0:T(128)} %stack.140.idx, bf16[512,768]{1,0:T(8,128)(2,1)} %get-tuple-element.361.q, bf16[512,1536]{1,0:T(8,128)(2,1)} %get-tuple-element.365.own, bf16[512,1536]{1,0:T(8,128)(2,1)} %copy-done.30), custom_call_target="tpu_custom_call" | custom-call | flops 1000 | bytes 1000 | tf_op jit(solution)/shard_map/attend_near/pallas_call | solution.py:140
  244.7 8.4 %attend_far.3 = (bf16[512,768]{1,0:T(8,128)(2,1)}, f32[12,1,512]{2,1,0:T(1,128)}) custom-call(s32[8]{0:T(128)} %stack.140.idx, bf16[512,768]{1,0:T(8,128)(2,1)} %get-tuple-element.361.q, bf16[512,1536]{1,0:T(8,128)(2,1)} %get-tuple-element.371.far, bf16[512,1536]{1,0:T(8,128)(2,1)} %copy-done.31, f32[512,768]{1,0:T(8,128)} %get-tuple-element.372.acc, ...), custom_call_target="tpu_custom_call" | custom-call | flops 1000 | bytes 1000 | tf_op jit(solution)/shard_map/attend_far/pallas_call | solution.py:140
  264.6 20.0 %feed.3 = (f32[512,768]{1,0:T(8,128)}, f32[512,768]{1,0:T(8,128)}, bf16[512,768]{1,0:T(8,128)(2,1)}, bf16[4,512,768]{2,1,0:T(8,128)(2,1)}, bf16[4,512,768]{2,1,0:T(8,128)(2,1)}) custom-call(s32[8]{0:T(128)} %stack.140.idx, f32[512,768]{1,0:T(8,128)} %get-tuple-element.356.x, bf16[512,768]{1,0:T(8,128)(2,1)} %get-tuple-element.379.o, ...), custom_call_target="tpu_custom_call" | custom-call | flops 1000 | bytes 1000 | tf_op jit(solution)/shard_map/feed/pallas_call | solution.py:140
  290.3 18.5 %feed_back.2 = (bf16[512,768]{1,0:T(8,128)(2,1)}, bf16[4,512,768]{2,1,0:T(8,128)(2,1)}, f32[512,768]{1,0:T(8,128)}, bf16[512,768]{1,0:T(8,128)(2,1)}, bf16[512,768]{1,0:T(8,128)(2,1)}, /*index=5*/f32[8,768]{1,0:T(8,128)}) custom-call(s32[8]{0:T(128)} %stack.140.idx, f32[512,768]{1,0:T(8,128)} %maximum_convert_fusion.1.e, f32[512,768]{1,0:T(8,128)} %get-tuple-element.388.x1, ...), custom_call_target="tpu_custom_call" | custom-call | flops 1000 | bytes 1000 | tf_op jit(solution)/shard_map/feed_back/pallas_call | solution.py:140
  308.8 11.6 %feed_grads.2 = (bf16[4,4,224,768]{3,2,1,0:T(8,128)(2,1)}, bf16[4,4,224,768]{3,2,1,0:T(8,128)(2,1)}) custom-call(s32[8]{0:T(128)} %stack.140.idx, bf16[4,512,768]{2,1,0:T(8,128)(2,1)} %get-tuple-element.392.g, bf16[512,768]{1,0:T(8,128)(2,1)} %get-tuple-element.393.dm, bf16[512,768]{1,0:T(8,128)(2,1)} %get-tuple-element.394.h2, ...), custom_call_target="tpu_custom_call" | custom-call | flops 1000 | bytes 1000 | tf_op jit(solution)/shard_map/feed_grads/pallas_call | solution.py:140
  327.6 11.3 %attend_back_far.2 = (f32[512,768]{1,0:T(8,128)}, bf16[512,1536]{1,0:T(8,128)(2,1)}, f32[12,1,512]{2,1,0:T(1,128)}) custom-call(s32[8]{0:T(128)} %stack.140.idx, bf16[512,768]{1,0:T(8,128)(2,1)} %get-tuple-element.361.q, bf16[512,768]{1,0:T(8,128)(2,1)} %get-tuple-element.402.do, bf16[512,768]{1,0:T(8,128)(2,1)} %get-tuple-element.379.o, ...), custom_call_target="tpu_custom_call" | custom-call | flops 1000 | bytes 1000 | tf_op jit(solution)/shard_map/attend_back_far/pallas_call | solution.py:140
  347.7 22.4 %attend_back_near.2 = (f32[512,768]{1,0:T(8,128)}, bf16[512,1536]{1,0:T(8,128)(2,1)}, bf16[512,1536]{1,0:T(8,128)(2,1)}) custom-call(s32[8]{0:T(128)} %stack.140.idx, bf16[512,768]{1,0:T(8,128)(2,1)} %get-tuple-element.361.q, bf16[512,768]{1,0:T(8,128)(2,1)} %get-tuple-element.402.do, f32[12,1,512]{2,1,0:T(1,128)} %get-tuple-element.403.lse, ...), custom_call_target="tpu_custom_call" | custom-call | flops 1000 | bytes 1000 | tf_op jit(solution)/shard_map/attend_back_near/pallas_call | solution.py:140
  370.2 7.7 %collective-permute-done.57.refs_4_ = bf16[2,4,224,768]{3,2,1,0:T(8,128)(2,1)S(1)} collective-permute-done((bf16[2,4,224,768]{3,2,1,0:T(8,128)(2,1)S(1)}, bf16[2,4,224,768]{3,2,1,0:T(8,128)(2,1)S(1)}, u32[]{:S(2)}, u32[]{:S(2)}) %collective-permute-start.57) | collective-permute-done | bytes 2752544 | tf_op jit(solution)/shard_map/ppermute | solution.py:988
  386.2 14.4 %project_back.2 = (bf16[4,512,576]{2,1,0:T(8,128)(2,1)}, f32[512,768]{1,0:T(8,128)}, f32[8,768]{1,0:T(8,128)}) custom-call(s32[8]{0:T(128)} %stack.140.idx, f32[512,768]{1,0:T(8,128)} %get-tuple-element.410.dq, bf16[512,1536]{1,0:T(8,128)(2,1)} %get-tuple-element.411.dn, bf16[512,1536]{1,0:T(8,128)(2,1)} %get-tuple-element.416.dcr, ...), custom_call_target="tpu_custom_call" | custom-call | flops 1000 | bytes 1000 | tf_op jit(solution)/shard_map/project_back/pallas_call | solution.py:140
  415.9 18.5 %feed_back.3 = (bf16[512,768]{1,0:T(8,128)(2,1)}, bf16[4,512,768]{2,1,0:T(8,128)(2,1)}, f32[512,768]{1,0:T(8,128)}, bf16[512,768]{1,0:T(8,128)(2,1)}, bf16[512,768]{1,0:T(8,128)(2,1)}, /*index=5*/f32[8,768]{1,0:T(8,128)}) custom-call(s32[8]{0:T(128)} %stack.140.idx, f32[512,768]{1,0:T(8,128)} %get-tuple-element.429.e, f32[512,768]{1,0:T(8,128)} %get-tuple-element.430.x1, ...), custom_call_target="tpu_custom_call" | custom-call | flops 1000 | bytes 1000 | tf_op jit(solution)/shard_map/feed_back/pallas_call | solution.py:140
  444.3 11.6 %feed_grads.3 = (bf16[4,4,224,768]{3,2,1,0:T(8,128)(2,1)}, bf16[4,4,224,768]{3,2,1,0:T(8,128)(2,1)}) custom-call(s32[8]{0:T(128)} %stack.140.idx, bf16[4,512,768]{2,1,0:T(8,128)(2,1)} %get-tuple-element.445.g, bf16[512,768]{1,0:T(8,128)(2,1)} %get-tuple-element.446.dm, bf16[512,768]{1,0:T(8,128)(2,1)} %get-tuple-element.447.h2, ...), custom_call_target="tpu_custom_call" | custom-call | flops 1000 | bytes 1000 | tf_op jit(solution)/shard_map/feed_grads/pallas_call | solution.py:140
  470.8 11.3 %attend_back_far.3 = (f32[512,768]{1,0:T(8,128)}, bf16[512,1536]{1,0:T(8,128)(2,1)}, f32[12,1,512]{2,1,0:T(1,128)}) custom-call(s32[8]{0:T(128)} %stack.140.idx, bf16[512,768]{1,0:T(8,128)(2,1)} %get-tuple-element.315.q, bf16[512,768]{1,0:T(8,128)(2,1)} %get-tuple-element.452.do, bf16[512,768]{1,0:T(8,128)(2,1)} %get-tuple-element.344.o, ...), custom_call_target="tpu_custom_call" | custom-call | flops 1000 | bytes 1000 | tf_op jit(solution)/shard_map/attend_back_far/pallas_call | solution.py:140
  494.1 22.4 %attend_back_near.3 = (f32[512,768]{1,0:T(8,128)}, bf16[512,1536]{1,0:T(8,128)(2,1)}, bf16[512,1536]{1,0:T(8,128)(2,1)}) custom-call(s32[8]{0:T(128)} %stack.140.idx, bf16[512,768]{1,0:T(8,128)(2,1)} %get-tuple-element.315.q, bf16[512,768]{1,0:T(8,128)(2,1)} %get-tuple-element.452.do, f32[12,1,512]{2,1,0:T(1,128)} %get-tuple-element.453.lse, ...), custom_call_target="tpu_custom_call" | custom-call | flops 1000 | bytes 1000 | tf_op jit(solution)/shard_map/attend_back_near/pallas_call | solution.py:140
  516.6 11.7 %collective-permute-done.73.refs_4_ = bf16[2,4,224,768]{3,2,1,0:T(8,128)(2,1)S(1)} collective-permute-done((bf16[2,4,224,768]{3,2,1,0:T(8,128)(2,1)S(1)}, bf16[2,4,224,768]{3,2,1,0:T(8,128)(2,1)S(1)}, u32[]{:S(2)}, u32[]{:S(2)}) %collective-permute-start.73) | collective-permute-done | bytes 2752544 | tf_op jit(solution)/shard_map/ppermute | solution.py:988
  538.2 14.4 %project_back.3 = (bf16[4,512,576]{2,1,0:T(8,128)(2,1)}, f32[512,768]{1,0:T(8,128)}, f32[8,768]{1,0:T(8,128)}) custom-call(s32[8]{0:T(128)} %stack.140.idx, f32[512,768]{1,0:T(8,128)} %get-tuple-element.468.dq, bf16[512,1536]{1,0:T(8,128)(2,1)} %get-tuple-element.469.dn, bf16[512,1536]{1,0:T(8,128)(2,1)} %get-tuple-element.476.dcr, ...), custom_call_target="tpu_custom_call" | custom-call | flops 1000 | bytes 1000 | tf_op jit(solution)/shard_map/project_back/pallas_call | solution.py:140
  564.3 8.3 %collective-permute-done.79.refs_4_ = bf16[2,224,768]{2,1,0:T(8,128)(2,1)S(1)} collective-permute-done((bf16[2,224,768]{2,1,0:T(8,128)(2,1)S(1)}, bf16[2,224,768]{2,1,0:T(8,128)(2,1)S(1)}, u32[]{:S(2)}, u32[]{:S(2)}) %collective-permute-start.79) | collective-permute-done | bytes 688160 | tf_op jit(solution)/shard_map/ppermute | solution.py:984
  599.4 8.8 %collective-permute-done.83.refs_3_ = bf16[4,96,576]{2,1,0:T(8,128)(2,1)S(1)} collective-permute-done((bf16[4,96,576]{2,1,0:T(8,128)(2,1)S(1)}, bf16[4,96,576]{2,1,0:T(8,128)(2,1)S(1)}, u32[]{:S(2)}, u32[]{:S(2)}) %collective-permute-start.83) | collective-permute-done | bytes 442400 | tf_op jit(solution)/shard_map/ppermute | solution.py:988
  (710 shorter events, 338.5 us)
Async XLA Ops:
  38.2 28.0 %collective-permute-start.12 = (bf16[224,768]{1,0:T(8,128)(2,1)}, bf16[224,768]{1,0:T(8,128)(2,1)S(1)}, u32[]{:S(2)}, u32[]{:S(2)}) collective-permute-start(bf16[224,768]{1,0:T(8,128)(2,1)} %get-tuple-element.304.refs_6_), channel_id=1, source_target_pairs={{0,2},{1,3},{2,0},{3,1},{4,6},{5,7},{6,4},{7,5},{8,10},{9,11},{10,... | collective-permute-start | bytes 1032200 | tf_op jit(solution)/shard_map/ppermute | solution.py:984
  39.6 26.6 %collective-permute-start.8 = (bf16[4,96,576]{2,1,0:T(8,128)(2,1)}, bf16[4,96,576]{2,1,0:T(8,128)(2,1)S(1)}, u32[]{:S(2)}, u32[]{:S(2)}) collective-permute-start(bf16[4,96,576]{2,1,0:T(8,128)(2,1)} %get-tuple-element.301.refs_0_), channel_id=1, source_target_pairs={{0,16},{4,12},{8,24},{12,4},{16,0},{20,28},{24,8},{28,20},{1,17},{... | collective-permute-start | bytes 1327112 | tf_op jit(solution)/shard_map/ppermute | solution.py:992
  41.1 25.1 %collective-permute-start.9 = (bf16[4,96,576]{2,1,0:T(8,128)(2,1)}, bf16[4,96,576]{2,1,0:T(8,128)(2,1)S(1)}, u32[]{:S(2)}, u32[]{:S(2)}) collective-permute-start(bf16[4,96,576]{2,1,0:T(8,128)(2,1)} %get-tuple-element.302.refs_1_), channel_id=1, source_target_pairs={{0,16},{4,12},{8,24},{12,4},{16,0},{20,28},{24,8},{28,20},{1,17},{... | collective-permute-start | bytes 1327112 | tf_op jit(solution)/shard_map/ppermute | solution.py:992
  85.4 25.7 %collective-permute-start.19 = (bf16[512,1536]{1,0:T(8,128)(2,1)}, bf16[512,1536]{1,0:T(8,128)(2,1)}, u32[]{:S(2)}, u32[]{:S(2)}) collective-permute-start(bf16[512,1536]{1,0:T(8,128)(2,1)} %get-tuple-element.319.own), channel_id=1, source_target_pairs={{4,5},{5,4},{6,7},{7,6},{12,13},{13,12},{14,15},{15,14},{20,21},{2... | collective-permute-start | bytes 4718600 | tf_op jit(solution)/shard_map/ppermute | solution.py:1126
  89.8 21.2 %collective-permute-start.20 = (bf16[4,224,768]{2,1,0:T(8,128)(2,1)S(1)}, bf16[4,224,768]{2,1,0:T(8,128)(2,1)S(1)}, u32[]{:S(2)}, u32[]{:S(2)}) collective-permute-start(bf16[4,224,768]{2,1,0:T(8,128)(2,1)S(1)} %constant_dynamic-update-slice_fusion.refs_4_), channel_id=1, source_target_pairs={{0,8},{4,20},{8,0},{12,28},{16,24},{20,4},{24,16},{28,12},{1,9},{5... | collective-permute-start | bytes 4128776 | tf_op jit(solution)/shard_map/ppermute | solution.py:988
  157.3 29.2 %collective-permute-start.35 = (bf16[2,224,768]{2,1,0:T(8,128)(2,1)S(1)}, bf16[2,224,768]{2,1,0:T(8,128)(2,1)S(1)}, u32[]{:S(2)}, u32[]{:S(2)}) collective-permute-start(bf16[2,224,768]{2,1,0:T(8,128)(2,1)S(1)} %pad_maximum_fusion.3.refs_5_), channel_id=1, source_target_pairs={{0,1},{1,0},{2,3},{3,2},{4,5},{5,4},{6,7},{7,6},{8,9},{9,8},{10,11... | collective-permute-start | bytes 2064392 | tf_op jit(solution)/shard_map/ppermute | solution.py:984
  159.5 27.0 %collective-permute-start.34 = (bf16[4,96,576]{2,1,0:T(8,128)(2,1)S(1)}, bf16[4,96,576]{2,1,0:T(8,128)(2,1)S(1)}, u32[]{:S(2)}, u32[]{:S(2)}) collective-permute-start(bf16[4,96,576]{2,1,0:T(8,128)(2,1)S(1)} %pad_maximum_fusion.5.refs_1_), channel_id=1, source_target_pairs={{0,24},{4,28},{8,16},{12,20},{16,8},{20,12},{24,0},{28,4},{1,25},{... | collective-permute-start | bytes 1327112 | tf_op jit(solution)/shard_map/ppermute | solution.py:980
  161.9 24.6 %collective-permute-start.33 = (bf16[4,96,576]{2,1,0:T(8,128)(2,1)S(1)}, bf16[4,96,576]{2,1,0:T(8,128)(2,1)S(1)}, u32[]{:S(2)}, u32[]{:S(2)}) collective-permute-start(bf16[4,96,576]{2,1,0:T(8,128)(2,1)S(1)} %pad_maximum_fusion.5.refs_1_), channel_id=1, source_target_pairs={{0,16},{4,12},{8,24},{12,4},{16,0},{20,28},{24,8},{28,20},{1,17},{... | collective-permute-start | bytes 1327112 | tf_op jit(solution)/shard_map/ppermute | solution.py:992
  162.4 24.1 %collective-permute-start.32 = (bf16[4,96,576]{2,1,0:T(8,128)(2,1)S(1)}, bf16[4,96,576]{2,1,0:T(8,128)(2,1)S(1)}, u32[]{:S(2)}, u32[]{:S(2)}) collective-permute-start(bf16[4,96,576]{2,1,0:T(8,128)(2,1)S(1)} %pad_maximum_fusion.5.refs_1_), channel_id=1, source_target_pairs={{0,8},{4,20},{8,0},{12,28},{16,24},{20,4},{24,16},{28,12},{1,9},{5... | collective-permute-start | bytes 1327112 | tf_op jit(solution)/shard_map/ppermute | solution.py:988
  211.6 23.9 %collective-permute-start.42 = (bf16[512,1536]{1,0:T(8,128)(2,1)}, bf16[512,1536]{1,0:T(8,128)(2,1)S(1)}, u32[]{:S(2)}, u32[]{:S(2)}) collective-permute-start(bf16[512,1536]{1,0:T(8,128)(2,1)} %get-tuple-element.365.own), channel_id=1, source_target_pairs={{4,5},{5,4},{6,7},{7,6},{12,13},{13,12},{14,15},{15,14},{20,21},{2... | collective-permute-start | bytes 4718600 | tf_op jit(solution)/shard_map/ppermute | solution.py:1126
  212.4 23.1 %collective-permute-start.43 = (bf16[4,224,768]{2,1,0:T(8,128)(2,1)}, bf16[4,224,768]{2,1,0:T(8,128)(2,1)S(1)}, u32[]{:S(2)}, u32[]{:S(2)}) collective-permute-start(bf16[4,224,768]{2,1,0:T(8,128)(2,1)} %get-tuple-element.369.refs_4_), channel_id=1, source_target_pairs={{0,16},{4,12},{8,24},{12,4},{16,0},{20,28},{24,8},{28,20},{1,17},{... | collective-permute-start | bytes 4128776 | tf_op jit(solution)/shard_map/ppermute | solution.py:992
  260.9 23.7 %collective-permute-start.51 = (bf16[256,768]{1,0:T(8,128)(2,1)S(1)}, bf16[256,768]{1,0:T(8,128)(2,1)S(1)}, u32[]{:S(2)}, u32[]{:S(2)}) collective-permute-start(bf16[256,768]{1,0:T(8,128)(2,1)S(1)} %get-tuple-element.628), channel_id=1, source_target_pairs={{0,1},{1,0},{2,5},{3,4},{4,3},{5,2},{6,7},{7,6},{8,9},{9,8},{10,13... | collective-permute-start | bytes 1179656 | tf_op jit(solution)/shard_map/ppermute | solution.py:1121
  262.1 22.5 %collective-permute-start.50 = (bf16[256,768]{1,0:T(8,128)(2,1)S(1)}, bf16[256,768]{1,0:T(8,128)(2,1)S(1)}, u32[]{:S(2)}, u32[]{:S(2)}) collective-permute-start(bf16[256,768]{1,0:T(8,128)(2,1)S(1)} %get-tuple-element.629), channel_id=1, source_target_pairs={{0,0},{1,1},{2,4},{3,5},{4,2},{5,3},{6,6},{7,7},{8,8},{9,9},{10,12... | collective-permute-start | bytes 1179656 | tf_op jit(solution)/shard_map/ppermute | solution.py:1121
  287.2 33.2 %collective-permute-start.53 = (bf16[256,768]{1,0:T(8,128)(2,1)S(1)}, bf16[256,768]{1,0:T(8,128)(2,1)S(1)}, u32[]{:S(2)}, u32[]{:S(2)}) collective-permute-start(bf16[256,768]{1,0:T(8,128)(2,1)S(1)} %get-tuple-element.626), channel_id=1, source_target_pairs={{0,1},{1,0},{2,5},{3,4},{4,3},{5,2},{6,7},{7,6},{8,9},{9,8},{10,13... | collective-permute-start | bytes 1179656 | tf_op jit(solution)/shard_map/ppermute | solution.py:1121
  288.1 32.3 %collective-permute-start.52 = (bf16[256,768]{1,0:T(8,128)(2,1)S(1)}, bf16[256,768]{1,0:T(8,128)(2,1)S(1)}, u32[]{:S(2)}, u32[]{:S(2)}) collective-permute-start(bf16[256,768]{1,0:T(8,128)(2,1)S(1)} %get-tuple-element.627), channel_id=1, source_target_pairs={{0,0},{1,1},{2,4},{3,5},{4,2},{5,3},{6,6},{7,7},{8,8},{9,9},{10,12... | collective-permute-start | bytes 1179656 | tf_op jit(solution)/shard_map/ppermute | solution.py:1121
  344.7 33.1 %collective-permute-start.57 = (bf16[2,4,224,768]{3,2,1,0:T(8,128)(2,1)S(1)}, bf16[2,4,224,768]{3,2,1,0:T(8,128)(2,1)S(1)}, u32[]{:S(2)}, u32[]{:S(2)}) collective-permute-start(bf16[2,4,224,768]{3,2,1,0:T(8,128)(2,1)S(1)} %add_convert_fusion.1), channel_id=1, source_target_pairs={{0,8},{4,20},{8,0},{12,28},{16,24},{20,4},{24,16},{28,12},{1,9},{5... | collective-permute-start | bytes 8257544 | tf_op jit(solution)/shard_map/ppermute | solution.py:988
  345.9 31.9 %collective-permute-start.56 = (bf16[512,1536]{1,0:T(8,128)(2,1)S(1)}, bf16[512,1536]{1,0:T(8,128)(2,1)}, u32[]{:S(2)}, u32[]{:S(2)}) collective-permute-start(bf16[512,1536]{1,0:T(8,128)(2,1)S(1)} %add_convert_fusion.3), channel_id=1, source_target_pairs={{4,5},{5,4},{6,7},{7,6},{12,13},{13,12},{14,15},{15,14},{20,21},{2... | collective-permute-start | bytes 4718600 | tf_op jit(solution)/shard_map/ppermute | solution.py:1126
  408.9 25.6 %collective-permute-start.61 = (bf16[4,4,96,576]{3,2,1,0:T(8,128)(2,1)}, bf16[4,4,96,576]{3,2,1,0:T(8,128)(2,1)}, u32[]{:S(2)}, u32[]{:S(2)}) collective-permute-start(bf16[4,4,96,576]{3,2,1,0:T(8,128)(2,1)} %get-tuple-element.439), channel_id=1, source_target_pairs={{0,4},{4,0},{8,12},{12,8},{16,20},{20,16},{24,28},{28,24},{1,5},{5... | collective-permute-start | bytes 5308424 | tf_op jit(solution)/shard_map/ppermute | solution.py:980
  487.8 40.5 %collective-permute-start.73 = (bf16[2,4,224,768]{3,2,1,0:T(8,128)(2,1)S(1)}, bf16[2,4,224,768]{3,2,1,0:T(8,128)(2,1)S(1)}, u32[]{:S(2)}, u32[]{:S(2)}) collective-permute-start(bf16[2,4,224,768]{3,2,1,0:T(8,128)(2,1)S(1)} %add_convert_fusion), channel_id=1, source_target_pairs={{0,8},{4,20},{8,0},{12,28},{16,24},{20,4},{24,16},{28,12},{1,9},{5... | collective-permute-start | bytes 8257544 | tf_op jit(solution)/shard_map/ppermute | solution.py:988
  490.0 38.3 %collective-permute-start.72 = (bf16[512,1536]{1,0:T(8,128)(2,1)}, bf16[512,1536]{1,0:T(8,128)(2,1)}, u32[]{:S(2)}, u32[]{:S(2)}) collective-permute-start(bf16[512,1536]{1,0:T(8,128)(2,1)} %add_convert_fusion.2), channel_id=1, source_target_pairs={{4,5},{5,4},{6,7},{7,6},{12,13},{13,12},{14,15},{15,14},{20,21},{2... | collective-permute-start | bytes 4718600 | tf_op jit(solution)/shard_map/ppermute | solution.py:1126
  492.0 24.5 %collective-permute-start.74 = (bf16[224,768]{1,0:T(8,128)(2,1)S(1)}, bf16[224,768]{1,0:T(8,128)(2,1)S(1)}, u32[]{:S(2)}, u32[]{:S(2)}) collective-permute-start(bf16[224,768]{1,0:T(8,128)(2,1)S(1)} %copy-done.21), channel_id=1, source_target_pairs={{0,16},{4,12},{8,24},{12,4},{16,0},{20,28},{24,8},{28,20},{1,17},{... | collective-permute-start | bytes 1032200 | tf_op jit(solution)/shard_map/ppermute | solution.py:992
  493.5 23.1 %collective-permute-start.75 = (bf16[224,768]{1,0:T(8,128)(2,1)S(1)}, bf16[224,768]{1,0:T(8,128)(2,1)S(1)}, u32[]{:S(2)}, u32[]{:S(2)}) collective-permute-start(bf16[224,768]{1,0:T(8,128)(2,1)S(1)} %copy-done.37), channel_id=1, source_target_pairs={{0,16},{4,12},{8,24},{12,4},{16,0},{20,28},{24,8},{28,20},{1,17},{... | collective-permute-start | bytes 1032200 | tf_op jit(solution)/shard_map/ppermute | solution.py:992
  585.1 23.0 %collective-permute-start.83 = (bf16[4,96,576]{2,1,0:T(8,128)(2,1)S(1)}, bf16[4,96,576]{2,1,0:T(8,128)(2,1)S(1)}, u32[]{:S(2)}, u32[]{:S(2)}) collective-permute-start(bf16[4,96,576]{2,1,0:T(8,128)(2,1)S(1)} %get-tuple-element.617), channel_id=1, source_target_pairs={{0,8},{4,20},{8,0},{12,28},{16,24},{20,4},{24,16},{28,12},{1,9},{5... | collective-permute-start | bytes 1327112 | tf_op jit(solution)/shard_map/ppermute | solution.py:988
  586.6 21.7 %collective-permute-start.82 = (bf16[4,96,576]{2,1,0:T(8,128)(2,1)S(1)}, bf16[4,96,576]{2,1,0:T(8,128)(2,1)S(1)}, u32[]{:S(2)}, u32[]{:S(2)}) collective-permute-start(bf16[4,96,576]{2,1,0:T(8,128)(2,1)S(1)} %get-tuple-element.618), channel_id=1, source_target_pairs={{0,16},{4,12},{8,24},{12,4},{16,0},{20,28},{24,8},{28,20},{1,17},{... | collective-permute-start | bytes 1327112 | tf_op jit(solution)/shard_map/ppermute | solution.py:992
  (259 other events, 1711.6 us)

commit v4 on v3

--- a/solution.py
+++ b/solution.py
@@ -230,9 +230,11 @@
     clean, level = idx[2], idx[4]
     qi = lax.shift_right_logical(lax.broadcasted_iota(jnp.int32, (HALF, HALF), query_dim), level)
     ki = lax.shift_right_logical(lax.broadcasted_iota(jnp.int32, (HALF, HALF), 1 - query_dim), level)
-    bias[...] = jnp.where(ki < qi + clean, 0.0, MASKED)
-    same = jnp.where(ki == qi, 0, 1) + clean
-    bias_n[...] = jnp.where(same[:128, :128] == 0, 0.0, MASKED)
+    allowed = jnp.where(ki < qi + clean, 0.0, MASKED)
+    bias[...] = jnp.concatenate([allowed, allowed], axis=query_dim)
+    same = (jnp.where(ki == qi, 0, 1) + clean)[:128, :128]
+    own = jnp.where(same == 0, 0.0, MASKED)
+    bias_n[...] = jnp.concatenate([own, own], axis=query_dim)
 
 
 def lanes(rows):
@@ -242,6 +244,15 @@
 def one_head(v, side):
     low_lane = lanes(v.shape[0]) < 64
     return jnp.where(low_lane if side == 0 else jnp.logical_not(low_lane), v, jnp.zeros_like(v))
+
+
+def both_heads(v):
+    return jnp.concatenate([one_head(v, 0), one_head(v, 1)], axis=0)
+
+
+def pair_lanes(v):
+    n = v.shape[0] // 2
+    return jnp.where(lanes(n) < 64, v[:n], v[n:])
 
 
 def pair_cols(hp):
@@ -275,34 +286,35 @@
             lane = lanes(HALF)
             for half, sources in tiles:
                 rows = half_rows(half)
-                q2 = q[rows, cols]
-                sides = []
-                for side in range(2):
-                    qm = one_head(q2, side)
-                    scores = []
-                    for kh, diagonal in sources:
-                        s = dot_nt(qm, kvc[half_rows(kh), cols])
-                        scores.append(s + bias[...] if diagonal else s)
-                    blocks = [slice(HALF * half + 128 * t, HALF * half + 128 * (t + 1)) for t in range(2)]
-                    parts = [slice(128 * t, 128 * (t + 1)) for t in range(2)]
-                    mine = [dot_nt(qm[part], kvn[block, cols]) + bias_n[...] for part, block in zip(parts, blocks)]
-                    top = jnp.concatenate([row_max(s) for s in mine], axis=0)
-                    for s in scores:
-                        top = jnp.maximum(top, row_max(s))
-                    total = jnp.concatenate(
-                        [
-                            dot(jnp.exp(s - top[part]).astype(BF), with_ones(kvn[block, vcols]))
-                            for s, part, block in zip(mine, parts, blocks)
-                        ],
-                        axis=0,
-                    )
-                    for s, (kh, diagonal) in zip(scores, sources):
-                        total = total + dot(jnp.exp(s - top).astype(BF), with_ones(kvc[half_rows(kh), vcols]))
-                    sides.append((total[:, :128], top, total[:, 128:]))
-                acc[rows, cols] = jnp.where(lane < 64, sides[0][0], sides[1][0])
-                for target, at in ((tops, 1), (counts, 2)):
+                qs = both_heads(q[rows, cols])
+                scores = []
+                for kh, diagonal in sources:
+                    s = dot_nt(qs, kvc[half_rows(kh), cols])
+                    scores.append(s + bias[...] if diagonal else s)
+                blocks = [slice(HALF * half + 128 * t, HALF * half + 128 * (t + 1)) for t in range(2)]
+
+                def of_block(v, t):
+                    return jnp.concatenate([v[128 * t : 128 * (t + 1)], v[HALF + 128 * t : HALF + 128 * (t + 1)]], axis=0)
+
+                def of_heads(a, b):
+                    return jnp.concatenate([a[:128], b[:128], a[128:], b[128:]], axis=0)
+
+                mine = [dot_nt(of_block(qs, t), kvn[blocks[t], cols]) + bias_n[...] for t in range(2)]
+                top = of_heads(*[row_max(s) for s in mine])
+                for s in scores:
+                    top = jnp.maximum(top, row_max(s))
+                total = of_heads(
+                    *[
+                        dot(jnp.exp(mine[t] - of_block(top, t)).astype(BF), with_ones(kvn[blocks[t], vcols]))
+                        for t in range(2)
+                    ]
+                )
+                for s, (kh, diagonal) in zip(scores, sources):
+                    total = total + dot(jnp.exp(s - top).astype(BF), with_ones(kvc[half_rows(kh), vcols]))
+                acc[rows, cols] = pair_lanes(total[:, :128])
+                for target, value in ((tops, top), (counts, total[:, 128:])):
                     target[rows] = jnp.where(
-                        lane == 2 * hp, sides[0][at], jnp.where(lane == 2 * hp + 1, sides[1][at], target[rows])
+                        lane == 2 * hp, value[:HALF], jnp.where(lane == 2 * hp + 1, value[HALF:], target[rows])
                     )
             return carry
 
@@ -321,8 +333,8 @@
         [
             pltpu.VMEM((ROWS, 2 * D), BF),
             pltpu.VMEM((ROWS, 2 * D), BF),
-            pltpu.VMEM((HALF, HALF), F32),
-            pltpu.VMEM((128, 128), F32),
+            pltpu.VMEM((2 * HALF, HALF), F32),
+            pltpu.VMEM((HALF, 128), F32),
             pltpu.SemaphoreType.DMA((2,)),
         ],
         (idx, q, own, near),
@@ -611,20 +623,17 @@
 
 
 def back_tile(q, do, lse, drow, cols, hp, k2, v2, qrow, n, bias_here):
-    q2, g2 = q[qrow : qrow + n, cols], do[qrow : qrow + n, cols]
-    sums = None
-    for side in range(2):
-        qm, gm, km = one_head(q2, side), one_head(g2, side), one_head(k2, side)
-        head = 2 * hp + side
-        s = dot_nt(k2, qm)
-        if bias_here is not None:
-            s = s + bias_here
-        p = jnp.exp(s - lse[head, :, qrow : qrow + n])
-        dp = dot_nt(v2, gm)
-        ds = (p * (dp - drow[head, :, qrow : qrow + n])).astype(BF)
-        parts = (dot(ds, qm), dot(p.astype(BF), gm), dot_tn(ds, km))
-        sums = parts if sums is None else tuple(a + b for a, b in zip(sums, parts))
-    return sums
+    qs, gs = both_heads(q[qrow : qrow + n, cols]), both_heads(do[qrow : qrow + n, cols])
+
+    def of_heads(ref):
+        return jnp.concatenate([ref[2 * hp + side, :, qrow : qrow + n] for side in range(2)], axis=1)
+
+    s = dot_nt(k2, qs)
+    if bias_here is not None:
+        s = s + bias_here
+    p = jnp.exp(s - of_heads(lse))
+    ds = (p * (dot_nt(v2, gs) - of_heads(drow))).astype(BF)
+    return dot(ds, qs), dot(p.astype(BF), gs), pair_lanes(dot_tn(ds, k2))
 
 
 def attend_back_far_body(idx, q, do, o, lse, far, far_near, dq, dr, drow, kvr, dcol, sem):
@@ -755,8 +764,8 @@
         [
             pltpu.VMEM((ROWS, 2 * D), BF),
             pltpu.VMEM((ROWS, 2 * D), BF),
-            pltpu.VMEM((HALF, HALF), F32),
-            pltpu.VMEM((128, 128), F32),
+            pltpu.VMEM((HALF, 2 * HALF), F32),
+            pltpu.VMEM((128, HALF), F32),
             pltpu.SemaphoreType.DMA((2,)),
         ],
         (idx, q, do, lse, drow, dq_far, own, near),
@@ -1048,19 +1057,27 @@
     return keep, flip_wide(send, 1)
 
 
-def reduce_first(pair):
+def reduce_first_sums(pair):
+    keep, got = pair
+    return keep, got, added(keep[3], got[3]), added(keep[2], got[2])
+
+
+def reduce_first(parts):
+    keep, got, passed, stays = parts
+    return keep, got, first_axis(passed), first_axis(stays)
+
+
+def reduce_first_whole(pair):
     keep, got = pair
     return keep, got, first_axis(added(keep[2:], got[2:]))
 
 
-def reduce_second(parts):
-    keep, got, first = parts
-    return keep, got, first, second_axis(added(keep[1], got[1], first[1]))
+def reduce_second(keep, got, passed):
+    return second_axis(added(keep[1], got[1], passed))
 
 
 def reduce_near(parts):
-    keep, got, first, second = parts
-    total = added(keep[0], got[0], first[0], second)
+    total = added(parts[0][0], parts[1][0], *parts[2:])
     bit = 8
     while bit < lax.axis_size("wide"):
         total = added(total, flip_wide(total, bit))
@@ -1115,10 +1132,18 @@
 BOTH = ("wide", "narrow")
 
 
+def relocate_first(rows):
+    pairs = device_pairs(lambda w, z: ((w & ~1) | (z >> 1), ((w & 1) << 1) | (z & 1)))
+    return lax.ppermute(rows[:HALF], BOTH, pairs)
+
+
+def relocate_second(rows):
+    pairs = device_pairs(lambda w, z: ((w & ~1) | (z >> 1), ((w & 1) << 1) | (1 - (z & 1))))
+    return lax.ppermute(rows[HALF:], BOTH, pairs)
+
+
 def relocate(rows):
-    first = device_pairs(lambda w, z: ((w & ~1) | (z >> 1), ((w & 1) << 1) | (z & 1)))
-    second = device_pairs(lambda w, z: ((w & ~1) | (z >> 1), ((w & 1) << 1) | (1 - (z & 1))))
-    return lax.ppermute(rows[:HALF], BOTH, first), lax.ppermute(rows[HALF:], BOTH, second)
+    return relocate_first(rows), relocate_second(rows)
 
 
 def between_chips(x):
@@ -1244,12 +1269,14 @@
     g_feed1 = reduce_core(g_feed1)
     dq, dr, drow = attend_back_far(idx, q_1, do, o_1, lse_1, far_1, far_near_1)
     dr, dq, g_feed1 = gate((dr, dq, g_feed1))
-    far = between_chips(added(dr, within_chip(dr, 0)))
+    dr, got, dq, g_feed1 = gate((dr, within_chip(dr, 0), dq, reduce_first_sums(g_feed1)))
+    far = between_chips(added(dr, got))
     g_feed1 = reduce_first(g_feed1)
     dq, dn, dc = attend_back_near(idx, q_1, do, lse_1, drow, dq, own_1, near_1)
-    dc, far, g_feed1 = gate((dc, far, g_feed1))
+    keep, gained, passed, stays = g_feed1
+    dc, far, keep, gained, passed = gate((dc, far, keep, gained, passed))
     got = within_chip(dc, 0)
-    g_feed1 = reduce_second(g_feed1)
+    g_feed1 = keep, gained, stays, reduce_second(keep, gained, passed)
     dpz, e, small_mixer1 = project_back(
         idx, dq, dn, dc, got, far, cosine, sine, x1, e1, norm_gain[1, 0:1], mixer1
     )
@@ -1260,41 +1287,41 @@
     g_mixer1 = reduce_core(g_mixer1)
     dm, dz, e1, da, do, small_feed0 = feed_back(idx, e, x1_0, gp_0, norm_gain[0, 1:2], feed0)
     dm, do, g_feed1, g_mixer1 = gate((dm, do, g_feed1, g_mixer1))
-    g_feed1, g_mixer1 = reduce_far(g_feed1), reduce_plane(g_mixer1)
+    g_feed1, g_mixer1 = reduce_far(g_feed1), reduce_first_whole(g_mixer1)
     g_feed0 = feed_grads(idx, g_0, dm, h2_0, dz, o_0, da)
     do, g_feed1, g_mixer1, g_feed0 = gate((do, g_feed1, g_mixer1, g_feed0))
-    g_mixer1, g_feed0 = reduce_narrow(g_mixer1), reduce_core(g_feed0)
+    keep1, gained1, both1 = g_mixer1
+    second1, g_feed0 = reduce_second(keep1, gained1, both1[1]), reduce_core(g_feed0)
     g_feed1 = spread_first(g_feed1)
     dq, dr, drow = attend_back_far(idx, q_0, do, o_0, lse_0, far_0, far_near_0)
-    dr, dq, g_feed1, g_mixer1, g_feed0 = gate((dr, dq, g_feed1, g_mixer1, g_feed0))
-    far = between_chips(added(dr, within_chip(dr, 0)))
+    dr, dq, g_feed1, second1, g_feed0 = gate((dr, dq, g_feed1, second1, g_feed0))
+    dr, got, dq, g_feed0, g_feed1 = gate((dr, within_chip(dr, 0), dq, reduce_first_sums(g_feed0), g_feed1))
+    far = between_chips(added(dr, got))
     g_feed0, g_feed1 = reduce_first(g_feed0), gather_second(g_feed1)
     dq, dn, dc = attend_back_near(idx, q_0, do, lse_0, drow, dq, own_0, near_0)
-    dc, far, g_feed0, g_feed1 = gate((dc, far, g_feed0, g_feed1))
+    keep, gained, passed, stays = g_feed0
+    dc, far, keep, gained, passed, g_feed1 = gate((dc, far, keep, gained, passed, g_feed1))
     got = within_chip(dc, 0)
-    g_feed0 = reduce_second(g_feed0)
-    total, *others = g_mixer1
-    g_mixer1 = gather_first(added(total[0], *others))
+    g_feed0 = keep, gained, stays, reduce_second(keep, gained, passed)
+    g_mixer1 = reduce_near((keep1, gained1, both1[0], second1))
     dpz, e, small_mixer0 = project_back(
         idx, dq, dn, dc, got, far, cosine, sine, x0, e1, norm_gain[0, 0:1], mixer0
     )
     e, dpz, g_feed0, g_mixer1 = gate((e, dpz, g_feed0, g_mixer1))
-    g_feed0 = reduce_near(g_feed0)
-    g_mixer0 = project_grads(idx, h1_0, dpz)
+    g_feed0, g_mixer1 = reduce_near(g_feed0), reduce_far(g_mixer1)
+    g_mixer0 = reduce_core(project_grads(idx, h1_0, dpz))
     smalls = jnp.concatenate([small_feed0, small_mixer0, small_feed1, small_mixer1])
-    g_mixer0, smalls, g_feed0, g_feed1, g_mixer1, e = gate((g_mixer0, smalls, g_feed0, g_feed1, g_mixer1, e))
-    g_mixer0 = reduce_core(g_mixer0)
+    g_feed1 = gather_last(g_feed1)
     smalls = smalls, flip_wide(smalls, 1)
-    g_mixer0, smalls, e = gate((g_mixer0, smalls, e))
+    g_mixer0, smalls, e, g_feed1, g_mixer1 = gate((g_mixer0, smalls, e, g_feed1, g_mixer1))
     g_mixer0 = reduce_plane(g_mixer0)
-    rows = relocate(e.astype(BF))
-    smalls = smalls[0] + smalls[1]
-    smalls = smalls, first_axis(smalls)
-    g_feed1 = gather_last(g_feed1)
+    early, e_late = relocate_first(e.astype(BF)), e
     feed_out = finish_feed(idx, 1, layers, g_feed1, None)
-    g_mixer0, g_feed0, smalls, feed_out, rows, g_mixer1 = gate((g_mixer0, g_feed0, smalls, feed_out, rows, g_mixer1))
-    keep, got, *others = g_mixer0
-    total = added(keep[0], got[0], *others)
+    g_mixer0, g_feed0, smalls, feed_out, early, e_late, g_mixer1 = gate(
+        (g_mixer0, g_feed0, smalls, feed_out, early, e_late, g_mixer1)
+    )
+    keep, gained, *others = g_mixer0
+    total = added(keep[0], gained[0], *others)
     bit = 8
     while bit < lax.axis_size("wide"):
         total = added(total, flip_wide(total, bit))
@@ -1302,10 +1329,15 @@
     g_mixer0 = total, flip_narrow(total[2:], 1)
     g_feed0 = reduce_far(g_feed0)
     smalls = smalls[0] + smalls[1]
+    smalls = smalls, first_axis(smalls)
+    g_mixer1 = spread_first(g_mixer1)
+    g_mixer0, g_feed0, smalls, g_mixer1 = gate((g_mixer0, g_feed0, smalls, g_mixer1))
+    g_mixer0, g_feed0 = reduce_far(g_mixer0), spread_first(g_feed0)
+    smalls = smalls[0] + smalls[1]
     smalls = smalls, second_axis(smalls)
     g_mixer1 = gather_second(g_mixer1)
     g_mixer0, g_feed0, smalls, g_mixer1 = gate((g_mixer0, g_feed0, smalls, g_mixer1))
-    g_mixer0, g_feed0 = reduce_far(g_mixer0), spread_first(g_feed0)
+    g_mixer0, g_feed0 = spread_first(g_mixer0), gather_second(g_feed0)
     smalls = smalls[0] + smalls[1]
     bit = 8
     while bit < lax.axis_size("wide"):
@@ -1314,19 +1346,17 @@
     smalls = smalls, flip_narrow(smalls, 1)
     g_mixer1 = gather_last(g_mixer1)
     mixer_out = finish_mixer(idx, 1, layers, g_mixer1, None)
-    g_mixer0, g_feed0, smalls, mixer_out = gate((g_mixer0, g_feed0, smalls, mixer_out))
-    g_mixer0, g_feed0 = spread_first(g_mixer0), gather_second(g_feed0)
+    g_mixer0, g_feed0, smalls, e_late, mixer_out = gate((g_mixer0, g_feed0, smalls, e_late, mixer_out))
+    g_mixer0, g_feed0 = gather_second(g_mixer0), gather_last(g_feed0)
+    late = relocate_second(e_late.astype(BF))
     smalls = smalls[0] + smalls[1]
     smalls = smalls, flip_narrow(smalls, 2)
-    g_mixer0, g_feed0, smalls = gate((g_mixer0, g_feed0, smalls))
-    g_mixer0 = gather_second(g_mixer0)
+    feed_out = finish_feed(idx, 0, layers, g_feed0, feed_out)
+    g_mixer0, smalls, late, feed_out = gate((g_mixer0, smalls, late, feed_out))
     smalls = smalls[0] + smalls[1]
-    g_feed0 = gather_last(g_feed0)
-    feed_out = finish_feed(idx, 0, layers, g_feed0, feed_out)
-    g_mixer0, feed_out = gate((g_mixer0, feed_out))
     g_mixer0 = gather_last(g_mixer0)
     mixer_out = finish_mixer(idx, 0, layers, g_mixer0, mixer_out)
-    tokens_grad = jnp.concatenate(rows)
+    tokens_grad = jnp.concatenate([early, late])
     x_out = jnp.concatenate(x_out)
 
     small = smalls.reshape(layers, 16, D)

time: 695 us -> 675 us (0.971)
  waiting for transfers between devices: 140 us -> 117 us
  Pallas kernels: 295 us -> 286 us
    ppermute x13 -> x15, waiting for transfers between devices: 42.8 us -> 23 us  [first_axis(): lax.ppermute(x, 'wide', [(i, i ^ (4 if i & 1 else 2)) for i in range(lax....]
    pallas_call x25, Pallas kernels: 295 us -> 286 us  [kernel_call(): pl.pallas_call(body, in_specs=in_specs, out_specs=out_specs, out_shape=ou...]
    convert_element_type x19 -> x21, other arithmetic: 36.1 us -> 43.1 us  [added(): return functools.reduce(jnp.add, [t.astype(F32) for t in terms]).astype(BF)]
    ppermute x13 -> x15, starting transfers between devices: 13.8 us -> 17.7 us  [first_axis(): lax.ppermute(x, 'wide', [(i, i ^ (4 if i & 1 else 2)) for i in range(lax....]
    ppermute x24 -> x23, starting transfers between devices: 32.7 us -> 30.9 us  [flip_narrow(): return lax.ppermute(x, 'narrow', [(i, i ^ bit) for i in range(QUARTERS)])]
    ppermute x41 -> x40, starting transfers between devices: 22.3 us -> 20.8 us  [flip_wide(): lax.ppermute(x, 'wide', [(i, i ^ bit) for i in range(lax.axis_size('wide'...]
    unnamed x337 -> x360, local copies, waits for them, and re-layouts: 53.3 us -> 54.2 us
    ppermute x24 -> x23, waiting for transfers between devices: 61.5 us -> 62 us  [flip_narrow(): return lax.ppermute(x, 'narrow', [(i, i ^ bit) for i in range(QUARTERS)])]
  transfers between devices with their start and end apart: 118 -> 118, of which waited for: 37 -> 35; matrix products, arithmetic and copies ran while one was open for 9% -> 10% of each run, Pallas kernels for 42% -> 41%
where the time goes in v4:
time: 675 us; the launch traced here: 664 us
  Pallas kernels  286 us (42%)
  waiting for transfers between devices  117 us (17%)
  starting transfers between devices  116 us (17%)
  local copies, waits for them, and re-layouts  78.7 us (12%)
  other arithmetic  61.8 us (9%)
    pallas_call x25, Pallas kernels, kernel_call(): pl.pallas_call(body, in_specs=in_specs, out_specs=out_specs, out_shape=ou...  286 us
    ppermute x23, waiting for transfers between devices, flip_narrow(): return lax.ppermute(x, 'narrow', [(i, i ^ bit) for i in range(QUARTERS)])  62 us
    unnamed x360, local copies, waits for them, and re-layouts  54.2 us
    convert_element_type x21, other arithmetic, added(): return functools.reduce(jnp.add, [t.astype(F32) for t in terms]).astype(BF)  43.1 us
    ppermute x23, starting transfers between devices, flip_narrow(): return lax.ppermute(x, 'narrow', [(i, i ^ bit) for i in range(QUARTERS)])  30.9 us
    ppermute x15, waiting for transfers between devices, first_axis(): lax.ppermute(x, 'wide', [(i, i ^ (4 if i & 1 else 2)) for i in range(lax....  23 us
    ppermute x20, starting transfers between devices, second_axis(): lax.ppermute(x, 'wide', [(i, i ^ (2 if i & 1 else 4)) for i in range(lax....  21.3 us
    ppermute x40, starting transfers between devices, flip_wide(): lax.ppermute(x, 'wide', [(i, i ^ bit) for i in range(lax.axis_size('wide'...  20.8 us
  transfers between devices with their start and end apart: 118, of which 35 were waited for; matrix products, arithmetic and copies ran while one was open for 10% of the time, Pallas kernels for 41%

profile of v4, /device:TPU:0, one launch (start us, length us, event | category | flops | bytes accessed | tf_op | source)
XLA Modules:
  0.0 664.1 jit_solution(13351487555820100512)
XLA Ops:
  43.1 23.1 %collective-permute-done.12.refs_7_ = bf16[224,768]{1,0:T(8,128)(2,1)S(1)} collective-permute-done((bf16[224,768]{1,0:T(8,128)(2,1)}, bf16[224,768]{1,0:T(8,128)(2,1)S(1)}, u32[]{:S(2)}, u32[]{:S(2)}) %collective-permute-start.12) | collective-permute-done | bytes 344096 | tf_op jit(solution)/shard_map/ppermute | solution.py:993
  75.1 8.2 %project.2 = (bf16[512,768]{1,0:T(8,128)(2,1)}, bf16[512,768]{1,0:T(8,128)(2,1)}, bf16[512,1536]{1,0:T(8,128)(2,1)}) custom-call(s32[8]{0:T(128)} %stack.140.idx, f32[512,768]{1,0:T(8,128)} %maximum_convert_fusion.x, f32[1,768]{1,0:T(1,128)} %get-tuple-element.705.gain, f32[1,768]{1,0:T(1,128)} %get-tuple-element.685.shift, ...), custom_call_target="tpu_custom_call" | custom-call | flops 1000 | bytes 1000 | tf_op jit(solution)/shard_map/project/pallas_call | solution.py:140
  92.9 15.3 %attend_near.2 = (f32[512,768]{1,0:T(8,128)}, f32[512,128]{1,0:T(8,128)}, f32[512,128]{1,0:T(8,128)}) custom-call(s32[8]{0:T(128)} %stack.140.idx, bf16[512,768]{1,0:T(8,128)(2,1)} %get-tuple-element.332.q, bf16[512,1536]{1,0:T(8,128)(2,1)} %get-tuple-element.336.own, bf16[512,1536]{1,0:T(8,128)(2,1)} %collective-permute-done.18.near), custom_call_target="tpu_custom_call" | custom-call | flops 1000 | bytes 1000 | tf_op jit(solution)/shard_map/attend_near/pallas_call | solution.py:140
  117.7 8.6 %attend_far.2 = (bf16[512,768]{1,0:T(8,128)(2,1)}, f32[12,1,512]{2,1,0:T(1,128)}) custom-call(s32[8]{0:T(128)} %stack.140.idx, bf16[512,768]{1,0:T(8,128)(2,1)} %get-tuple-element.332.q, bf16[512,1536]{1,0:T(8,128)(2,1)} %get-tuple-element.343.far, bf16[512,1536]{1,0:T(8,128)(2,1)} %copy-done.32, f32[512,768]{1,0:T(8,128)} %get-tuple-element.344.acc, ...), custom_call_target="tpu_custom_call" | custom-call | flops 1000 | bytes 1000 | tf_op jit(solution)/shard_map/attend_far/pallas_call | solution.py:140
  134.8 15.3 %collective-permute-done.30.refs_10_ = bf16[224,768]{1,0:T(8,128)(2,1)S(1)} collective-permute-done((bf16[224,768]{1,0:T(8,128)(2,1)}, bf16[224,768]{1,0:T(8,128)(2,1)S(1)}, u32[]{:S(2)}, u32[]{:S(2)}) %collective-permute-start.30) | collective-permute-done | bytes 344096 | tf_op jit(solution)/shard_map/ppermute | solution.py:993
  163.4 20.0 %feed.2 = (f32[512,768]{1,0:T(8,128)}, f32[512,768]{1,0:T(8,128)}, bf16[512,768]{1,0:T(8,128)(2,1)}, bf16[4,512,768]{2,1,0:T(8,128)(2,1)}, bf16[4,512,768]{2,1,0:T(8,128)(2,1)}) custom-call(s32[8]{0:T(128)} %stack.140.idx, f32[512,768]{1,0:T(8,128)} %maximum_convert_fusion.x, bf16[512,768]{1,0:T(8,128)(2,1)} %get-tuple-element.361.o, ...), custom_call_target="tpu_custom_call" | custom-call | flops 1000 | bytes 1000 | tf_op jit(solution)/shard_map/feed/pallas_call | solution.py:140
  194.2 8.2 %project.3 = (bf16[512,768]{1,0:T(8,128)(2,1)}, bf16[512,768]{1,0:T(8,128)(2,1)}, bf16[512,1536]{1,0:T(8,128)(2,1)}) custom-call(s32[8]{0:T(128)} %stack.140.idx, f32[512,768]{1,0:T(8,128)} %get-tuple-element.373.x, f32[1,768]{1,0:T(1,128)} %get-tuple-element.704.gain, f32[1,768]{1,0:T(1,128)} %get-tuple-element.686.shift, ...), custom_call_target="tpu_custom_call" | custom-call | flops 1000 | bytes 1000 | tf_op jit(solution)/shard_map/project/pallas_call | solution.py:140
  214.0 15.7 %attend_near.3 = (f32[512,768]{1,0:T(8,128)}, f32[512,128]{1,0:T(8,128)}, f32[512,128]{1,0:T(8,128)}) custom-call(s32[8]{0:T(128)} %stack.140.idx, bf16[512,768]{1,0:T(8,128)(2,1)} %get-tuple-element.378.q, bf16[512,1536]{1,0:T(8,128)(2,1)} %get-tuple-element.382.own, bf16[512,1536]{1,0:T(8,128)(2,1)} %copy-done.33), custom_call_target="tpu_custom_call" | custom-call | flops 1000 | bytes 1000 | tf_op jit(solution)/shard_map/attend_near/pallas_call | solution.py:140
  238.7 8.4 %attend_far.3 = (bf16[512,768]{1,0:T(8,128)(2,1)}, f32[12,1,512]{2,1,0:T(1,128)}) custom-call(s32[8]{0:T(128)} %stack.140.idx, bf16[512,768]{1,0:T(8,128)(2,1)} %get-tuple-element.378.q, bf16[512,1536]{1,0:T(8,128)(2,1)} %get-tuple-element.388.far, bf16[512,1536]{1,0:T(8,128)(2,1)} %copy-done.34, f32[512,768]{1,0:T(8,128)} %get-tuple-element.389.acc, ...), custom_call_target="tpu_custom_call" | custom-call | flops 1000 | bytes 1000 | tf_op jit(solution)/shard_map/attend_far/pallas_call | solution.py:140
  247.1 6.6 collective-permute-done.45.refs_1_
  258.8 20.0 %feed.3 = (f32[512,768]{1,0:T(8,128)}, f32[512,768]{1,0:T(8,128)}, bf16[512,768]{1,0:T(8,128)(2,1)}, bf16[4,512,768]{2,1,0:T(8,128)(2,1)}, bf16[4,512,768]{2,1,0:T(8,128)(2,1)}) custom-call(s32[8]{0:T(128)} %stack.140.idx, f32[512,768]{1,0:T(8,128)} %get-tuple-element.373.x, bf16[512,768]{1,0:T(8,128)(2,1)} %get-tuple-element.396.o, ...), custom_call_target="tpu_custom_call" | custom-call | flops 1000 | bytes 1000 | tf_op jit(solution)/shard_map/feed/pallas_call | solution.py:140
  284.4 18.5 %feed_back.2 = (bf16[512,768]{1,0:T(8,128)(2,1)}, bf16[4,512,768]{2,1,0:T(8,128)(2,1)}, f32[512,768]{1,0:T(8,128)}, bf16[512,768]{1,0:T(8,128)(2,1)}, bf16[512,768]{1,0:T(8,128)(2,1)}, /*index=5*/f32[8,768]{1,0:T(8,128)}) custom-call(s32[8]{0:T(128)} %stack.140.idx, f32[512,768]{1,0:T(8,128)} %maximum_convert_fusion.1.e, f32[512,768]{1,0:T(8,128)} %get-tuple-element.405.x1, ...), custom_call_target="tpu_custom_call" | custom-call | flops 1000 | bytes 1000 | tf_op jit(solution)/shard_map/feed_back/pallas_call | solution.py:140
  302.9 11.6 %feed_grads.2 = (bf16[4,4,224,768]{3,2,1,0:T(8,128)(2,1)}, bf16[4,4,224,768]{3,2,1,0:T(8,128)(2,1)}) custom-call(s32[8]{0:T(128)} %stack.140.idx, bf16[4,512,768]{2,1,0:T(8,128)(2,1)} %get-tuple-element.409.g, bf16[512,768]{1,0:T(8,128)(2,1)} %get-tuple-element.410.dm, bf16[512,768]{1,0:T(8,128)(2,1)} %get-tuple-element.411.h2, ...), custom_call_target="tpu_custom_call" | custom-call | flops 1000 | bytes 1000 | tf_op jit(solution)/shard_map/feed_grads/pallas_call | solution.py:140
  315.4 6.2 collective-permute-start.54
  321.6 10.7 %attend_back_far.2 = (f32[512,768]{1,0:T(8,128)}, bf16[512,1536]{1,0:T(8,128)(2,1)}, f32[12,1,512]{2,1,0:T(1,128)}) custom-call(s32[8]{0:T(128)} %stack.140.idx, bf16[512,768]{1,0:T(8,128)(2,1)} %get-tuple-element.378.q, bf16[512,768]{1,0:T(8,128)(2,1)} %get-tuple-element.419.do, bf16[512,768]{1,0:T(8,128)(2,1)} %get-tuple-element.396.o, ...), custom_call_target="tpu_custom_call" | custom-call | flops 1000 | bytes 1000 | tf_op jit(solution)/shard_map/attend_back_far/pallas_call | solution.py:140
  346.0 20.7 %attend_back_near.2 = (f32[512,768]{1,0:T(8,128)}, bf16[512,1536]{1,0:T(8,128)(2,1)}, bf16[512,1536]{1,0:T(8,128)(2,1)}) custom-call(s32[8]{0:T(128)} %stack.140.idx, bf16[512,768]{1,0:T(8,128)(2,1)} %get-tuple-element.378.q, bf16[512,768]{1,0:T(8,128)(2,1)} %get-tuple-element.419.do, f32[12,1,512]{2,1,0:T(1,128)} %get-tuple-element.420.lse, ...), custom_call_target="tpu_custom_call" | custom-call | flops 1000 | bytes 1000 | tf_op jit(solution)/shard_map/attend_back_near/pallas_call | solution.py:140
  377.6 14.4 %project_back.2 = (bf16[4,512,576]{2,1,0:T(8,128)(2,1)}, f32[512,768]{1,0:T(8,128)}, f32[8,768]{1,0:T(8,128)}) custom-call(s32[8]{0:T(128)} %stack.140.idx, f32[512,768]{1,0:T(8,128)} %get-tuple-element.431.dq, bf16[512,1536]{1,0:T(8,128)(2,1)} %get-tuple-element.432.dn, bf16[512,1536]{1,0:T(8,128)(2,1)} %get-tuple-element.439.dcr, ...), custom_call_target="tpu_custom_call" | custom-call | flops 1000 | bytes 1000 | tf_op jit(solution)/shard_map/project_back/pallas_call | solution.py:140
  404.7 18.8 %feed_back.3 = (bf16[512,768]{1,0:T(8,128)(2,1)}, bf16[4,512,768]{2,1,0:T(8,128)(2,1)}, f32[512,768]{1,0:T(8,128)}, bf16[512,768]{1,0:T(8,128)(2,1)}, bf16[512,768]{1,0:T(8,128)(2,1)}, /*index=5*/f32[8,768]{1,0:T(8,128)}) custom-call(s32[8]{0:T(128)} %stack.140.idx, f32[512,768]{1,0:T(8,128)} %get-tuple-element.453.e, f32[512,768]{1,0:T(8,128)} %get-tuple-element.454.x1, ...), custom_call_target="tpu_custom_call" | custom-call | flops 1000 | bytes 1000 | tf_op jit(solution)/shard_map/feed_back/pallas_call | solution.py:140
  431.2 11.6 %feed_grads.3 = (bf16[4,4,224,768]{3,2,1,0:T(8,128)(2,1)}, bf16[4,4,224,768]{3,2,1,0:T(8,128)(2,1)}) custom-call(s32[8]{0:T(128)} %stack.140.idx, bf16[4,512,768]{2,1,0:T(8,128)(2,1)} %get-tuple-element.469.g, bf16[512,768]{1,0:T(8,128)(2,1)} %get-tuple-element.470.dm, bf16[512,768]{1,0:T(8,128)(2,1)} %get-tuple-element.471.h2, ...), custom_call_target="tpu_custom_call" | custom-call | flops 1000 | bytes 1000 | tf_op jit(solution)/shard_map/feed_grads/pallas_call | solution.py:140
  452.8 10.7 %attend_back_far.3 = (f32[512,768]{1,0:T(8,128)}, bf16[512,1536]{1,0:T(8,128)(2,1)}, f32[12,1,512]{2,1,0:T(1,128)}) custom-call(s32[8]{0:T(128)} %stack.140.idx, bf16[512,768]{1,0:T(8,128)(2,1)} %get-tuple-element.332.q, bf16[512,768]{1,0:T(8,128)(2,1)} %get-tuple-element.476.do, bf16[512,768]{1,0:T(8,128)(2,1)} %get-tuple-element.361.o, ...), custom_call_target="tpu_custom_call" | custom-call | flops 1000 | bytes 1000 | tf_op jit(solution)/shard_map/attend_back_far/pallas_call | solution.py:140
  479.6 21.1 %attend_back_near.3 = (f32[512,768]{1,0:T(8,128)}, bf16[512,1536]{1,0:T(8,128)(2,1)}, bf16[512,1536]{1,0:T(8,128)(2,1)}) custom-call(s32[8]{0:T(128)} %stack.140.idx, bf16[512,768]{1,0:T(8,128)(2,1)} %get-tuple-element.332.q, bf16[512,768]{1,0:T(8,128)(2,1)} %get-tuple-element.476.do, f32[12,1,512]{2,1,0:T(1,128)} %get-tuple-element.477.lse, ...), custom_call_target="tpu_custom_call" | custom-call | flops 1000 | bytes 1000 | tf_op jit(solution)/shard_map/attend_back_near/pallas_call | solution.py:140
  513.7 14.4 %project_back.3 = (bf16[4,512,576]{2,1,0:T(8,128)(2,1)}, f32[512,768]{1,0:T(8,128)}, f32[8,768]{1,0:T(8,128)}) custom-call(s32[8]{0:T(128)} %stack.140.idx, f32[512,768]{1,0:T(8,128)} %get-tuple-element.496.dq, bf16[512,1536]{1,0:T(8,128)(2,1)} %get-tuple-element.497.dn, bf16[512,1536]{1,0:T(8,128)(2,1)} %get-tuple-element.506.dcr, ...), custom_call_target="tpu_custom_call" | custom-call | flops 1000 | bytes 1000 | tf_op jit(solution)/shard_map/project_back/pallas_call | solution.py:140
  531.3 6.1 project_grads.3
  570.2 8.7 %collective-permute-done.85.refs_3_ = bf16[4,96,576]{2,1,0:T(8,128)(2,1)S(1)} collective-permute-done((bf16[4,96,576]{2,1,0:T(8,128)(2,1)S(1)}, bf16[4,96,576]{2,1,0:T(8,128)(2,1)S(1)}, u32[]{:S(2)}, u32[]{:S(2)}) %collective-permute-start.85) | collective-permute-done | bytes 442400 | tf_op jit(solution)/shard_map/ppermute | solution.py:997
  (736 shorter events, 336.4 us)
Async XLA Ops:
  38.2 28.0 %collective-permute-start.12 = (bf16[224,768]{1,0:T(8,128)(2,1)}, bf16[224,768]{1,0:T(8,128)(2,1)S(1)}, u32[]{:S(2)}, u32[]{:S(2)}) collective-permute-start(bf16[224,768]{1,0:T(8,128)(2,1)} %get-tuple-element.321.refs_6_), channel_id=1, source_target_pairs={{0,2},{1,3},{2,0},{3,1},{4,6},{5,7},{6,4},{7,5},{8,10},{9,11},{10,... | collective-permute-start | bytes 1032200 | tf_op jit(solution)/shard_map/ppermute | solution.py:993
  39.5 26.7 %collective-permute-start.8 = (bf16[4,96,576]{2,1,0:T(8,128)(2,1)}, bf16[4,96,576]{2,1,0:T(8,128)(2,1)S(1)}, u32[]{:S(2)}, u32[]{:S(2)}) collective-permute-start(bf16[4,96,576]{2,1,0:T(8,128)(2,1)} %get-tuple-element.318.refs_0_), channel_id=1, source_target_pairs={{0,16},{4,12},{8,24},{12,4},{16,0},{20,28},{24,8},{28,20},{1,17},{... | collective-permute-start | bytes 1327112 | tf_op jit(solution)/shard_map/ppermute | solution.py:1001
  41.0 25.2 %collective-permute-start.9 = (bf16[4,96,576]{2,1,0:T(8,128)(2,1)}, bf16[4,96,576]{2,1,0:T(8,128)(2,1)S(1)}, u32[]{:S(2)}, u32[]{:S(2)}) collective-permute-start(bf16[4,96,576]{2,1,0:T(8,128)(2,1)} %get-tuple-element.319.refs_1_), channel_id=1, source_target_pairs={{0,16},{4,12},{8,24},{12,4},{16,0},{20,28},{24,8},{28,20},{1,17},{... | collective-permute-start | bytes 1327112 | tf_op jit(solution)/shard_map/ppermute | solution.py:1001
  85.4 22.9 %collective-permute-start.19 = (bf16[512,1536]{1,0:T(8,128)(2,1)}, bf16[512,1536]{1,0:T(8,128)(2,1)}, u32[]{:S(2)}, u32[]{:S(2)}) collective-permute-start(bf16[512,1536]{1,0:T(8,128)(2,1)} %get-tuple-element.336.own), channel_id=1, source_target_pairs={{4,5},{5,4},{6,7},{7,6},{12,13},{13,12},{14,15},{15,14},{20,21},{2... | collective-permute-start | bytes 4718600 | tf_op jit(solution)/shard_map/ppermute | solution.py:1151
  154.3 29.3 %collective-permute-start.35 = (bf16[2,224,768]{2,1,0:T(8,128)(2,1)S(1)}, bf16[2,224,768]{2,1,0:T(8,128)(2,1)S(1)}, u32[]{:S(2)}, u32[]{:S(2)}) collective-permute-start(bf16[2,224,768]{2,1,0:T(8,128)(2,1)S(1)} %pad_maximum_fusion.3.refs_5_), channel_id=1, source_target_pairs={{0,1},{1,0},{2,3},{3,2},{4,5},{5,4},{6,7},{7,6},{8,9},{9,8},{10,11... | collective-permute-start | bytes 2064392 | tf_op jit(solution)/shard_map/ppermute | solution.py:993
  156.4 27.1 %collective-permute-start.34 = (bf16[4,96,576]{2,1,0:T(8,128)(2,1)S(1)}, bf16[4,96,576]{2,1,0:T(8,128)(2,1)S(1)}, u32[]{:S(2)}, u32[]{:S(2)}) collective-permute-start(bf16[4,96,576]{2,1,0:T(8,128)(2,1)S(1)} %pad_maximum_fusion.5.refs_1_), channel_id=1, source_target_pairs={{0,24},{4,28},{8,16},{12,20},{16,8},{20,12},{24,0},{28,4},{1,25},{... | collective-permute-start | bytes 1327112 | tf_op jit(solution)/shard_map/ppermute | solution.py:989
  158.9 24.6 %collective-permute-start.33 = (bf16[4,96,576]{2,1,0:T(8,128)(2,1)S(1)}, bf16[4,96,576]{2,1,0:T(8,128)(2,1)S(1)}, u32[]{:S(2)}, u32[]{:S(2)}) collective-permute-start(bf16[4,96,576]{2,1,0:T(8,128)(2,1)S(1)} %pad_maximum_fusion.5.refs_1_), channel_id=1, source_target_pairs={{0,16},{4,12},{8,24},{12,4},{16,0},{20,28},{24,8},{28,20},{1,17},{... | collective-permute-start | bytes 1327112 | tf_op jit(solution)/shard_map/ppermute | solution.py:1001
  159.4 24.1 %collective-permute-start.32 = (bf16[4,96,576]{2,1,0:T(8,128)(2,1)S(1)}, bf16[4,96,576]{2,1,0:T(8,128)(2,1)S(1)}, u32[]{:S(2)}, u32[]{:S(2)}) collective-permute-start(bf16[4,96,576]{2,1,0:T(8,128)(2,1)S(1)} %pad_maximum_fusion.5.refs_1_), channel_id=1, source_target_pairs={{0,8},{4,20},{8,0},{12,28},{16,24},{20,4},{24,16},{28,12},{1,9},{5... | collective-permute-start | bytes 1327112 | tf_op jit(solution)/shard_map/ppermute | solution.py:997
  255.0 23.8 %collective-permute-start.51 = (bf16[256,768]{1,0:T(8,128)(2,1)S(1)}, bf16[256,768]{1,0:T(8,128)(2,1)S(1)}, u32[]{:S(2)}, u32[]{:S(2)}) collective-permute-start(bf16[256,768]{1,0:T(8,128)(2,1)S(1)} %get-tuple-element.661), channel_id=1, source_target_pairs={{0,1},{1,0},{2,5},{3,4},{4,3},{5,2},{6,7},{7,6},{8,9},{9,8},{10,13... | collective-permute-start | bytes 1179656 | tf_op jit(solution)/shard_map/ppermute | solution.py:1142
  256.3 22.6 %collective-permute-start.50 = (bf16[256,768]{1,0:T(8,128)(2,1)S(1)}, bf16[256,768]{1,0:T(8,128)(2,1)S(1)}, u32[]{:S(2)}, u32[]{:S(2)}) collective-permute-start(bf16[256,768]{1,0:T(8,128)(2,1)S(1)} %get-tuple-element.662), channel_id=1, source_target_pairs={{0,0},{1,1},{2,4},{3,5},{4,2},{5,3},{6,6},{7,7},{8,8},{9,9},{10,12... | collective-permute-start | bytes 1179656 | tf_op jit(solution)/shard_map/ppermute | solution.py:1137
  281.3 33.2 %collective-permute-start.53 = (bf16[256,768]{1,0:T(8,128)(2,1)S(1)}, bf16[256,768]{1,0:T(8,128)(2,1)S(1)}, u32[]{:S(2)}, u32[]{:S(2)}) collective-permute-start(bf16[256,768]{1,0:T(8,128)(2,1)S(1)} %get-tuple-element.659), channel_id=1, source_target_pairs={{0,1},{1,0},{2,5},{3,4},{4,3},{5,2},{6,7},{7,6},{8,9},{9,8},{10,13... | collective-permute-start | bytes 1179656 | tf_op jit(solution)/shard_map/ppermute | solution.py:1142
  282.2 32.3 %collective-permute-start.52 = (bf16[256,768]{1,0:T(8,128)(2,1)S(1)}, bf16[256,768]{1,0:T(8,128)(2,1)S(1)}, u32[]{:S(2)}, u32[]{:S(2)}) collective-permute-start(bf16[256,768]{1,0:T(8,128)(2,1)S(1)} %get-tuple-element.660), channel_id=1, source_target_pairs={{0,0},{1,1},{2,4},{3,5},{4,2},{5,3},{6,6},{7,7},{8,8},{9,9},{10,12... | collective-permute-start | bytes 1179656 | tf_op jit(solution)/shard_map/ppermute | solution.py:1137
  343.1 23.6 %collective-permute-start.56 = (bf16[512,1536]{1,0:T(8,128)(2,1)S(1)}, bf16[512,1536]{1,0:T(8,128)(2,1)S(1)}, u32[]{:S(2)}, u32[]{:S(2)}) collective-permute-start(bf16[512,1536]{1,0:T(8,128)(2,1)S(1)} %add_convert_fusion.1), channel_id=1, source_target_pairs={{4,5},{5,4},{6,7},{7,6},{12,13},{13,12},{14,15},{15,14},{20,21},{2... | collective-permute-start | bytes 4718600 | tf_op jit(solution)/shard_map/ppermute | solution.py:1151
  343.9 22.8 %collective-permute-start.57 = (bf16[4,224,768]{2,1,0:T(8,128)(2,1)S(1)}, bf16[4,224,768]{2,1,0:T(8,128)(2,1)S(1)}, u32[]{:S(2)}, u32[]{:S(2)}) collective-permute-start(bf16[4,224,768]{2,1,0:T(8,128)(2,1)S(1)} %copy-done.46), channel_id=1, source_target_pairs={{0,8},{4,20},{8,0},{12,28},{16,24},{20,4},{24,16},{28,12},{1,9},{5... | collective-permute-start | bytes 4128776 | tf_op jit(solution)/shard_map/ppermute | solution.py:997
  344.8 47.2 %collective-permute-start.59 = (bf16[4,224,768]{2,1,0:T(8,128)(2,1)}, bf16[4,224,768]{2,1,0:T(8,128)(2,1)S(1)}, u32[]{:S(2)}, u32[]{:S(2)}) collective-permute-start(bf16[4,224,768]{2,1,0:T(8,128)(2,1)} %get-tuple-element.446), channel_id=1, source_target_pairs={{0,8},{4,20},{8,0},{12,28},{16,24},{20,4},{24,16},{28,12},{1,9},{5... | collective-permute-start | bytes 4128776 | tf_op jit(solution)/shard_map/ppermute | solution.py:997
  400.4 23.2 %collective-permute-start.62 = (bf16[4,4,96,576]{3,2,1,0:T(8,128)(2,1)}, bf16[4,4,96,576]{3,2,1,0:T(8,128)(2,1)S(1)}, u32[]{:S(2)}, u32[]{:S(2)}) collective-permute-start(bf16[4,4,96,576]{3,2,1,0:T(8,128)(2,1)} %get-tuple-element.463), channel_id=1, source_target_pairs={{0,4},{4,0},{8,12},{12,8},{16,20},{20,16},{24,28},{28,24},{1,5},{5... | collective-permute-start | bytes 5308424 | tf_op jit(solution)/shard_map/ppermute | solution.py:989
  474.7 26.5 %collective-permute-start.69 = (bf16[512,1536]{1,0:T(8,128)(2,1)S(1)}, bf16[512,1536]{1,0:T(8,128)(2,1)S(1)}, u32[]{:S(2)}, u32[]{:S(2)}) collective-permute-start(bf16[512,1536]{1,0:T(8,128)(2,1)S(1)} %add_convert_fusion), channel_id=1, source_target_pairs={{4,5},{5,4},{6,7},{7,6},{12,13},{13,12},{14,15},{15,14},{20,21},{2... | collective-permute-start | bytes 4718600 | tf_op jit(solution)/shard_map/ppermute | solution.py:1151
  475.4 25.7 %collective-permute-start.70 = (bf16[4,224,768]{2,1,0:T(8,128)(2,1)S(1)}, bf16[4,224,768]{2,1,0:T(8,128)(2,1)S(1)}, u32[]{:S(2)}, u32[]{:S(2)}) collective-permute-start(bf16[4,224,768]{2,1,0:T(8,128)(2,1)S(1)} %copy-done.45), channel_id=1, source_target_pairs={{0,8},{4,20},{8,0},{12,28},{16,24},{20,4},{24,16},{28,12},{1,9},{5... | collective-permute-start | bytes 4128776 | tf_op jit(solution)/shard_map/ppermute | solution.py:997
  476.1 24.5 %collective-permute-start.71 = (bf16[224,768]{1,0:T(8,128)(2,1)S(1)}, bf16[224,768]{1,0:T(8,128)(2,1)S(1)}, u32[]{:S(2)}, u32[]{:S(2)}) collective-permute-start(bf16[224,768]{1,0:T(8,128)(2,1)S(1)} %copy-done.10), channel_id=1, source_target_pairs={{0,16},{4,12},{8,24},{12,4},{16,0},{20,28},{24,8},{28,20},{1,17},{... | collective-permute-start | bytes 1032200 | tf_op jit(solution)/shard_map/ppermute | solution.py:1001
  477.6 23.1 %collective-permute-start.72 = (bf16[224,768]{1,0:T(8,128)(2,1)S(1)}, bf16[224,768]{1,0:T(8,128)(2,1)S(1)}, u32[]{:S(2)}, u32[]{:S(2)}) collective-permute-start(bf16[224,768]{1,0:T(8,128)(2,1)S(1)} %copy-done.21), channel_id=1, source_target_pairs={{0,16},{4,12},{8,24},{12,4},{16,0},{20,28},{24,8},{28,20},{1,17},{... | collective-permute-start | bytes 1032200 | tf_op jit(solution)/shard_map/ppermute | solution.py:1001
  478.2 50.0 %collective-permute-start.74 = (bf16[4,224,768]{2,1,0:T(8,128)(2,1)}, bf16[4,224,768]{2,1,0:T(8,128)(2,1)}, u32[]{:S(2)}, u32[]{:S(2)}) collective-permute-start(bf16[4,224,768]{2,1,0:T(8,128)(2,1)} %get-tuple-element.513), channel_id=1, source_target_pairs={{0,8},{4,20},{8,0},{12,28},{16,24},{20,4},{24,16},{28,12},{1,9},{5... | collective-permute-start | bytes 4128776 | tf_op jit(solution)/shard_map/ppermute | solution.py:997
  507.8 22.3 %collective-permute-start.75 = (bf16[4,224,768]{2,1,0:T(8,128)(2,1)S(1)}, bf16[4,224,768]{2,1,0:T(8,128)(2,1)S(1)}, u32[]{:S(2)}, u32[]{:S(2)}) collective-permute-start(bf16[4,224,768]{2,1,0:T(8,128)(2,1)S(1)} %fusion.2), channel_id=1, source_target_pairs={{0,16},{4,12},{8,24},{12,4},{16,0},{20,28},{24,8},{28,20},{1,17},{... | collective-permute-start | bytes 4128776 | tf_op jit(solution)/shard_map/ppermute | solution.py:1001
  546.6 21.7 %collective-permute-start.87 = (bf16[2,224,768]{2,1,0:T(8,128)(2,1)}, bf16[2,224,768]{2,1,0:T(8,128)(2,1)}, u32[]{:S(2)}, u32[]{:S(2)}) collective-permute-start(bf16[2,224,768]{2,1,0:T(8,128)(2,1)} %slice.486), channel_id=1, source_target_pairs={{0,1},{1,0},{2,3},{3,2},{4,5},{5,4},{6,7},{7,6},{8,9},{9,8},{10,11... | collective-permute-start | bytes 2064392 | tf_op jit(solution)/shard_map/ppermute | solution.py:993
  556.5 22.4 %collective-permute-start.85 = (bf16[4,96,576]{2,1,0:T(8,128)(2,1)S(1)}, bf16[4,96,576]{2,1,0:T(8,128)(2,1)S(1)}, u32[]{:S(2)}, u32[]{:S(2)}) collective-permute-start(bf16[4,96,576]{2,1,0:T(8,128)(2,1)S(1)} %get-tuple-element.655), channel_id=1, source_target_pairs={{0,8},{4,20},{8,0},{12,28},{16,24},{20,4},{24,16},{28,12},{1,9},{5... | collective-permute-start | bytes 1327112 | tf_op jit(solution)/shard_map/ppermute | solution.py:997
  (269 other events, 1752.2 us)

commit v5 on v4

--- a/solution.py
+++ b/solution.py
@@ -1134,16 +1134,20 @@
 
 def relocate_first(rows):
     pairs = device_pairs(lambda w, z: ((w & ~1) | (z >> 1), ((w & 1) << 1) | (z & 1)))
-    return lax.ppermute(rows[:HALF], BOTH, pairs)
+    return lax.ppermute(rows, BOTH, pairs)
 
 
 def relocate_second(rows):
     pairs = device_pairs(lambda w, z: ((w & ~1) | (z >> 1), ((w & 1) << 1) | (1 - (z & 1))))
-    return lax.ppermute(rows[HALF:], BOTH, pairs)
+    return lax.ppermute(rows, BOTH, pairs)
 
 
 def relocate(rows):
-    return relocate_first(rows), relocate_second(rows)
+    return relocate_halves((rows[:HALF], rows[HALF:]))
+
+
+def relocate_halves(halves):
+    return relocate_first(halves[0]), relocate_second(halves[1])
 
 
 def between_chips(x):
@@ -1212,33 +1216,33 @@
     mixer0 = gather_direct(mixer_piece(0))
     feed0, feed1 = pack(idx, up_weight, down_weight, output_weight)
     biases = [biases] + [flip_narrow(biases, k) for k in (1, 2, 3)]
-    mixer0, tokens, feed0, biases = gate((mixer0, tokens, feed0, biases))
+    halves = tokens[:HALF], tokens[HALF:]
+    mixer0, halves, feed0, biases = gate((mixer0, halves, feed0, biases))
     mixer0 = gather_first(whole(mixer0))
-    rows = relocate(tokens)
-    mixer0, feed0 = gate((mixer0, feed0))
+    feed0 = gather_far(feed0)
+    mixer0, feed0, halves, mixer1 = gate((mixer0, feed0, halves, mixer_piece(1)))
     own, first = mixer0
     mixer0 = [own, first, second_axis(own), second_axis(first)]
-    feed0 = gather_far(feed0)
-    mixer0, rows, feed0 = gate((mixer0, rows, feed0))
+    rows = relocate_halves(halves)
+    feed0 = gather_near(feed0)
+    mixer0, rows, feed0, mixer1 = gate((mixer0, rows, feed0, mixer1))
     mixer0 = gather_last(mixer0)
-    feed0 = gather_near(feed0)
+    own, first = gather_first(whole(feed0))
+    mixer1 = gather_far(mixer1)
     x0 = jnp.concatenate(rows).astype(F32)
     h1_0, q_0, kv = run_project(0, x0, mixer0)
-    own_0, feed0 = gate((kv, feed0))
+    own_0, own, first, mixer1 = gate((kv, own, first, mixer1))
     near_0, far = within_chip(own_0, 1), between_chips(own_0)
-    own, first = gather_first(whole(feed0))
-    mixer1 = mixer_piece(1)
+    second = second_axis(own)
+    others = [flip_wide(own, 1), flip_wide(first, 1)]
     state = attend_near(idx, q_0, own_0, near_0)
-    state, far_0, own, first, mixer1, feed1 = gate((state, far, own, first, mixer1, feed1))
+    state, far_0, first, second, others, mixer1, feed1 = gate((state, far, first, second, others, mixer1, feed1))
     far_near_0 = within_chip(far_0, 1)
-    second = second_axis(own)
-    mixer1 = gather_direct(mixer1)
+    third = second_axis(first)
+    others = others + [flip_wide(second, 1)]
+    mixer1, feed1 = gather_near(mixer1), gather_far(feed1)
     o_0, lse_0 = attend_far(idx, q_0, far_0, far_near_0, state)
-    o_0, own, first, second, mixer1, feed1 = gate((o_0, own, first, second, mixer1, feed1))
-    third = second_axis(first)
-    others = [flip_wide(own, 1), flip_wide(first, 1), flip_wide(second, 1)]
-    feed1 = gather_far(feed1)
-    third, others, o_0, mixer1, feed1 = gate((third, others, o_0, mixer1, feed1))
+    o_0, third, others, mixer1, feed1 = gate((o_0, third, others, mixer1, feed1))
     feed0 = [own, first, second, third] + others + [flip_wide(third, 1)]
     mixer1, feed1 = gather_plane(whole(mixer1)), gather_near(feed1)
     x1, x1_0, h2_0, g_0, gp_0 = run_feed(0, x0, o_0, feed0)
@@ -1255,8 +1259,8 @@
     third = second_axis(first)
     others = [flip_wide(own, 1), flip_wide(first, 1), flip_wide(second, 1)]
     o_1, lse_1 = attend_far(idx, q_1, far_1, far_near_1, state)
-    o_1, third, others, cotangent = gate((o_1, third, others, cotangent))
-    e = relocate(cotangent)
+    o_1, third, others, halves = gate((o_1, third, others, (cotangent[:HALF], cotangent[HALF:])))
+    e = relocate_halves(halves)
     feed1 = [own, first, second, third] + others + [flip_wide(third, 1)]
     x2, x1_1, h2_1, g_1, gp_1 = run_feed(1, x1, o_1, feed1)
     x2, e = gate((x2, e))
@@ -1315,7 +1319,7 @@
     smalls = smalls, flip_wide(smalls, 1)
     g_mixer0, smalls, e, g_feed1, g_mixer1 = gate((g_mixer0, smalls, e, g_feed1, g_mixer1))
     g_mixer0 = reduce_plane(g_mixer0)
-    early, e_late = relocate_first(e.astype(BF)), e
+    early, e_late = relocate_first(e[:HALF].astype(BF)), e
     feed_out = finish_feed(idx, 1, layers, g_feed1, None)
     g_mixer0, g_feed0, smalls, feed_out, early, e_late, g_mixer1 = gate(
         (g_mixer0, g_feed0, smalls, feed_out, early, e_late, g_mixer1)
@@ -1331,12 +1335,15 @@
     smalls = smalls[0] + smalls[1]
     smalls = smalls, first_axis(smalls)
     g_mixer1 = spread_first(g_mixer1)
-    g_mixer0, g_feed0, smalls, g_mixer1 = gate((g_mixer0, g_feed0, smalls, g_mixer1))
+    g_mixer0, g_feed0, smalls, g_mixer1, e_late = gate((g_mixer0, g_feed0, smalls, g_mixer1, e_late))
     g_mixer0, g_feed0 = reduce_far(g_mixer0), spread_first(g_feed0)
     smalls = smalls[0] + smalls[1]
     smalls = smalls, second_axis(smalls)
-    g_mixer1 = gather_second(g_mixer1)
-    g_mixer0, g_feed0, smalls, g_mixer1 = gate((g_mixer0, g_feed0, smalls, g_mixer1))
+    own, first = g_mixer1
+    both = second_axis(jnp.stack([own, first]))
+    late = relocate_second(e_late[HALF:].astype(BF))
+    g_mixer0, g_feed0, smalls, own, first, both, late = gate((g_mixer0, g_feed0, smalls, own, first, both, late))
+    g_mixer1 = [own, first, both[0], both[1]]
     g_mixer0, g_feed0 = spread_first(g_mixer0), gather_second(g_feed0)
     smalls = smalls[0] + smalls[1]
     bit = 8
@@ -1346,13 +1353,12 @@
     smalls = smalls, flip_narrow(smalls, 1)
     g_mixer1 = gather_last(g_mixer1)
     mixer_out = finish_mixer(idx, 1, layers, g_mixer1, None)
-    g_mixer0, g_feed0, smalls, e_late, mixer_out = gate((g_mixer0, g_feed0, smalls, e_late, mixer_out))
+    g_mixer0, g_feed0, smalls, mixer_out = gate((g_mixer0, g_feed0, smalls, mixer_out))
     g_mixer0, g_feed0 = gather_second(g_mixer0), gather_last(g_feed0)
-    late = relocate_second(e_late.astype(BF))
     smalls = smalls[0] + smalls[1]
     smalls = smalls, flip_narrow(smalls, 2)
     feed_out = finish_feed(idx, 0, layers, g_feed0, feed_out)
-    g_mixer0, smalls, late, feed_out = gate((g_mixer0, smalls, late, feed_out))
+    g_mixer0, smalls, feed_out = gate((g_mixer0, smalls, feed_out))
     smalls = smalls[0] + smalls[1]
     g_mixer0 = gather_last(g_mixer0)
     mixer_out = finish_mixer(idx, 0, layers, g_mixer0, mixer_out)

time: 675 us -> 664 us (0.984)
  waiting for transfers between devices: 117 us -> 109 us
    ppermute x8, waiting for transfers between devices: 0.72 us -> 15.3 us  [the longest x4 15.3 us: relocate_second(): return lax.ppermute(rows, BOTH, pairs)]
    ppermute x23 -> x22, waiting for transfers between devices: 62 us -> 48.4 us  [flip_narrow(): return lax.ppermute(x, 'narrow', [(i, i ^ bit) for i in range(QUARTERS)])]
    ppermute x23 -> x22, starting transfers between devices: 30.9 us -> 22.9 us  [flip_narrow(): return lax.ppermute(x, 'narrow', [(i, i ^ bit) for i in range(QUARTERS)])]
    unnamed x360 -> x383, local copies, waits for them, and re-layouts: 54.2 us -> 48.3 us
    ppermute x20 -> x19, starting transfers between devices: 21.3 us -> 21.1 us  [second_axis(): lax.ppermute(x, 'wide', [(i, i ^ (2 if i & 1 else 4)) for i in range(lax....]
    ppermute x20 -> x19, waiting for transfers between devices: 19.6 us -> 19.5 us  [second_axis(): lax.ppermute(x, 'wide', [(i, i ^ (2 if i & 1 else 4)) for i in range(lax....]
  transfers between devices with their start and end apart: 118 -> 116, of which waited for: 35 -> 31; matrix products, arithmetic and copies ran while one was open for 10% -> 10% of each run, Pallas kernels for 41% -> 42%
where the time goes in v5:
time: 664 us; the launch traced here: 654 us
  Pallas kernels  286 us (43%)
  starting transfers between devices  116 us (17%)
  waiting for transfers between devices  109 us (16%)
  local copies, waits for them, and re-layouts  74 us (11%)
  other arithmetic  63.8 us (10%)
    pallas_call x25, Pallas kernels, kernel_call(): pl.pallas_call(body, in_specs=in_specs, out_specs=out_specs, out_shape=ou...  286 us
    ppermute x22, waiting for transfers between devices, flip_narrow(): return lax.ppermute(x, 'narrow', [(i, i ^ bit) for i in range(QUARTERS)])  48.4 us
    unnamed x383, local copies, waits for them, and re-layouts  48.3 us
    convert_element_type x21, other arithmetic, added(): return functools.reduce(jnp.add, [t.astype(F32) for t in terms]).astype(BF)  43.3 us
    ppermute x40, starting transfers between devices, flip_wide(): lax.ppermute(x, 'wide', [(i, i ^ bit) for i in range(lax.axis_size('wide'...  26.2 us
    ppermute x22, starting transfers between devices, flip_narrow(): return lax.ppermute(x, 'narrow', [(i, i ^ bit) for i in range(QUARTERS)])  22.9 us
    ppermute x19, starting transfers between devices, second_axis(): lax.ppermute(x, 'wide', [(i, i ^ (2 if i & 1 else 4)) for i in range(lax....  21.1 us
    ppermute x19, waiting for transfers between devices, second_axis(): lax.ppermute(x, 'wide', [(i, i ^ (2 if i & 1 else 4)) for i in range(lax....  19.5 us
  transfers between devices with their start and end apart: 116, of which 31 were waited for; matrix products, arithmetic and copies ran while one was open for 10% of the time, Pallas kernels for 42%

profile of v5, /device:TPU:0, one launch (start us, length us, event | category | flops | bytes accessed | tf_op | source)
XLA Modules:
  0.0 653.8 jit_solution(9867952937746794701)
XLA Ops:
  30.2 15.8 %collective-permute-done.8.refs_3_ = bf16[224,768]{1,0:T(8,128)(2,1)S(1)} collective-permute-done((bf16[224,768]{1,0:T(8,128)(2,1)}, bf16[224,768]{1,0:T(8,128)(2,1)S(1)}, u32[]{:S(2)}, u32[]{:S(2)}) %collective-permute-start.8) | collective-permute-done | bytes 344096 | tf_op jit(solution)/shard_map/ppermute | solution.py:993
  58.7 15.3 %collective-permute-done.12.refs_5_ = bf16[256,768]{1,0:T(8,128)(2,1)} collective-permute-done((bf16[256,768]{1,0:T(8,128)(2,1)}, bf16[256,768]{1,0:T(8,128)(2,1)}, u32[]{:S(2)}, u32[]{:S(2)}) %collective-permute-start.12) | collective-permute-done | bytes 393248 | tf_op jit(solution)/shard_map/ppermute | solution.py:1142
  88.6 8.3 %project.2 = (bf16[512,768]{1,0:T(8,128)(2,1)}, bf16[512,768]{1,0:T(8,128)(2,1)}, bf16[512,1536]{1,0:T(8,128)(2,1)}) custom-call(s32[8]{0:T(128)} %stack.143.idx, f32[512,768]{1,0:T(8,128)} %maximum_convert_fusion.x, f32[1,768]{1,0:T(1,128)} %get-tuple-element.707.gain, f32[1,768]{1,0:T(1,128)} %get-tuple-element.687.shift, ...), custom_call_target="tpu_custom_call" | custom-call | flops 1000 | bytes 1000 | tf_op jit(solution)/shard_map/project/pallas_call | solution.py:140
  107.9 15.3 %attend_near.2 = (f32[512,768]{1,0:T(8,128)}, f32[512,128]{1,0:T(8,128)}, f32[512,128]{1,0:T(8,128)}) custom-call(s32[8]{0:T(128)} %stack.143.idx, bf16[512,768]{1,0:T(8,128)(2,1)} %get-tuple-element.337.q, bf16[512,1536]{1,0:T(8,128)(2,1)} %get-tuple-element.342.own, bf16[512,1536]{1,0:T(8,128)(2,1)} %copy-done.32), custom_call_target="tpu_custom_call" | custom-call | flops 1000 | bytes 1000 | tf_op jit(solution)/shard_map/attend_near/pallas_call | solution.py:140
  134.6 8.6 %attend_far.2 = (bf16[512,768]{1,0:T(8,128)(2,1)}, f32[12,1,512]{2,1,0:T(1,128)}) custom-call(s32[8]{0:T(128)} %stack.143.idx, bf16[512,768]{1,0:T(8,128)(2,1)} %get-tuple-element.337.q, bf16[512,1536]{1,0:T(8,128)(2,1)} %get-tuple-element.351.far, bf16[512,1536]{1,0:T(8,128)(2,1)} %copy-done.33, f32[512,768]{1,0:T(8,128)} %get-tuple-element.352.acc, ...), custom_call_target="tpu_custom_call" | custom-call | flops 1000 | bytes 1000 | tf_op jit(solution)/shard_map/attend_far/pallas_call | solution.py:140
  155.6 20.0 %feed.2 = (f32[512,768]{1,0:T(8,128)}, f32[512,768]{1,0:T(8,128)}, bf16[512,768]{1,0:T(8,128)(2,1)}, bf16[4,512,768]{2,1,0:T(8,128)(2,1)}, bf16[4,512,768]{2,1,0:T(8,128)(2,1)}) custom-call(s32[8]{0:T(128)} %stack.143.idx, f32[512,768]{1,0:T(8,128)} %maximum_convert_fusion.x, bf16[512,768]{1,0:T(8,128)(2,1)} %get-tuple-element.363.o, ...), custom_call_target="tpu_custom_call" | custom-call | flops 1000 | bytes 1000 | tf_op jit(solution)/shard_map/feed/pallas_call | solution.py:140
  186.2 8.2 %project.3 = (bf16[512,768]{1,0:T(8,128)(2,1)}, bf16[512,768]{1,0:T(8,128)(2,1)}, bf16[512,1536]{1,0:T(8,128)(2,1)}) custom-call(s32[8]{0:T(128)} %stack.143.idx, f32[512,768]{1,0:T(8,128)} %get-tuple-element.373.x, f32[1,768]{1,0:T(1,128)} %get-tuple-element.706.gain, f32[1,768]{1,0:T(1,128)} %get-tuple-element.688.shift, ...), custom_call_target="tpu_custom_call" | custom-call | flops 1000 | bytes 1000 | tf_op jit(solution)/shard_map/project/pallas_call | solution.py:140
  206.2 15.7 %attend_near.3 = (f32[512,768]{1,0:T(8,128)}, f32[512,128]{1,0:T(8,128)}, f32[512,128]{1,0:T(8,128)}) custom-call(s32[8]{0:T(128)} %stack.143.idx, bf16[512,768]{1,0:T(8,128)(2,1)} %get-tuple-element.378.q, bf16[512,1536]{1,0:T(8,128)(2,1)} %get-tuple-element.382.own, bf16[512,1536]{1,0:T(8,128)(2,1)} %copy-done.34), custom_call_target="tpu_custom_call" | custom-call | flops 1000 | bytes 1000 | tf_op jit(solution)/shard_map/attend_near/pallas_call | solution.py:140
  231.6 8.4 %attend_far.3 = (bf16[512,768]{1,0:T(8,128)(2,1)}, f32[12,1,512]{2,1,0:T(1,128)}) custom-call(s32[8]{0:T(128)} %stack.143.idx, bf16[512,768]{1,0:T(8,128)(2,1)} %get-tuple-element.378.q, bf16[512,1536]{1,0:T(8,128)(2,1)} %get-tuple-element.388.far, bf16[512,1536]{1,0:T(8,128)(2,1)} %copy-done.35, f32[512,768]{1,0:T(8,128)} %get-tuple-element.389.acc, ...), custom_call_target="tpu_custom_call" | custom-call | flops 1000 | bytes 1000 | tf_op jit(solution)/shard_map/attend_far/pallas_call | solution.py:140
  250.5 20.0 %feed.3 = (f32[512,768]{1,0:T(8,128)}, f32[512,768]{1,0:T(8,128)}, bf16[512,768]{1,0:T(8,128)(2,1)}, bf16[4,512,768]{2,1,0:T(8,128)(2,1)}, bf16[4,512,768]{2,1,0:T(8,128)(2,1)}) custom-call(s32[8]{0:T(128)} %stack.143.idx, f32[512,768]{1,0:T(8,128)} %get-tuple-element.373.x, bf16[512,768]{1,0:T(8,128)(2,1)} %get-tuple-element.396.o, ...), custom_call_target="tpu_custom_call" | custom-call | flops 1000 | bytes 1000 | tf_op jit(solution)/shard_map/feed/pallas_call | solution.py:140
  276.3 18.4 %feed_back.2 = (bf16[512,768]{1,0:T(8,128)(2,1)}, bf16[4,512,768]{2,1,0:T(8,128)(2,1)}, f32[512,768]{1,0:T(8,128)}, bf16[512,768]{1,0:T(8,128)(2,1)}, bf16[512,768]{1,0:T(8,128)(2,1)}, /*index=5*/f32[8,768]{1,0:T(8,128)}) custom-call(s32[8]{0:T(128)} %stack.143.idx, f32[512,768]{1,0:T(8,128)} %maximum_convert_fusion.1.e, f32[512,768]{1,0:T(8,128)} %get-tuple-element.406.x1, ...), custom_call_target="tpu_custom_call" | custom-call | flops 1000 | bytes 1000 | tf_op jit(solution)/shard_map/feed_back/pallas_call | solution.py:140
  294.7 11.5 %feed_grads.2 = (bf16[4,4,224,768]{3,2,1,0:T(8,128)(2,1)}, bf16[4,4,224,768]{3,2,1,0:T(8,128)(2,1)}) custom-call(s32[8]{0:T(128)} %stack.143.idx, bf16[4,512,768]{2,1,0:T(8,128)(2,1)} %get-tuple-element.410.g, bf16[512,768]{1,0:T(8,128)(2,1)} %get-tuple-element.411.dm, bf16[512,768]{1,0:T(8,128)(2,1)} %get-tuple-element.412.h2, ...), custom_call_target="tpu_custom_call" | custom-call | flops 1000 | bytes 1000 | tf_op jit(solution)/shard_map/feed_grads/pallas_call | solution.py:140
  312.7 10.7 %attend_back_far.2 = (f32[512,768]{1,0:T(8,128)}, bf16[512,1536]{1,0:T(8,128)(2,1)}, f32[12,1,512]{2,1,0:T(1,128)}) custom-call(s32[8]{0:T(128)} %stack.143.idx, bf16[512,768]{1,0:T(8,128)(2,1)} %get-tuple-element.378.q, bf16[512,768]{1,0:T(8,128)(2,1)} %get-tuple-element.420.do, bf16[512,768]{1,0:T(8,128)(2,1)} %get-tuple-element.396.o, ...), custom_call_target="tpu_custom_call" | custom-call | flops 1000 | bytes 1000 | tf_op jit(solution)/shard_map/attend_back_far/pallas_call | solution.py:140
  337.0 20.7 %attend_back_near.2 = (f32[512,768]{1,0:T(8,128)}, bf16[512,1536]{1,0:T(8,128)(2,1)}, bf16[512,1536]{1,0:T(8,128)(2,1)}) custom-call(s32[8]{0:T(128)} %stack.143.idx, bf16[512,768]{1,0:T(8,128)(2,1)} %get-tuple-element.378.q, bf16[512,768]{1,0:T(8,128)(2,1)} %get-tuple-element.420.do, f32[12,1,512]{2,1,0:T(1,128)} %get-tuple-element.421.lse, ...), custom_call_target="tpu_custom_call" | custom-call | flops 1000 | bytes 1000 | tf_op jit(solution)/shard_map/attend_back_near/pallas_call | solution.py:140
  369.5 14.4 %project_back.2 = (bf16[4,512,576]{2,1,0:T(8,128)(2,1)}, f32[512,768]{1,0:T(8,128)}, f32[8,768]{1,0:T(8,128)}) custom-call(s32[8]{0:T(128)} %stack.143.idx, f32[512,768]{1,0:T(8,128)} %get-tuple-element.432.dq, bf16[512,1536]{1,0:T(8,128)(2,1)} %get-tuple-element.433.dn, bf16[512,1536]{1,0:T(8,128)(2,1)} %get-tuple-element.440.dcr, ...), custom_call_target="tpu_custom_call" | custom-call | flops 1000 | bytes 1000 | tf_op jit(solution)/shard_map/project_back/pallas_call | solution.py:140
  395.6 18.9 %feed_back.3 = (bf16[512,768]{1,0:T(8,128)(2,1)}, bf16[4,512,768]{2,1,0:T(8,128)(2,1)}, f32[512,768]{1,0:T(8,128)}, bf16[512,768]{1,0:T(8,128)(2,1)}, bf16[512,768]{1,0:T(8,128)(2,1)}, /*index=5*/f32[8,768]{1,0:T(8,128)}) custom-call(s32[8]{0:T(128)} %stack.143.idx, f32[512,768]{1,0:T(8,128)} %get-tuple-element.454.e, f32[512,768]{1,0:T(8,128)} %get-tuple-element.455.x1, ...), custom_call_target="tpu_custom_call" | custom-call | flops 1000 | bytes 1000 | tf_op jit(solution)/shard_map/feed_back/pallas_call | solution.py:140
  422.1 11.6 %feed_grads.3 = (bf16[4,4,224,768]{3,2,1,0:T(8,128)(2,1)}, bf16[4,4,224,768]{3,2,1,0:T(8,128)(2,1)}) custom-call(s32[8]{0:T(128)} %stack.143.idx, bf16[4,512,768]{2,1,0:T(8,128)(2,1)} %get-tuple-element.470.g, bf16[512,768]{1,0:T(8,128)(2,1)} %get-tuple-element.471.dm, bf16[512,768]{1,0:T(8,128)(2,1)} %get-tuple-element.472.h2, ...), custom_call_target="tpu_custom_call" | custom-call | flops 1000 | bytes 1000 | tf_op jit(solution)/shard_map/feed_grads/pallas_call | solution.py:140
  445.3 10.7 %attend_back_far.3 = (f32[512,768]{1,0:T(8,128)}, bf16[512,1536]{1,0:T(8,128)(2,1)}, f32[12,1,512]{2,1,0:T(1,128)}) custom-call(s32[8]{0:T(128)} %stack.143.idx, bf16[512,768]{1,0:T(8,128)(2,1)} %get-tuple-element.337.q, bf16[512,768]{1,0:T(8,128)(2,1)} %get-tuple-element.477.do, bf16[512,768]{1,0:T(8,128)(2,1)} %get-tuple-element.363.o, ...), custom_call_target="tpu_custom_call" | custom-call | flops 1000 | bytes 1000 | tf_op jit(solution)/shard_map/attend_back_far/pallas_call | solution.py:140
  472.0 21.0 %attend_back_near.3 = (f32[512,768]{1,0:T(8,128)}, bf16[512,1536]{1,0:T(8,128)(2,1)}, bf16[512,1536]{1,0:T(8,128)(2,1)}) custom-call(s32[8]{0:T(128)} %stack.143.idx, bf16[512,768]{1,0:T(8,128)(2,1)} %get-tuple-element.337.q, bf16[512,768]{1,0:T(8,128)(2,1)} %get-tuple-element.477.do, f32[12,1,512]{2,1,0:T(1,128)} %get-tuple-element.478.lse, ...), custom_call_target="tpu_custom_call" | custom-call | flops 1000 | bytes 1000 | tf_op jit(solution)/shard_map/attend_back_near/pallas_call | solution.py:140
  505.1 14.4 %project_back.3 = (bf16[4,512,576]{2,1,0:T(8,128)(2,1)}, f32[512,768]{1,0:T(8,128)}, f32[8,768]{1,0:T(8,128)}) custom-call(s32[8]{0:T(128)} %stack.143.idx, f32[512,768]{1,0:T(8,128)} %get-tuple-element.497.dq, bf16[512,1536]{1,0:T(8,128)(2,1)} %get-tuple-element.498.dn, bf16[512,1536]{1,0:T(8,128)(2,1)} %get-tuple-element.507.dcr, ...), custom_call_target="tpu_custom_call" | custom-call | flops 1000 | bytes 1000 | tf_op jit(solution)/shard_map/project_back/pallas_call | solution.py:140
  523.8 6.1 project_grads.3
  562.5 8.6 %collective-permute-done.84.refs_3_ = bf16[4,96,576]{2,1,0:T(8,128)(2,1)S(1)} collective-permute-done((bf16[4,96,576]{2,1,0:T(8,128)(2,1)S(1)}, bf16[4,96,576]{2,1,0:T(8,128)(2,1)S(1)}, u32[]{:S(2)}, u32[]{:S(2)}) %collective-permute-start.84) | collective-permute-done | bytes 442400 | tf_op jit(solution)/shard_map/ppermute | solution.py:997
  585.2 6.3 collective-permute-done.88.refs_1_
  604.9 6.2 collective-permute-done.92.refs_2_
  (757 shorter events, 333.7 us)
Async XLA Ops:
  48.1 26.0 %collective-permute-start.13 = (bf16[2,224,768]{2,1,0:T(8,128)(2,1)S(1)}, bf16[2,224,768]{2,1,0:T(8,128)(2,1)S(1)}, u32[]{:S(2)}, u32[]{:S(2)}) collective-permute-start(bf16[2,224,768]{2,1,0:T(8,128)(2,1)S(1)} %pad_maximum_fusion.2.refs_6_), channel_id=1, source_target_pairs={{0,1},{1,0},{2,3},{3,2},{4,5},{5,4},{6,7},{7,6},{8,9},{9,8},{10,11... | collective-permute-start | bytes 2064392 | tf_op jit(solution)/shard_map/ppermute | solution.py:993
  49.9 24.2 %collective-permute-start.12 = (bf16[256,768]{1,0:T(8,128)(2,1)}, bf16[256,768]{1,0:T(8,128)(2,1)}, u32[]{:S(2)}, u32[]{:S(2)}) collective-permute-start(bf16[256,768]{1,0:T(8,128)(2,1)} %get-tuple-element.323), channel_id=1, source_target_pairs={{0,1},{1,0},{2,5},{3,4},{4,3},{5,2},{6,7},{7,6},{8,9},{9,8},{10,13... | collective-permute-start | bytes 1179656 | tf_op jit(solution)/shard_map/ppermute | solution.py:1142
  51.9 22.1 %collective-permute-start.9 = (bf16[4,96,576]{2,1,0:T(8,128)(2,1)}, bf16[4,96,576]{2,1,0:T(8,128)(2,1)S(1)}, u32[]{:S(2)}, u32[]{:S(2)}) collective-permute-start(bf16[4,96,576]{2,1,0:T(8,128)(2,1)} %get-tuple-element.320.refs_0_), channel_id=1, source_target_pairs={{0,16},{4,12},{8,24},{12,4},{16,0},{20,28},{24,8},{28,20},{1,17},{... | collective-permute-start | bytes 1327112 | tf_op jit(solution)/shard_map/ppermute | solution.py:1001
  99.3 25.6 %collective-permute-start.21 = (bf16[512,1536]{1,0:T(8,128)(2,1)}, bf16[512,1536]{1,0:T(8,128)(2,1)}, u32[]{:S(2)}, u32[]{:S(2)}) collective-permute-start(bf16[512,1536]{1,0:T(8,128)(2,1)} %get-tuple-element.342.own), channel_id=1, source_target_pairs={{4,5},{5,4},{6,7},{7,6},{12,13},{13,12},{14,15},{15,14},{20,21},{2... | collective-permute-start | bytes 4718600 | tf_op jit(solution)/shard_map/ppermute | solution.py:1155
  149.9 25.9 %collective-permute-start.34 = (bf16[2,224,768]{2,1,0:T(8,128)(2,1)S(1)}, bf16[2,224,768]{2,1,0:T(8,128)(2,1)S(1)}, u32[]{:S(2)}, u32[]{:S(2)}) collective-permute-start(bf16[2,224,768]{2,1,0:T(8,128)(2,1)S(1)} %pad_maximum_fusion.3.refs_5_), channel_id=1, source_target_pairs={{0,1},{1,0},{2,3},{3,2},{4,5},{5,4},{6,7},{7,6},{8,9},{9,8},{10,11... | collective-permute-start | bytes 2064392 | tf_op jit(solution)/shard_map/ppermute | solution.py:993
  150.1 25.6 %collective-permute-start.33 = (bf16[4,96,576]{2,1,0:T(8,128)(2,1)S(1)}, bf16[4,96,576]{2,1,0:T(8,128)(2,1)S(1)}, u32[]{:S(2)}, u32[]{:S(2)}) collective-permute-start(bf16[4,96,576]{2,1,0:T(8,128)(2,1)S(1)} %constant_dynamic-update-slice_fusion.2.refs_1_), channel_id=1, source_target_pairs={{0,24},{4,28},{8,16},{12,20},{16,8},{20,12},{24,0},{28,4},{1,25},{... | collective-permute-start | bytes 1327112 | tf_op jit(solution)/shard_map/ppermute | solution.py:989
  151.7 24.0 %collective-permute-start.32 = (bf16[4,96,576]{2,1,0:T(8,128)(2,1)S(1)}, bf16[4,96,576]{2,1,0:T(8,128)(2,1)S(1)}, u32[]{:S(2)}, u32[]{:S(2)}) collective-permute-start(bf16[4,96,576]{2,1,0:T(8,128)(2,1)S(1)} %constant_dynamic-update-slice_fusion.2.refs_1_), channel_id=1, source_target_pairs={{0,16},{4,12},{8,24},{12,4},{16,0},{20,28},{24,8},{28,20},{1,17},{... | collective-permute-start | bytes 1327112 | tf_op jit(solution)/shard_map/ppermute | solution.py:1001
  152.9 22.8 %collective-permute-start.31 = (bf16[4,96,576]{2,1,0:T(8,128)(2,1)S(1)}, bf16[4,96,576]{2,1,0:T(8,128)(2,1)S(1)}, u32[]{:S(2)}, u32[]{:S(2)}) collective-permute-start(bf16[4,96,576]{2,1,0:T(8,128)(2,1)S(1)} %constant_dynamic-update-slice_fusion.2.refs_1_), channel_id=1, source_target_pairs={{0,8},{4,20},{8,0},{12,28},{16,24},{20,4},{24,16},{28,12},{1,9},{5... | collective-permute-start | bytes 1327112 | tf_op jit(solution)/shard_map/ppermute | solution.py:997
  245.8 24.7 %collective-permute-start.49 = (bf16[256,768]{1,0:T(8,128)(2,1)}, bf16[256,768]{1,0:T(8,128)(2,1)S(1)}, u32[]{:S(2)}, u32[]{:S(2)}) collective-permute-start(bf16[256,768]{1,0:T(8,128)(2,1)} %get-tuple-element.402), channel_id=1, source_target_pairs={{0,0},{1,1},{2,4},{3,5},{4,2},{5,3},{6,6},{7,7},{8,8},{9,9},{10,12... | collective-permute-start | bytes 1179656 | tf_op jit(solution)/shard_map/ppermute | solution.py:1137
  247.4 23.1 %collective-permute-start.50 = (bf16[256,768]{1,0:T(8,128)(2,1)}, bf16[256,768]{1,0:T(8,128)(2,1)S(1)}, u32[]{:S(2)}, u32[]{:S(2)}) collective-permute-start(bf16[256,768]{1,0:T(8,128)(2,1)} %get-tuple-element.403), channel_id=1, source_target_pairs={{0,1},{1,0},{2,5},{3,4},{4,3},{5,2},{6,7},{7,6},{8,9},{9,8},{10,13... | collective-permute-start | bytes 1179656 | tf_op jit(solution)/shard_map/ppermute | solution.py:1142
  273.1 33.2 %collective-permute-start.52 = (bf16[256,768]{1,0:T(8,128)(2,1)S(1)}, bf16[256,768]{1,0:T(8,128)(2,1)S(1)}, u32[]{:S(2)}, u32[]{:S(2)}) collective-permute-start(bf16[256,768]{1,0:T(8,128)(2,1)S(1)} %get-tuple-element.659), channel_id=1, source_target_pairs={{0,1},{1,0},{2,5},{3,4},{4,3},{5,2},{6,7},{7,6},{8,9},{9,8},{10,13... | collective-permute-start | bytes 1179656 | tf_op jit(solution)/shard_map/ppermute | solution.py:1142
  274.1 32.1 %collective-permute-start.51 = (bf16[256,768]{1,0:T(8,128)(2,1)S(1)}, bf16[256,768]{1,0:T(8,128)(2,1)S(1)}, u32[]{:S(2)}, u32[]{:S(2)}) collective-permute-start(bf16[256,768]{1,0:T(8,128)(2,1)S(1)} %get-tuple-element.660), channel_id=1, source_target_pairs={{0,0},{1,1},{2,4},{3,5},{4,2},{5,3},{6,6},{7,7},{8,8},{9,9},{10,12... | collective-permute-start | bytes 1179656 | tf_op jit(solution)/shard_map/ppermute | solution.py:1137
  334.2 23.7 %collective-permute-start.55 = (bf16[512,1536]{1,0:T(8,128)(2,1)S(1)}, bf16[512,1536]{1,0:T(8,128)(2,1)S(1)}, u32[]{:S(2)}, u32[]{:S(2)}) collective-permute-start(bf16[512,1536]{1,0:T(8,128)(2,1)S(1)} %add_convert_fusion.1), channel_id=1, source_target_pairs={{4,5},{5,4},{6,7},{7,6},{12,13},{13,12},{14,15},{15,14},{20,21},{2... | collective-permute-start | bytes 4718600 | tf_op jit(solution)/shard_map/ppermute | solution.py:1155
  335.0 22.9 %collective-permute-start.56 = (bf16[4,224,768]{2,1,0:T(8,128)(2,1)S(1)}, bf16[4,224,768]{2,1,0:T(8,128)(2,1)S(1)}, u32[]{:S(2)}, u32[]{:S(2)}) collective-permute-start(bf16[4,224,768]{2,1,0:T(8,128)(2,1)S(1)} %copy-done.47), channel_id=1, source_target_pairs={{0,8},{4,20},{8,0},{12,28},{16,24},{20,4},{24,16},{28,12},{1,9},{5... | collective-permute-start | bytes 4128776 | tf_op jit(solution)/shard_map/ppermute | solution.py:997
  335.7 48.2 %collective-permute-start.58 = (bf16[4,224,768]{2,1,0:T(8,128)(2,1)}, bf16[4,224,768]{2,1,0:T(8,128)(2,1)S(1)}, u32[]{:S(2)}, u32[]{:S(2)}) collective-permute-start(bf16[4,224,768]{2,1,0:T(8,128)(2,1)} %get-tuple-element.447), channel_id=1, source_target_pairs={{0,8},{4,20},{8,0},{12,28},{16,24},{20,4},{24,16},{28,12},{1,9},{5... | collective-permute-start | bytes 4128776 | tf_op jit(solution)/shard_map/ppermute | solution.py:997
  392.1 22.4 %collective-permute-start.61 = (bf16[4,4,96,576]{3,2,1,0:T(8,128)(2,1)}, bf16[4,4,96,576]{3,2,1,0:T(8,128)(2,1)S(1)}, u32[]{:S(2)}, u32[]{:S(2)}) collective-permute-start(bf16[4,4,96,576]{3,2,1,0:T(8,128)(2,1)} %get-tuple-element.464), channel_id=1, source_target_pairs={{0,4},{4,0},{8,12},{12,8},{16,20},{20,16},{24,28},{28,24},{1,5},{5... | collective-permute-start | bytes 5308424 | tf_op jit(solution)/shard_map/ppermute | solution.py:989
  467.1 26.5 %collective-permute-start.68 = (bf16[512,1536]{1,0:T(8,128)(2,1)S(1)}, bf16[512,1536]{1,0:T(8,128)(2,1)S(1)}, u32[]{:S(2)}, u32[]{:S(2)}) collective-permute-start(bf16[512,1536]{1,0:T(8,128)(2,1)S(1)} %add_convert_fusion), channel_id=1, source_target_pairs={{4,5},{5,4},{6,7},{7,6},{12,13},{13,12},{14,15},{15,14},{20,21},{2... | collective-permute-start | bytes 4718600 | tf_op jit(solution)/shard_map/ppermute | solution.py:1155
  467.9 25.7 %collective-permute-start.69 = (bf16[4,224,768]{2,1,0:T(8,128)(2,1)S(1)}, bf16[4,224,768]{2,1,0:T(8,128)(2,1)S(1)}, u32[]{:S(2)}, u32[]{:S(2)}) collective-permute-start(bf16[4,224,768]{2,1,0:T(8,128)(2,1)S(1)} %copy-done.46), channel_id=1, source_target_pairs={{0,8},{4,20},{8,0},{12,28},{16,24},{20,4},{24,16},{28,12},{1,9},{5... | collective-permute-start | bytes 4128776 | tf_op jit(solution)/shard_map/ppermute | solution.py:997
  468.8 24.3 %collective-permute-start.70 = (bf16[224,768]{1,0:T(8,128)(2,1)S(1)}, bf16[224,768]{1,0:T(8,128)(2,1)S(1)}, u32[]{:S(2)}, u32[]{:S(2)}) collective-permute-start(bf16[224,768]{1,0:T(8,128)(2,1)S(1)} %copy-done.12), channel_id=1, source_target_pairs={{0,16},{4,12},{8,24},{12,4},{16,0},{20,28},{24,8},{28,20},{1,17},{... | collective-permute-start | bytes 1032200 | tf_op jit(solution)/shard_map/ppermute | solution.py:1001
  470.4 22.6 %collective-permute-start.71 = (bf16[224,768]{1,0:T(8,128)(2,1)S(1)}, bf16[224,768]{1,0:T(8,128)(2,1)S(1)}, u32[]{:S(2)}, u32[]{:S(2)}) collective-permute-start(bf16[224,768]{1,0:T(8,128)(2,1)S(1)} %copy-done.23), channel_id=1, source_target_pairs={{0,16},{4,12},{8,24},{12,4},{16,0},{20,28},{24,8},{28,20},{1,17},{... | collective-permute-start | bytes 1032200 | tf_op jit(solution)/shard_map/ppermute | solution.py:1001
  470.8 48.8 %collective-permute-start.73 = (bf16[4,224,768]{2,1,0:T(8,128)(2,1)}, bf16[4,224,768]{2,1,0:T(8,128)(2,1)}, u32[]{:S(2)}, u32[]{:S(2)}) collective-permute-start(bf16[4,224,768]{2,1,0:T(8,128)(2,1)} %get-tuple-element.514), channel_id=1, source_target_pairs={{0,8},{4,20},{8,0},{12,28},{16,24},{20,4},{24,16},{28,12},{1,9},{5... | collective-permute-start | bytes 4128776 | tf_op jit(solution)/shard_map/ppermute | solution.py:997
  500.3 22.3 %collective-permute-start.74 = (bf16[4,224,768]{2,1,0:T(8,128)(2,1)S(1)}, bf16[4,224,768]{2,1,0:T(8,128)(2,1)S(1)}, u32[]{:S(2)}, u32[]{:S(2)}) collective-permute-start(bf16[4,224,768]{2,1,0:T(8,128)(2,1)S(1)} %fusion.2), channel_id=1, source_target_pairs={{0,16},{4,12},{8,24},{12,4},{16,0},{20,28},{24,8},{28,20},{1,17},{... | collective-permute-start | bytes 4128776 | tf_op jit(solution)/shard_map/ppermute | solution.py:1001
  548.7 22.5 %collective-permute-start.84 = (bf16[4,96,576]{2,1,0:T(8,128)(2,1)S(1)}, bf16[4,96,576]{2,1,0:T(8,128)(2,1)S(1)}, u32[]{:S(2)}, u32[]{:S(2)}) collective-permute-start(bf16[4,96,576]{2,1,0:T(8,128)(2,1)S(1)} %get-tuple-element.655), channel_id=1, source_target_pairs={{0,8},{4,20},{8,0},{12,28},{16,24},{20,4},{24,16},{28,12},{1,9},{5... | collective-permute-start | bytes 1327112 | tf_op jit(solution)/shard_map/ppermute | solution.py:997
  549.8 22.1 %collective-permute-start.83 = (bf16[4,96,576]{2,1,0:T(8,128)(2,1)S(1)}, bf16[4,96,576]{2,1,0:T(8,128)(2,1)S(1)}, u32[]{:S(2)}, u32[]{:S(2)}) collective-permute-start(bf16[4,96,576]{2,1,0:T(8,128)(2,1)S(1)} %get-tuple-element.656), channel_id=1, source_target_pairs={{0,16},{4,12},{8,24},{12,4},{16,0},{20,28},{24,8},{28,20},{1,17},{... | collective-permute-start | bytes 1327112 | tf_op jit(solution)/shard_map/ppermute | solution.py:1001
  (279 other events, 1824.8 us)

commit v6 on v5

--- a/solution.py
+++ b/solution.py
@@ -96,14 +96,26 @@
 
 
 def up_down_copies(refs, idx, sems, ups, downs):
-    def place(src, k, zq, wq):
-        rows = rows_at(wq * PIECE, PIECE, 32)
-        return [
-            (src.at[pl.ds(0, PIECE)], ups.at[k, rows]),
-            (src.at[pl.ds(PIECE, PIECE)], downs.at[k, rows]),
-        ]
-
-    return piece_copies(refs, idx, sems, place)
+    groups = []
+    for k in range(QUARTERS):
+        up, down = [], []
+        for i, (flip, ref) in enumerate(zip(flips(idx), refs)):
+            rows = rows_at((idx[0] ^ flip) * PIECE, PIECE, 32)
+            src = ref.at[ORDER.index(k)]
+            up.append(pltpu.make_async_copy(src.at[pl.ds(0, PIECE)], ups.at[k, rows], sems.at[16 * k + i]))
+            down.append(pltpu.make_async_copy(src.at[pl.ds(PIECE, PIECE)], downs.at[k, rows], sems.at[16 * k + 8 + i]))
+        groups.append((up, down))
+    return groups
+
+
+def begin(copies):
+    for copy in copies:
+        copy.start()
+
+
+def finish(copies):
+    for copy in copies:
+        copy.wait()
 
 
 def packed_copies(refs, idx, sems, packed):
@@ -414,16 +426,20 @@
     )
 
 
-def feed_body(idx, x, o, gain, shift, out_bias, down_bias, up_bias, *rest):
-    pieces, (x2, x1, h2, g, gp, ups, downs, packed, outw, sems, sems_o) = rest[:8], rest[8:]
+def feed_body(idx, x_in, o_in, gain, shift, out_bias, down_bias, up_bias, *rest):
+    pieces, (x2_out, x1_out, h2_out, g_out, gp_out), rest = rest[:8], rest[8:13], rest[13:]
+    ups, downs, packed, outw, x, o, x2, x1, h2, g, gp, sems, sems_o, sems_io = rest
     first = packed_copies(pieces, idx, sems_o, packed)
+    loads = [pltpu.make_async_copy(o_in, o, sems_io.at[0]), pltpu.make_async_copy(x_in, x, sems_io.at[1])]
     later = up_down_copies(pieces, idx, sems, ups, downs)
-    for copy in first + later:
-        copy.start()
-    for copy in first:
-        copy.wait()
+    begin(first + loads + later[0][0])
+    finish(first)
     unpack_output(packed, outw)
+    finish(loads)
+    begin(later[0][1])
     x1[...] = x[...] + (dot(o[...], outw[...]) + out_bias[...])
+    stores = [pltpu.make_async_copy(x1, x1_out, sems_io.at[2])]
+    begin(stores)
 
     def norm_rows(i, carry):
         rows = rows_at(i * 128, 128, 128)
@@ -433,23 +449,32 @@
         return carry
 
     lax.fori_loop(0, 4, norm_rows, 0)
-    for copy in later:
-        copy.wait()
-
-    def hidden(k, carry):
+    stores.append(pltpu.make_async_copy(h2, h2_out, sems_io.at[3]))
+    begin(stores[-1:])
+    for k, (up, down) in enumerate(later):
+        finish(up)
+        if k + 1 < QUARTERS:
+            begin(later[k + 1][0] + later[k + 1][1])
         for n in range(3):
             cols = slice(256 * n, 256 * (n + 1))
             u = dot(h2[...], ups[k, :, cols]) + up_bias[k, :, cols]
             uu = u * u
-            t = jnp.tanh(0.7978845608028654 * u * (1.0 + 0.044715 * uu))
+            t = jnp.tanh(u * (0.7978845608028654 + (0.7978845608028654 * 0.044715) * uu))
             half_t = 0.5 + 0.5 * t
             g[k, :, cols] = (u * half_t).astype(BF)
-            slope = half_t + (0.5 * 0.7978845608028654) * u * (1.0 - t * t) * (1.0 + 0.134145 * uu)
-            gp[k, :, cols] = slope.astype(BF)
+            inner = (0.5 * 0.7978845608028654) + (0.5 * 0.7978845608028654 * 0.134145) * uu
+            gp[k, :, cols] = (half_t + u * inner * (1.0 - t * t)).astype(BF)
+        ends = [
+            pltpu.make_async_copy(g.at[k], g_out.at[k], sems_io.at[4 + 2 * k]),
+            pltpu.make_async_copy(gp.at[k], gp_out.at[k], sems_io.at[5 + 2 * k]),
+        ]
+        begin(ends)
+        stores += ends
+        finish(down)
         x2[...] += dot(g[k], downs[k])
-        return carry
-
-    lax.fori_loop(0, QUARTERS, hidden, 0)
+    stores.append(pltpu.make_async_copy(x2, x2_out, sems_io.at[12]))
+    begin(stores[-1:])
+    finish(stores)
 
 
 WEIGHT_SCRATCH = [
@@ -463,7 +488,7 @@
 def feed(idx, x, o, gain, shift, out_bias, down_bias, up_bias, pieces):
     return kernel_call(
         feed_body,
-        [smem_spec()] + [vmem_spec()] * 7 + [any_spec()] * 8,
+        [smem_spec()] + [any_spec()] * 2 + [vmem_spec()] * 5 + [any_spec()] * 8,
         [
             sds((ROWS, D), F32),
             sds((ROWS, D), F32),
@@ -471,9 +496,11 @@
             sds((QUARTERS, ROWS, D), BF),
             sds((QUARTERS, ROWS, D), BF),
         ],
-        [vmem_spec()] * 5,
+        [any_spec()] * 5,
         [pltpu.VMEM(s, t) for s, t in WEIGHT_SCRATCH]
-        + [pltpu.SemaphoreType.DMA((64,)), pltpu.SemaphoreType.DMA((32,))],
+        + [pltpu.VMEM((ROWS, D), t) for t in (F32, BF, F32, F32, BF)]
+        + [pltpu.VMEM((QUARTERS, ROWS, D), BF)] * 2
+        + [pltpu.SemaphoreType.DMA((64,)), pltpu.SemaphoreType.DMA((32,)), pltpu.SemaphoreType.DMA((13,))],
         (idx, x, o, gain, shift, out_bias, down_bias, up_bias, *pieces),
         2 * ROWS * D * D * 9,
         25e6,
@@ -481,34 +508,44 @@
     )
 
 
-def feed_back_body(idx, e, x1, gp, gain, *rest):
-    pieces, (dm, dz, e1, da, do, small, ups, downs, packed, outw, dh2, hidden_sums, sems, sems_o) = rest[:8], rest[8:]
-    first = packed_copies(pieces, idx, sems_o, packed)
-    later = up_down_copies(pieces, idx, sems, ups, downs)
-    for copy in later + first:
-        copy.start()
+def feed_back_body(idx, e_in, x1_in, gp_in, gain, *rest):
+    pieces, (dm_out, dz_out, e1_out, da_out, do_out, small), rest = rest[:8], rest[8:14], rest[14:]
+    ups, downs, packed, outw, e, x1, gp, dm, dz, da, do, dh2, hidden_sums, sems, sems_o, sems_io = rest
+    load_e = pltpu.make_async_copy(e_in, e, sems_io.at[0])
+    load_x1 = pltpu.make_async_copy(x1_in, x1, sems_io.at[1])
+    load_gp = [pltpu.make_async_copy(gp_in.at[k], gp.at[k], sems_io.at[2 + k]) for k in range(QUARTERS)]
+    last = packed_copies(pieces, idx, sems_o, packed)
+    weights = up_down_copies(pieces, idx, sems, ups, downs)
+    begin([load_e] + weights[0][1] + [load_gp[0]])
+    load_e.wait()
+    begin(weights[0][0])
     dm[...] = e[...].astype(BF)
+    stores = [pltpu.make_async_copy(dm, dm_out, sems_io.at[6])]
+    begin(stores)
     small[4:5] = jnp.sum(dm[...].astype(F32), axis=0, keepdims=True)
-    dh2[...] = jnp.zeros_like(dh2)
-    for copy in later:
-        copy.wait()
-
-    def hidden(k, carry):
-        zq = idx[1] ^ k
+    for k, (up, down) in enumerate(weights):
+        finish(down + [load_gp[k]])
+        if k + 1 < QUARTERS:
+            begin(weights[k + 1][1] + [load_gp[k + 1]] + weights[k + 1][0])
+        else:
+            begin(last + [load_x1])
         for n in range(3):
             cols = slice(256 * n, 256 * (n + 1))
             part = (dot_nt(dm[...], downs[k, cols]) * gp[k, :, cols].astype(F32)).astype(BF)
             dz[k, :, cols] = part
-            hidden_sums[zq, :, cols] = jnp.sum(part.astype(F32), axis=0, keepdims=True)
-        dh2[...] += dot_nt(dz[k], ups[k])
-        return carry
-
-    lax.fori_loop(0, QUARTERS, hidden, 0)
-    for copy in first:
-        copy.wait()
-    unpack_output(packed, outw)
+            hidden_sums[idx[1] ^ k, :, cols] = jnp.sum(part.astype(F32), axis=0, keepdims=True)
+        stores.append(pltpu.make_async_copy(dz.at[k], dz_out.at[k], sems_io.at[7 + k]))
+        begin(stores[-1:])
+        finish(up)
+        grown = dot_nt(dz[k], ups[k])
+        if k == 0:
+            dh2[...] = grown
+        else:
+            dh2[...] += grown
     for zq in range(QUARTERS):
         small[zq : zq + 1] = hidden_sums[zq]
+    finish(last + [load_x1])
+    unpack_output(packed, outw)
     small[5:8] = jnp.zeros((3, D), F32)
 
     def norm_rows(i, carry):
@@ -516,7 +553,7 @@
         unit, inverse = norm_parts(x1[rows])
         grad = dh2[rows]
         up = e[rows] + norm_backward(grad, unit, inverse, gain[...])
-        e1[rows] = up
+        e[rows] = up
         low = up.astype(BF)
         da[rows] = low
         small[5:6] += jnp.sum(low.astype(F32), axis=0, keepdims=True)
@@ -525,13 +562,18 @@
         return carry
 
     lax.fori_loop(0, 4, norm_rows, 0)
+    ends = [pltpu.make_async_copy(e, e1_out, sems_io.at[11]), pltpu.make_async_copy(da, da_out, sems_io.at[12])]
+    begin(ends)
     do[...] = dot_nt(da[...], outw[...]).astype(BF)
+    ends.append(pltpu.make_async_copy(do, do_out, sems_io.at[13]))
+    begin(ends[-1:])
+    finish(stores + ends)
 
 
 def feed_back(idx, e, x1, gp, gain, pieces):
     return kernel_call(
         feed_back_body,
-        [smem_spec()] + [vmem_spec()] * 4 + [any_spec()] * 8,
+        [smem_spec()] + [any_spec()] * 3 + [vmem_spec()] + [any_spec()] * 8,
         [
             sds((ROWS, D), BF),
             sds((QUARTERS, ROWS, D), BF),
@@ -540,9 +582,22 @@
             sds((ROWS, D), BF),
             sds((8, D), F32),
         ],
-        [vmem_spec()] * 6,
+        [any_spec()] * 5 + [vmem_spec()],
         [pltpu.VMEM(s, t) for s, t in WEIGHT_SCRATCH]
-        + [pltpu.VMEM((ROWS, D), F32), pltpu.VMEM((QUARTERS, 1, D), F32), pltpu.SemaphoreType.DMA((64,)), pltpu.SemaphoreType.DMA((32,))],
+        + [
+            pltpu.VMEM((ROWS, D), F32),
+            pltpu.VMEM((ROWS, D), F32),
+            pltpu.VMEM((QUARTERS, ROWS, D), BF),
+            pltpu.VMEM((ROWS, D), BF),
+            pltpu.VMEM((QUARTERS, ROWS, D), BF),
+            pltpu.VMEM((ROWS, D), BF),
+            pltpu.VMEM((ROWS, D), BF),
+            pltpu.VMEM((ROWS, D), F32),
+            pltpu.VMEM((QUARTERS, 1, D), F32),
+            pltpu.SemaphoreType.DMA((64,)),
+            pltpu.SemaphoreType.DMA((32,)),
+            pltpu.SemaphoreType.DMA((14,)),
+        ],
         (idx, e, x1, gp, gain, *pieces),
         2 * ROWS * D * D * 9,
         25e6,

time: 664 us -> 664 us (level)
  starting transfers between devices: 116 us -> 130 us
  Pallas kernels: 286 us -> 278 us
    ppermute x4, starting transfers between devices: 4.09 us -> 17.8 us  [between_chips(): return lax.ppermute(x, BOTH, pairs)]
    pallas_call x25, Pallas kernels: 286 us -> 278 us  [kernel_call(): pl.pallas_call(body, in_specs=in_specs, out_specs=out_specs, out_shape=ou...]
  transfers between devices with their start and end apart: 116 -> 116, of which waited for: 31 -> 34; matrix products, arithmetic and copies ran while one was open for 10% -> 10% of each run, Pallas kernels for 42% -> 40%
where the time goes in v6:
time: 664 us; the launch traced here: 660 us
  Pallas kernels  278 us (42%)
  starting transfers between devices  130 us (20%)
  waiting for transfers between devices  109 us (16%)
  local copies, waits for them, and re-layouts  73.8 us (11%)
  other arithmetic  63.8 us (10%)
    pallas_call x25, Pallas kernels, kernel_call(): pl.pallas_call(body, in_specs=in_specs, out_specs=out_specs, out_shape=ou...  278 us
    unnamed x383, local copies, waits for them, and re-layouts  48.2 us
    ppermute x22, waiting for transfers between devices, flip_narrow(): return lax.ppermute(x, 'narrow', [(i, i ^ bit) for i in range(QUARTERS)])  47.4 us
    convert_element_type x21, other arithmetic, added(): return functools.reduce(jnp.add, [t.astype(F32) for t in terms]).astype(BF)  43.3 us
    ppermute x40, starting transfers between devices, flip_wide(): lax.ppermute(x, 'wide', [(i, i ^ bit) for i in range(lax.axis_size('wide'...  26.7 us
    ppermute x22, starting transfers between devices, flip_narrow(): return lax.ppermute(x, 'narrow', [(i, i ^ bit) for i in range(QUARTERS)])  24.6 us
    ppermute x19, starting transfers between devices, second_axis(): lax.ppermute(x, 'wide', [(i, i ^ (2 if i & 1 else 4)) for i in range(lax....  21.5 us
    ppermute x19, waiting for transfers between devices, second_axis(): lax.ppermute(x, 'wide', [(i, i ^ (2 if i & 1 else 4)) for i in range(lax....  21.1 us
  transfers between devices with their start and end apart: 116, of which 34 were waited for; matrix products, arithmetic and copies ran while one was open for 10% of the time, Pallas kernels for 40%

profile of v6, /device:TPU:0, one launch (start us, length us, event | category | flops | bytes accessed | tf_op | source)
XLA Modules:
  0.0 659.8 jit_solution(4635329901054868628)
XLA Ops:
  30.2 15.8 %collective-permute-done.8.refs_3_ = bf16[224,768]{1,0:T(8,128)(2,1)S(1)} collective-permute-done((bf16[224,768]{1,0:T(8,128)(2,1)}, bf16[224,768]{1,0:T(8,128)(2,1)S(1)}, u32[]{:S(2)}, u32[]{:S(2)}) %collective-permute-start.8) | collective-permute-done | bytes 344096 | tf_op jit(solution)/shard_map/ppermute | solution.py:1048
  58.7 15.3 %collective-permute-done.12.refs_5_ = bf16[256,768]{1,0:T(8,128)(2,1)} collective-permute-done((bf16[256,768]{1,0:T(8,128)(2,1)}, bf16[256,768]{1,0:T(8,128)(2,1)}, u32[]{:S(2)}, u32[]{:S(2)}) %collective-permute-start.12) | collective-permute-done | bytes 393248 | tf_op jit(solution)/shard_map/ppermute | solution.py:1197
  88.6 8.3 %project.2 = (bf16[512,768]{1,0:T(8,128)(2,1)}, bf16[512,768]{1,0:T(8,128)(2,1)}, bf16[512,1536]{1,0:T(8,128)(2,1)}) custom-call(s32[8]{0:T(128)} %stack.143.idx, f32[512,768]{1,0:T(8,128)} %maximum_convert_fusion.x.x_in, f32[1,768]{1,0:T(1,128)} %get-tuple-element.707.gain, f32[1,768]{1,0:T(1,128)} %get-tuple-element.687.shift, ...), custom_call_target="tpu_custom_call" | custom-call | flops 1000 | bytes 1000 | tf_op jit(solution)/shard_map/project/pallas_call | solution.py:152
  107.9 15.3 %attend_near.2 = (f32[512,768]{1,0:T(8,128)}, f32[512,128]{1,0:T(8,128)}, f32[512,128]{1,0:T(8,128)}) custom-call(s32[8]{0:T(128)} %stack.143.idx, bf16[512,768]{1,0:T(8,128)(2,1)} %get-tuple-element.337.q, bf16[512,1536]{1,0:T(8,128)(2,1)} %get-tuple-element.342.own, bf16[512,1536]{1,0:T(8,128)(2,1)} %copy-done.32), custom_call_target="tpu_custom_call" | custom-call | flops 1000 | bytes 1000 | tf_op jit(solution)/shard_map/attend_near/pallas_call | solution.py:152
  134.6 8.6 %attend_far.2 = (bf16[512,768]{1,0:T(8,128)(2,1)}, f32[12,1,512]{2,1,0:T(1,128)}) custom-call(s32[8]{0:T(128)} %stack.143.idx, bf16[512,768]{1,0:T(8,128)(2,1)} %get-tuple-element.337.q, bf16[512,1536]{1,0:T(8,128)(2,1)} %get-tuple-element.351.far, bf16[512,1536]{1,0:T(8,128)(2,1)} %copy-done.33, f32[512,768]{1,0:T(8,128)} %get-tuple-element.352.acc, ...), custom_call_target="tpu_custom_call" | custom-call | flops 1000 | bytes 1000 | tf_op jit(solution)/shard_map/attend_far/pallas_call | solution.py:152
  155.6 16.8 %feed.2 = (f32[512,768]{1,0:T(8,128)}, f32[512,768]{1,0:T(8,128)}, bf16[512,768]{1,0:T(8,128)(2,1)}, bf16[4,512,768]{2,1,0:T(8,128)(2,1)}, bf16[4,512,768]{2,1,0:T(8,128)(2,1)}) custom-call(s32[8]{0:T(128)} %stack.143.idx, f32[512,768]{1,0:T(8,128)} %maximum_convert_fusion.x.x_in, bf16[512,768]{1,0:T(8,128)(2,1)} %get-tuple-element.363.o_in.o, ...), custom_call_target="tpu_custom_call" | custom-call | flops 1000 | bytes 1000 | tf_op jit(solution)/shard_map/feed/pallas_call | solution.py:152
  185.6 8.2 %project.3 = (bf16[512,768]{1,0:T(8,128)(2,1)}, bf16[512,768]{1,0:T(8,128)(2,1)}, bf16[512,1536]{1,0:T(8,128)(2,1)}) custom-call(s32[8]{0:T(128)} %stack.143.idx, f32[512,768]{1,0:T(8,128)} %get-tuple-element.373.x.x_in, f32[1,768]{1,0:T(1,128)} %get-tuple-element.706.gain, f32[1,768]{1,0:T(1,128)} %get-tuple-element.688.shift, ...), custom_call_target="tpu_custom_call" | custom-call | flops 1000 | bytes 1000 | tf_op jit(solution)/shard_map/project/pallas_call | solution.py:152
  200.3 14.5 %collective-permute-start.41 = (bf16[512,1536]{1,0:T(8,128)(2,1)}, bf16[512,1536]{1,0:T(8,128)(2,1)S(1)}, u32[]{:S(2)}, u32[]{:S(2)}) collective-permute-start(bf16[512,1536]{1,0:T(8,128)(2,1)} %get-tuple-element.382.own), channel_id=1, source_target_pairs={{4,5},{5,4},{6,7},{7,6},{12,13},{13,12},{14,15},{15,14},{20,21},{2... | collective-permute-start | bytes 4718600 | tf_op jit(solution)/shard_map/ppermute | solution.py:1210
  217.7 15.3 %attend_near.3 = (f32[512,768]{1,0:T(8,128)}, f32[512,128]{1,0:T(8,128)}, f32[512,128]{1,0:T(8,128)}) custom-call(s32[8]{0:T(128)} %stack.143.idx, bf16[512,768]{1,0:T(8,128)(2,1)} %get-tuple-element.378.q, bf16[512,1536]{1,0:T(8,128)(2,1)} %get-tuple-element.382.own, bf16[512,1536]{1,0:T(8,128)(2,1)} %copy-done.34), custom_call_target="tpu_custom_call" | custom-call | flops 1000 | bytes 1000 | tf_op jit(solution)/shard_map/attend_near/pallas_call | solution.py:152
  244.4 8.4 %attend_far.3 = (bf16[512,768]{1,0:T(8,128)(2,1)}, f32[12,1,512]{2,1,0:T(1,128)}) custom-call(s32[8]{0:T(128)} %stack.143.idx, bf16[512,768]{1,0:T(8,128)(2,1)} %get-tuple-element.378.q, bf16[512,1536]{1,0:T(8,128)(2,1)} %get-tuple-element.388.far, bf16[512,1536]{1,0:T(8,128)(2,1)} %copy-done.35, f32[512,768]{1,0:T(8,128)} %get-tuple-element.389.acc, ...), custom_call_target="tpu_custom_call" | custom-call | flops 1000 | bytes 1000 | tf_op jit(solution)/shard_map/attend_far/pallas_call | solution.py:152
  262.7 16.8 %feed.3 = (f32[512,768]{1,0:T(8,128)}, f32[512,768]{1,0:T(8,128)}, bf16[512,768]{1,0:T(8,128)(2,1)}, bf16[4,512,768]{2,1,0:T(8,128)(2,1)}, bf16[4,512,768]{2,1,0:T(8,128)(2,1)}) custom-call(s32[8]{0:T(128)} %stack.143.idx, f32[512,768]{1,0:T(8,128)} %get-tuple-element.373.x.x_in, bf16[512,768]{1,0:T(8,128)(2,1)} %get-tuple-element.396.o_in.o, ...), custom_call_target="tpu_custom_call" | custom-call | flops 1000 | bytes 1000 | tf_op jit(solution)/shard_map/feed/pallas_call | solution.py:152
  285.1 17.7 %feed_back.2 = (bf16[512,768]{1,0:T(8,128)(2,1)}, bf16[4,512,768]{2,1,0:T(8,128)(2,1)}, f32[512,768]{1,0:T(8,128)}, bf16[512,768]{1,0:T(8,128)(2,1)}, bf16[512,768]{1,0:T(8,128)(2,1)}, /*index=5*/f32[8,768]{1,0:T(8,128)}) custom-call(s32[8]{0:T(128)} %stack.143.idx, f32[512,768]{1,0:T(8,128)} %maximum_convert_fusion.1.e_in, ...), custom_call_target="tpu_custom_call" | custom-call | flops 1000 | bytes 1000 | tf_op jit(solution)/shard_map/feed_back/pallas_call | solution.py:152
  302.8 11.5 %feed_grads.2 = (bf16[4,4,224,768]{3,2,1,0:T(8,128)(2,1)}, bf16[4,4,224,768]{3,2,1,0:T(8,128)(2,1)}) custom-call(s32[8]{0:T(128)} %stack.143.idx, bf16[4,512,768]{2,1,0:T(8,128)(2,1)} %get-tuple-element.410.g, bf16[512,768]{1,0:T(8,128)(2,1)} %get-tuple-element.411.dm, bf16[512,768]{1,0:T(8,128)(2,1)} %get-tuple-element.412.h2, ...), custom_call_target="tpu_custom_call" | custom-call | flops 1000 | bytes 1000 | tf_op jit(solution)/shard_map/feed_grads/pallas_call | solution.py:152
  319.8 10.7 %attend_back_far.2 = (f32[512,768]{1,0:T(8,128)}, bf16[512,1536]{1,0:T(8,128)(2,1)}, f32[12,1,512]{2,1,0:T(1,128)}) custom-call(s32[8]{0:T(128)} %stack.143.idx, bf16[512,768]{1,0:T(8,128)(2,1)} %get-tuple-element.378.q, bf16[512,768]{1,0:T(8,128)(2,1)} %get-tuple-element.420.do, bf16[512,768]{1,0:T(8,128)(2,1)} %get-tuple-element.396.o_in.o, ...), custom_call_target="tpu_custom_call" | custom-call | flops 1000 | bytes 1000 | tf_op jit(solution)/shard_map/attend_back_far/pallas_call | solution.py:152
  343.7 20.9 %attend_back_near.2 = (f32[512,768]{1,0:T(8,128)}, bf16[512,1536]{1,0:T(8,128)(2,1)}, bf16[512,1536]{1,0:T(8,128)(2,1)}) custom-call(s32[8]{0:T(128)} %stack.143.idx, bf16[512,768]{1,0:T(8,128)(2,1)} %get-tuple-element.378.q, bf16[512,768]{1,0:T(8,128)(2,1)} %get-tuple-element.420.do, f32[12,1,512]{2,1,0:T(1,128)} %get-tuple-element.421.lse, ...), custom_call_target="tpu_custom_call" | custom-call | flops 1000 | bytes 1000 | tf_op jit(solution)/shard_map/attend_back_near/pallas_call | solution.py:152
  376.4 14.6 %project_back.2 = (bf16[4,512,576]{2,1,0:T(8,128)(2,1)}, f32[512,768]{1,0:T(8,128)}, f32[8,768]{1,0:T(8,128)}) custom-call(s32[8]{0:T(128)} %stack.143.idx, f32[512,768]{1,0:T(8,128)} %get-tuple-element.432.dq, bf16[512,1536]{1,0:T(8,128)(2,1)} %get-tuple-element.433.dn, bf16[512,1536]{1,0:T(8,128)(2,1)} %get-tuple-element.440.dcr, ...), custom_call_target="tpu_custom_call" | custom-call | flops 1000 | bytes 1000 | tf_op jit(solution)/shard_map/project_back/pallas_call | solution.py:152
  402.6 17.8 %feed_back.3 = (bf16[512,768]{1,0:T(8,128)(2,1)}, bf16[4,512,768]{2,1,0:T(8,128)(2,1)}, f32[512,768]{1,0:T(8,128)}, bf16[512,768]{1,0:T(8,128)(2,1)}, bf16[512,768]{1,0:T(8,128)(2,1)}, /*index=5*/f32[8,768]{1,0:T(8,128)}) custom-call(s32[8]{0:T(128)} %stack.143.idx, f32[512,768]{1,0:T(8,128)} %get-tuple-element.454.e_in, ...), custom_call_target="tpu_custom_call" | custom-call | flops 1000 | bytes 1000 | tf_op jit(solution)/shard_map/feed_back/pallas_call | solution.py:152
  428.4 11.6 %feed_grads.3 = (bf16[4,4,224,768]{3,2,1,0:T(8,128)(2,1)}, bf16[4,4,224,768]{3,2,1,0:T(8,128)(2,1)}) custom-call(s32[8]{0:T(128)} %stack.143.idx, bf16[4,512,768]{2,1,0:T(8,128)(2,1)} %get-tuple-element.470.g, bf16[512,768]{1,0:T(8,128)(2,1)} %get-tuple-element.471.dm, bf16[512,768]{1,0:T(8,128)(2,1)} %get-tuple-element.472.h2, ...), custom_call_target="tpu_custom_call" | custom-call | flops 1000 | bytes 1000 | tf_op jit(solution)/shard_map/feed_grads/pallas_call | solution.py:152
  451.1 10.7 %attend_back_far.3 = (f32[512,768]{1,0:T(8,128)}, bf16[512,1536]{1,0:T(8,128)(2,1)}, f32[12,1,512]{2,1,0:T(1,128)}) custom-call(s32[8]{0:T(128)} %stack.143.idx, bf16[512,768]{1,0:T(8,128)(2,1)} %get-tuple-element.337.q, bf16[512,768]{1,0:T(8,128)(2,1)} %get-tuple-element.477.do, bf16[512,768]{1,0:T(8,128)(2,1)} %get-tuple-element.363.o_in.o, ...), custom_call_target="tpu_custom_call" | custom-call | flops 1000 | bytes 1000 | tf_op jit(solution)/shard_map/attend_back_far/pallas_call | solution.py:152
  477.8 21.0 %attend_back_near.3 = (f32[512,768]{1,0:T(8,128)}, bf16[512,1536]{1,0:T(8,128)(2,1)}, bf16[512,1536]{1,0:T(8,128)(2,1)}) custom-call(s32[8]{0:T(128)} %stack.143.idx, bf16[512,768]{1,0:T(8,128)(2,1)} %get-tuple-element.337.q, bf16[512,768]{1,0:T(8,128)(2,1)} %get-tuple-element.477.do, f32[12,1,512]{2,1,0:T(1,128)} %get-tuple-element.478.lse, ...), custom_call_target="tpu_custom_call" | custom-call | flops 1000 | bytes 1000 | tf_op jit(solution)/shard_map/attend_back_near/pallas_call | solution.py:152
  511.4 14.4 %project_back.3 = (bf16[4,512,576]{2,1,0:T(8,128)(2,1)}, f32[512,768]{1,0:T(8,128)}, f32[8,768]{1,0:T(8,128)}) custom-call(s32[8]{0:T(128)} %stack.143.idx, f32[512,768]{1,0:T(8,128)} %get-tuple-element.497.dq, bf16[512,1536]{1,0:T(8,128)(2,1)} %get-tuple-element.498.dn, bf16[512,1536]{1,0:T(8,128)(2,1)} %get-tuple-element.507.dcr, ...), custom_call_target="tpu_custom_call" | custom-call | flops 1000 | bytes 1000 | tf_op jit(solution)/shard_map/project_back/pallas_call | solution.py:152
  529.6 6.1 project_grads.3
  568.5 8.9 %collective-permute-done.84.refs_3_ = bf16[4,96,576]{2,1,0:T(8,128)(2,1)S(1)} collective-permute-done((bf16[4,96,576]{2,1,0:T(8,128)(2,1)S(1)}, bf16[4,96,576]{2,1,0:T(8,128)(2,1)S(1)}, u32[]{:S(2)}, u32[]{:S(2)}) %collective-permute-start.84) | collective-permute-done | bytes 442400 | tf_op jit(solution)/shard_map/ppermute | solution.py:1052
  611.0 6.3 collective-permute-done.92.refs_2_
  (757 shorter events, 339.6 us)
Async XLA Ops:
  48.1 26.0 %collective-permute-start.13 = (bf16[2,224,768]{2,1,0:T(8,128)(2,1)S(1)}, bf16[2,224,768]{2,1,0:T(8,128)(2,1)S(1)}, u32[]{:S(2)}, u32[]{:S(2)}) collective-permute-start(bf16[2,224,768]{2,1,0:T(8,128)(2,1)S(1)} %pad_maximum_fusion.2.refs_6_), channel_id=1, source_target_pairs={{0,1},{1,0},{2,3},{3,2},{4,5},{5,4},{6,7},{7,6},{8,9},{9,8},{10,11... | collective-permute-start | bytes 2064392 | tf_op jit(solution)/shard_map/ppermute | solution.py:1048
  49.9 24.2 %collective-permute-start.12 = (bf16[256,768]{1,0:T(8,128)(2,1)}, bf16[256,768]{1,0:T(8,128)(2,1)}, u32[]{:S(2)}, u32[]{:S(2)}) collective-permute-start(bf16[256,768]{1,0:T(8,128)(2,1)} %get-tuple-element.323), channel_id=1, source_target_pairs={{0,1},{1,0},{2,5},{3,4},{4,3},{5,2},{6,7},{7,6},{8,9},{9,8},{10,13... | collective-permute-start | bytes 1179656 | tf_op jit(solution)/shard_map/ppermute | solution.py:1197
  51.9 22.1 %collective-permute-start.9 = (bf16[4,96,576]{2,1,0:T(8,128)(2,1)}, bf16[4,96,576]{2,1,0:T(8,128)(2,1)S(1)}, u32[]{:S(2)}, u32[]{:S(2)}) collective-permute-start(bf16[4,96,576]{2,1,0:T(8,128)(2,1)} %get-tuple-element.320.refs_0_), channel_id=1, source_target_pairs={{0,16},{4,12},{8,24},{12,4},{16,0},{20,28},{24,8},{28,20},{1,17},{... | collective-permute-start | bytes 1327112 | tf_op jit(solution)/shard_map/ppermute | solution.py:1056
  52.4 21.6 %collective-permute-start.10 = (bf16[4,96,576]{2,1,0:T(8,128)(2,1)}, bf16[4,96,576]{2,1,0:T(8,128)(2,1)S(1)}, u32[]{:S(2)}, u32[]{:S(2)}) collective-permute-start(bf16[4,96,576]{2,1,0:T(8,128)(2,1)} %get-tuple-element.321.refs_1_), channel_id=1, source_target_pairs={{0,16},{4,12},{8,24},{12,4},{16,0},{20,28},{24,8},{28,20},{1,17},{... | collective-permute-start | bytes 1327112 | tf_op jit(solution)/shard_map/ppermute | solution.py:1056
  99.3 25.6 %collective-permute-start.21 = (bf16[512,1536]{1,0:T(8,128)(2,1)}, bf16[512,1536]{1,0:T(8,128)(2,1)}, u32[]{:S(2)}, u32[]{:S(2)}) collective-permute-start(bf16[512,1536]{1,0:T(8,128)(2,1)} %get-tuple-element.342.own), channel_id=1, source_target_pairs={{4,5},{5,4},{6,7},{7,6},{12,13},{13,12},{14,15},{15,14},{20,21},{2... | collective-permute-start | bytes 4718600 | tf_op jit(solution)/shard_map/ppermute | solution.py:1210
  101.1 22.1 %collective-permute-start.24 = (bf16[4,224,768]{2,1,0:T(8,128)(2,1)}, bf16[4,224,768]{2,1,0:T(8,128)(2,1)S(1)}, u32[]{:S(2)}, u32[]{:S(2)}) collective-permute-start(bf16[4,224,768]{2,1,0:T(8,128)(2,1)} %get-tuple-element.346.refs_4_), channel_id=1, source_target_pairs={{0,4},{4,0},{8,12},{12,8},{16,20},{20,16},{24,28},{28,24},{1,5},{5... | collective-permute-start | bytes 4128776 | tf_op jit(solution)/shard_map/ppermute | solution.py:1044
  149.9 25.6 %collective-permute-start.34 = (bf16[2,224,768]{2,1,0:T(8,128)(2,1)S(1)}, bf16[2,224,768]{2,1,0:T(8,128)(2,1)S(1)}, u32[]{:S(2)}, u32[]{:S(2)}) collective-permute-start(bf16[2,224,768]{2,1,0:T(8,128)(2,1)S(1)} %pad_maximum_fusion.3.refs_5_), channel_id=1, source_target_pairs={{0,1},{1,0},{2,3},{3,2},{4,5},{5,4},{6,7},{7,6},{8,9},{9,8},{10,11... | collective-permute-start | bytes 2064392 | tf_op jit(solution)/shard_map/ppermute | solution.py:1048
  150.1 22.3 %collective-permute-start.33 = (bf16[4,96,576]{2,1,0:T(8,128)(2,1)S(1)}, bf16[4,96,576]{2,1,0:T(8,128)(2,1)S(1)}, u32[]{:S(2)}, u32[]{:S(2)}) collective-permute-start(bf16[4,96,576]{2,1,0:T(8,128)(2,1)S(1)} %constant_dynamic-update-slice_fusion.2.refs_1_), channel_id=1, source_target_pairs={{0,24},{4,28},{8,16},{12,20},{16,8},{20,12},{24,0},{28,4},{1,25},{... | collective-permute-start | bytes 1327112 | tf_op jit(solution)/shard_map/ppermute | solution.py:1044
  151.7 23.3 %collective-permute-start.32 = (bf16[4,96,576]{2,1,0:T(8,128)(2,1)S(1)}, bf16[4,96,576]{2,1,0:T(8,128)(2,1)S(1)}, u32[]{:S(2)}, u32[]{:S(2)}) collective-permute-start(bf16[4,96,576]{2,1,0:T(8,128)(2,1)S(1)} %constant_dynamic-update-slice_fusion.2.refs_1_), channel_id=1, source_target_pairs={{0,16},{4,12},{8,24},{12,4},{16,0},{20,28},{24,8},{28,20},{1,17},{... | collective-permute-start | bytes 1327112 | tf_op jit(solution)/shard_map/ppermute | solution.py:1056
  152.9 22.6 %collective-permute-start.31 = (bf16[4,96,576]{2,1,0:T(8,128)(2,1)S(1)}, bf16[4,96,576]{2,1,0:T(8,128)(2,1)S(1)}, u32[]{:S(2)}, u32[]{:S(2)}) collective-permute-start(bf16[4,96,576]{2,1,0:T(8,128)(2,1)S(1)} %constant_dynamic-update-slice_fusion.2.refs_1_), channel_id=1, source_target_pairs={{0,8},{4,20},{8,0},{12,28},{16,24},{20,4},{24,16},{28,12},{1,9},{5... | collective-permute-start | bytes 1327112 | tf_op jit(solution)/shard_map/ppermute | solution.py:1052
  200.3 33.1 %collective-permute-start.41 = (bf16[512,1536]{1,0:T(8,128)(2,1)}, bf16[512,1536]{1,0:T(8,128)(2,1)S(1)}, u32[]{:S(2)}, u32[]{:S(2)}) collective-permute-start(bf16[512,1536]{1,0:T(8,128)(2,1)} %get-tuple-element.382.own), channel_id=1, source_target_pairs={{4,5},{5,4},{6,7},{7,6},{12,13},{13,12},{14,15},{15,14},{20,21},{2... | collective-permute-start | bytes 4718600 | tf_op jit(solution)/shard_map/ppermute | solution.py:1210
  282.0 32.3 %collective-permute-start.52 = (bf16[256,768]{1,0:T(8,128)(2,1)S(1)}, bf16[256,768]{1,0:T(8,128)(2,1)S(1)}, u32[]{:S(2)}, u32[]{:S(2)}) collective-permute-start(bf16[256,768]{1,0:T(8,128)(2,1)S(1)} %get-tuple-element.659), channel_id=1, source_target_pairs={{0,1},{1,0},{2,5},{3,4},{4,3},{5,2},{6,7},{7,6},{8,9},{9,8},{10,13... | collective-permute-start | bytes 1179656 | tf_op jit(solution)/shard_map/ppermute | solution.py:1197
  283.1 31.3 %collective-permute-start.51 = (bf16[256,768]{1,0:T(8,128)(2,1)S(1)}, bf16[256,768]{1,0:T(8,128)(2,1)S(1)}, u32[]{:S(2)}, u32[]{:S(2)}) collective-permute-start(bf16[256,768]{1,0:T(8,128)(2,1)S(1)} %get-tuple-element.660), channel_id=1, source_target_pairs={{0,0},{1,1},{2,4},{3,5},{4,2},{5,3},{6,6},{7,7},{8,8},{9,9},{10,12... | collective-permute-start | bytes 1179656 | tf_op jit(solution)/shard_map/ppermute | solution.py:1192
  340.9 23.8 %collective-permute-start.55 = (bf16[512,1536]{1,0:T(8,128)(2,1)S(1)}, bf16[512,1536]{1,0:T(8,128)(2,1)S(1)}, u32[]{:S(2)}, u32[]{:S(2)}) collective-permute-start(bf16[512,1536]{1,0:T(8,128)(2,1)S(1)} %add_convert_fusion.1), channel_id=1, source_target_pairs={{4,5},{5,4},{6,7},{7,6},{12,13},{13,12},{14,15},{15,14},{20,21},{2... | collective-permute-start | bytes 4718600 | tf_op jit(solution)/shard_map/ppermute | solution.py:1210
  341.6 23.0 %collective-permute-start.56 = (bf16[4,224,768]{2,1,0:T(8,128)(2,1)S(1)}, bf16[4,224,768]{2,1,0:T(8,128)(2,1)S(1)}, u32[]{:S(2)}, u32[]{:S(2)}) collective-permute-start(bf16[4,224,768]{2,1,0:T(8,128)(2,1)S(1)} %copy-done.47), channel_id=1, source_target_pairs={{0,8},{4,20},{8,0},{12,28},{16,24},{20,4},{24,16},{28,12},{1,9},{5... | collective-permute-start | bytes 4128776 | tf_op jit(solution)/shard_map/ppermute | solution.py:1052
  342.7 48.4 %collective-permute-start.58 = (bf16[4,224,768]{2,1,0:T(8,128)(2,1)}, bf16[4,224,768]{2,1,0:T(8,128)(2,1)S(1)}, u32[]{:S(2)}, u32[]{:S(2)}) collective-permute-start(bf16[4,224,768]{2,1,0:T(8,128)(2,1)} %get-tuple-element.447), channel_id=1, source_target_pairs={{0,8},{4,20},{8,0},{12,28},{16,24},{20,4},{24,16},{28,12},{1,9},{5... | collective-permute-start | bytes 4128776 | tf_op jit(solution)/shard_map/ppermute | solution.py:1052
  472.9 26.5 %collective-permute-start.68 = (bf16[512,1536]{1,0:T(8,128)(2,1)S(1)}, bf16[512,1536]{1,0:T(8,128)(2,1)S(1)}, u32[]{:S(2)}, u32[]{:S(2)}) collective-permute-start(bf16[512,1536]{1,0:T(8,128)(2,1)S(1)} %add_convert_fusion), channel_id=1, source_target_pairs={{4,5},{5,4},{6,7},{7,6},{12,13},{13,12},{14,15},{15,14},{20,21},{2... | collective-permute-start | bytes 4718600 | tf_op jit(solution)/shard_map/ppermute | solution.py:1210
  473.7 25.7 %collective-permute-start.69 = (bf16[4,224,768]{2,1,0:T(8,128)(2,1)S(1)}, bf16[4,224,768]{2,1,0:T(8,128)(2,1)S(1)}, u32[]{:S(2)}, u32[]{:S(2)}) collective-permute-start(bf16[4,224,768]{2,1,0:T(8,128)(2,1)S(1)} %copy-done.46), channel_id=1, source_target_pairs={{0,8},{4,20},{8,0},{12,28},{16,24},{20,4},{24,16},{28,12},{1,9},{5... | collective-permute-start | bytes 4128776 | tf_op jit(solution)/shard_map/ppermute | solution.py:1052
  474.7 24.1 %collective-permute-start.70 = (bf16[224,768]{1,0:T(8,128)(2,1)S(1)}, bf16[224,768]{1,0:T(8,128)(2,1)S(1)}, u32[]{:S(2)}, u32[]{:S(2)}) collective-permute-start(bf16[224,768]{1,0:T(8,128)(2,1)S(1)} %copy-done.12), channel_id=1, source_target_pairs={{0,16},{4,12},{8,24},{12,4},{16,0},{20,28},{24,8},{28,20},{1,17},{... | collective-permute-start | bytes 1032200 | tf_op jit(solution)/shard_map/ppermute | solution.py:1056
  476.3 22.6 %collective-permute-start.71 = (bf16[224,768]{1,0:T(8,128)(2,1)S(1)}, bf16[224,768]{1,0:T(8,128)(2,1)S(1)}, u32[]{:S(2)}, u32[]{:S(2)}) collective-permute-start(bf16[224,768]{1,0:T(8,128)(2,1)S(1)} %copy-done.23), channel_id=1, source_target_pairs={{0,16},{4,12},{8,24},{12,4},{16,0},{20,28},{24,8},{28,20},{1,17},{... | collective-permute-start | bytes 1032200 | tf_op jit(solution)/shard_map/ppermute | solution.py:1056
  476.7 49.1 %collective-permute-start.73 = (bf16[4,224,768]{2,1,0:T(8,128)(2,1)}, bf16[4,224,768]{2,1,0:T(8,128)(2,1)}, u32[]{:S(2)}, u32[]{:S(2)}) collective-permute-start(bf16[4,224,768]{2,1,0:T(8,128)(2,1)} %get-tuple-element.514), channel_id=1, source_target_pairs={{0,8},{4,20},{8,0},{12,28},{16,24},{20,4},{24,16},{28,12},{1,9},{5... | collective-permute-start | bytes 4128776 | tf_op jit(solution)/shard_map/ppermute | solution.py:1052
  506.1 22.3 %collective-permute-start.74 = (bf16[4,224,768]{2,1,0:T(8,128)(2,1)S(1)}, bf16[4,224,768]{2,1,0:T(8,128)(2,1)S(1)}, u32[]{:S(2)}, u32[]{:S(2)}) collective-permute-start(bf16[4,224,768]{2,1,0:T(8,128)(2,1)S(1)} %fusion.2), channel_id=1, source_target_pairs={{0,16},{4,12},{8,24},{12,4},{16,0},{20,28},{24,8},{28,20},{1,17},{... | collective-permute-start | bytes 4128776 | tf_op jit(solution)/shard_map/ppermute | solution.py:1056
  555.1 22.3 %collective-permute-start.84 = (bf16[4,96,576]{2,1,0:T(8,128)(2,1)S(1)}, bf16[4,96,576]{2,1,0:T(8,128)(2,1)S(1)}, u32[]{:S(2)}, u32[]{:S(2)}) collective-permute-start(bf16[4,96,576]{2,1,0:T(8,128)(2,1)S(1)} %get-tuple-element.655), channel_id=1, source_target_pairs={{0,8},{4,20},{8,0},{12,28},{16,24},{20,4},{24,16},{28,12},{1,9},{5... | collective-permute-start | bytes 1327112 | tf_op jit(solution)/shard_map/ppermute | solution.py:1052
  556.1 21.5 %collective-permute-start.83 = (bf16[4,96,576]{2,1,0:T(8,128)(2,1)S(1)}, bf16[4,96,576]{2,1,0:T(8,128)(2,1)S(1)}, u32[]{:S(2)}, u32[]{:S(2)}) collective-permute-start(bf16[4,96,576]{2,1,0:T(8,128)(2,1)S(1)} %get-tuple-element.656), channel_id=1, source_target_pairs={{0,16},{4,12},{8,24},{12,4},{16,0},{20,28},{24,8},{28,20},{1,17},{... | collective-permute-start | bytes 1327112 | tf_op jit(solution)/shard_map/ppermute | solution.py:1056
  (279 other events, 1831.4 us)
